TPU v7x, 128 devices: a whole 4x4x4 slice. The times are simulated.
128 devices in a mesh: row: 16 (over y, z_lo, core), col: 8 (over x, z_hi).
Axes of the slice: x: 4, y: 4, z: 4 (z_hi: 2, z_lo: 2; z = z_hi * 2 + z_lo), core: 2. Of those that a mesh axis runs over, the one named last changes fastest.
Arguments:
- matrix: float32 [16384, 16384], P('row', 'col'), may hold values from -8 to 8, as said below
- vectors: float32 [16384, 8192], P('row', 'col'), may hold values from -6 to 6
Outputs:
- updated: float32 [16384, 16384], P('row', 'col')
- rotated: float32 [16384, 8192], P('row', 'col')
Inputs may be any that keep to these rules, and one draw needn't show every extreme that they name: matrix is symmetric up to rounding.
All inputs are finite; a program needn't handle non-finite values.
Results may differ from a plain program's by a relative error of at most 0.00011.
Values sent between devices are 32-bit elements; how exact they have to be, the bound alone decides.
No kernel may reach another device: no remote copies, remote signals or barrier semaphores. Data moves between devices by JAX's collectives and lax.ppermute only.
A program may use at most 128 MiB of HBM per device.

v0:
```python
import jax
import jax.numpy as jnp
from jax import lax
from jax.sharding import PartitionSpec as P

B = 256


def broadcast(array, axis, root):
    mine = lax.axis_index(axis) == root
    return lax.psum(jnp.where(mine, array, jnp.zeros_like(array)), axis)


def matmul(left, right):
    return jnp.dot(left, right, preferred_element_type=jnp.float32, precision=lax.Precision.HIGHEST)


def inner_product(left, right):
    return lax.dot_general(
        left,
        right,
        (((0,), (0,)), ((), ())),
        preferred_element_type=jnp.float32,
        precision=lax.Precision.HIGHEST,
    )


def outer_product(left, right):
    return lax.dot_general(
        left,
        right,
        (((1,), (1,)), ((), ())),
        preferred_element_type=jnp.float32,
        precision=lax.Precision.HIGHEST,
    )


def body(matrix, vectors):
    rows_here = matrix.shape[0]
    columns_here = matrix.shape[1]
    row_index = lax.axis_index("row")
    column_index = lax.axis_index("col")
    row_panel = broadcast(matrix[:, :B], "col", 0)
    column_panel = broadcast(matrix[:B, :], "row", 0)
    global_rows = row_index * rows_here + jnp.arange(rows_here, dtype=jnp.int32)
    global_columns = column_index * columns_here + jnp.arange(columns_here, dtype=jnp.int32)
    row_panel = jnp.where(global_rows[:, None] >= B, row_panel, jnp.float32(0.0))
    column_panel = jnp.where(global_columns[None, :] >= B, column_panel, jnp.float32(0.0))
    gram = lax.psum(inner_product(row_panel, row_panel), "row")
    factor = jnp.linalg.cholesky(gram)
    basis_rows = lax.linalg.triangular_solve(
        factor, row_panel, left_side=False, lower=True, transpose_a=True
    )
    basis_columns = lax.linalg.triangular_solve(
        factor, column_panel.T, left_side=False, lower=True, transpose_a=True
    )
    product_rows = lax.psum(matmul(matrix, basis_columns), "col")
    product_columns = lax.psum(inner_product(matrix, basis_rows), "row")
    coupling = lax.psum(inner_product(basis_rows, product_rows), "row")
    wide_rows = 2.0 * product_rows - 2.0 * matmul(basis_rows, coupling)
    wide_columns = 2.0 * product_columns - 2.0 * matmul(basis_columns, coupling)
    updated = (
        matrix - outer_product(basis_rows, wide_columns) - outer_product(wide_rows, basis_columns)
    )
    mixing = lax.psum(inner_product(basis_rows, vectors), "row")
    rotated = vectors - 2.0 * matmul(basis_rows, mixing)
    return (updated, rotated)


def solution(mesh):
    placed = (P("row", "col"), P("row", "col"))
    return jax.shard_map(
        body,
        mesh=mesh,
        in_specs=placed,
        out_specs=(P("row", "col"), P("row", "col")),
        check_vma=False,
    )
```

profile of v0, /device:TPU:1, one launch (start us, length us, event | category | flops | bytes accessed | tf_op | source)
XLA Modules:
  0.0 560.3 jit_solution(9244692297078776420)
XLA Ops:
  7.2 0.0 all-reduce.8.cloned.1.call-start
  7.2 2.3 slice_select_fusion.1
  9.5 0.0 all-reduce.8.cloned.1.call-update
  9.5 0.0 all-reduce.14.cloned.1.call-start
  9.6 3.1 slice_select_fusion
  12.7 85.5 %all-reduce.8.cloned.1.call-done = f32[1024,256]{1,0:T(8,128)} async-done(((f32[1024,256]{1,0:T(8,128)}), f32[1024,256]{1,0:T(8,128)}) %all-reduce.8.cloned.1.call-update) | async-done | bytes 1048592 | tf_op jit(solution)/shard_map/psum | solution.py:11
  98.2 1.4 broadcast_select_fusion
  99.7 0.0 copy-start.1
  99.7 2.5 fusion.27
  102.2 0.0 all-reduce.14.cloned.1.call-update
  102.2 0.6 all-reduce.10.cloned.1.call-start
  102.9 126.8 %all-reduce.14.cloned.1.call-done = (f32[256,2048]{1,0:T(8,128)}, f32[256,256]{0,1:T(8,128)}) async-done(((f32[256,2048]{1,0:T(8,128)}, f32[256,256]{0,1:T(8,128)}), (f32[256,2048]{1,0:T(8,128)}, f32[256,256]{0,1:T(8,128)})) %all-reduce.14.cloned.1.call-update) | async-done | bytes 2359312 | tf_op jit(solution)/shard_map/psum | solution.py:11
  229.6 1.1 copy.5
  230.7 1.0 fusion.6
  231.7 11.7 %cholesky.50 = f32[128,128]{1,0:T(8,128)S(1)} custom-call(f32[128,128]{1,0:T(8,128)S(1)} %cholesky.118), custom_call_target="Cholesky" | custom-call | tf_op jit(solution)/shard_map/jit(cholesky)/cholesky | solution.py:50
  243.5 9.8 %custom-call.16 = f32[1,128,128]{1,2,0:T(8,128)S(1)} custom-call(f32[1,128,128]{2,1,0:T(8,128)S(1)} %get-tuple-element.28), custom_call_target="InvertDiagBlocksLowerTriangular" | custom-call | tf_op jit(solution)/shard_map/jit(cholesky)/cholesky | solution.py:50
  253.3 0.2 constant_dynamic-update-slice_fusion.1
  253.5 0.3 convolution_subtract_fusion.2
  253.8 11.7 %cholesky.105 = f32[128,128]{1,0:T(8,128)S(1)} custom-call(f32[128,128]{1,0:T(8,128)S(1)} %convolution_subtract_fusion.2), custom_call_target="Cholesky" | custom-call | tf_op jit(solution)/shard_map/jit(cholesky)/cholesky | solution.py:50
  265.5 0.6 compare_reduce_fusion
  267.5 0.1 triangular_solve.73
  267.6 4.2 while.1
  267.8 0.6 fusion.46
  268.3 1.4 bitcast_dynamic-update-slice_fusion.2
  269.8 0.6 fusion.46
  270.3 1.4 bitcast_dynamic-update-slice_fusion.2
  271.7 19.7 %custom-call.17 = f32[2,128,128]{1,2,0:T(8,128)S(1)} custom-call(f32[2,128,128]{2,1,0:T(8,128)S(1)} %get-tuple-element.9), custom_call_target="InvertDiagBlocksLowerTriangular" | custom-call | tf_op jit(solution)/shard_map/triangular_solve | solution.py:51
  291.4 0.0 copy-done.1
  291.4 0.6 fusion.4
  292.0 1.7 select_bitcast_fusion
  293.8 1.1 fusion.2
  294.9 1.1 convolution_subtract_fusion
  296.0 1.1 fusion.13
  297.1 10.4 %convolution_bitcast_fusion.1 = f32[1024,256]{0,1:T(8,128)} fusion(f32[1024,2048]{1,0:T(8,128)} %param.2, f32[2048,128]{0,1:T(8,128)S(1)} %fusion.13, f32[2048,128]{0,1:T(8,128)S(1)} %fusion.2), kind=kOutput, calls=%fused_computation.11 | convolution fusion | flops 6442975232 | bytes 11534336 | tf_op jit(solution)/shard_map/dot_general | solution.py:15
  307.5 0.0 all-reduce.10.cloned.1.call-update
  307.5 0.3 all-reduce.12.cloned.1.call-start
  307.7 2.0 convolution_subtract_fusion.1
  309.8 0.6 fusion.14
  310.4 6.8 %fusion.7 = f32[256,1024]{1,0:T(8,128)} fusion(f32[1024,1024]{1,0:T(8,128)} %param.3, f32[1024,128]{0,1:T(8,128)S(1)} %fusion.14, f32[1024,128]{0,1:T(8,128)S(1)} %fusion.4), kind=kOutput, calls=%fused_computation.27 | convolution fusion | flops 3221487616 | bytes 6291456 | tf_op jit(solution)/shard_map/dot_general | solution.py:19
  317.2 10.8 %convolution_bitcast_fusion = f32[2048,256]{0,1:T(8,128)} fusion(f32[1024,2048]{1,0:T(8,128)} %param.2, f32[1024,128]{0,1:T(8,128)S(1)} %fusion.14, f32[1024,128]{0,1:T(8,128)S(1)} %fusion.4), kind=kOutput, calls=%fused_computation.6 | convolution fusion | flops 6442713088 | bytes 11534336 | tf_op jit(solution)/shard_map/dot_general | solution.py:19
  328.1 64.7 %all-reduce.10.cloned.1.call-done = f32[1024,256]{0,1:T(8,128)} async-done(((f32[1024,256]{0,1:T(8,128)}), f32[1024,256]{0,1:T(8,128)}) %all-reduce.10.cloned.1.call-update) | async-done | bytes 1048592 | tf_op jit(solution)/shard_map/psum | solution.py:57
  392.7 3.0 fusion.9
  395.7 0.0 all-reduce.12.cloned.1.call-update
  395.7 130.6 %all-reduce.12.cloned.1.call-done = (f32[256,256]{1,0:T(8,128)}, f32[2048,256]{0,1:T(8,128)}, f32[256,1024]{1,0:T(8,128)}) async-done(((f32[256,256]{1,0:T(8,128)}, f32[2048,256]{0,1:T(8,128)}, f32[256,1024]{1,0:T(8,128)}), (f32[256,256]{1,0:T(8,128)}, f32[2048,256]{0,1:T(8,128)}, f32[256,1024]{1,0:T(8,128)})) %all-reduce.12.cloned.1.call-update) | async-done | bytes 3407888 | tf_op jit(solution)/shard_map/psum | solution.py:59
  526.3 3.9 fusion
  530.1 0.0 copy-start
  530.2 0.0 copy-start.3
  530.2 0.0 slice-start
  530.2 6.8 %fusion.8 = f32[1024,2048]{1,0:T(8,128)S(1)} fusion(f32[2048,256]{0,1:T(8,128)S(1)} %fusion, f32[1024,128]{0,1:T(8,128)S(1)} %fusion.14, f32[1024,128]{0,1:T(8,128)S(1)} %fusion.4), kind=kOutput, calls=%fused_computation.28 | convolution fusion | flops 6442713088 | bytes 11534336 | tf_op jit(solution)/shard_map/dot_general | solution.py:29
  537.0 0.0 copy-done
  537.0 0.0 copy-done.3
  537.0 0.0 copy-start.2
  537.0 0.0 copy-start.4
  537.0 0.0 slice-start.1
  537.0 5.4 multiply_subtract_fusion
  542.4 0.0 copy-done.2
  542.4 0.0 copy-done.4
  542.4 1.2 fusion.1
  543.6 0.0 slice-done
  543.6 0.0 slice-done.1
  543.6 9.6 %subtract_subtract_fusion = f32[1024,2048]{1,0:T(8,128)} fusion(f32[1024,2048]{1,0:T(8,128)S(1)} %bitcast.53, f32[1024,2048]{1,0:T(8,128)S(1)} %fusion.8, f32[1024,256]{0,1:T(8,128)S(1)} %fusion.1, f32[2048,128]{0,1:T(8,128)S(1)} %fusion.13, f32[2048,128]{0,1:T(8,128)S(1)} %fusion.2), kind=kOutput, calls=%fused_computation.2 | convolution fusion | flops 6447169536 | bytes 28311552 | tf_op jit(solution)/shard_map/dot_general | solution.py:29
  (12 shorter events, 0.2 us)
Async XLA Ops:
  7.2 91.1 %all-reduce.8.cloned.1.call-start = ((), (), s32[]{:S(2)}) async-start(), calls=%async_computation | async-start | bytes 2097152 | tf_op jit(solution)/shard_map/psum | solution.py:11
  9.5 220.1 %all-reduce.14.cloned.1.call-start = ((), (), s32[]{:S(2)}) async-start(), calls=%async_computation.3 | async-start | bytes 4718592 | tf_op jit(solution)/shard_map/psum | solution.py:11
  99.7 191.7 %copy-start.1 = (f32[1024,256]{1,0:T(8,128)}, f32[1024,256]{1,0:T(8,128)S(1)}, u32[]{:S(2)}) copy-start(f32[1024,256]{1,0:T(8,128)S(1)} %broadcast_select_fusion) | copy-start | bytes 3145732
  102.2 290.5 %all-reduce.10.cloned.1.call-start = ((), (), s32[]{:S(2)}) async-start(), calls=%async_computation.1 | async-start | bytes 2097152 | tf_op jit(solution)/shard_map/psum | solution.py:57
  307.5 218.8 %all-reduce.12.cloned.1.call-start = ((), (), s32[]{:S(2)}) async-start(), calls=%async_computation.2 | async-start | bytes 6815744 | tf_op jit(solution)/shard_map/psum | solution.py:59
  530.1 6.8 %copy-start = (f32[1024,1024]{1,0:T(8,128)S(1)}, f32[1024,1024]{1,0:T(8,128)}, u32[]{:S(2)}) copy-start(f32[1024,1024]{1,0:T(8,128)} %param.3) | copy-start | bytes 12582916
  530.2 6.8 %copy-start.3 = (f32[256,1024]{1,0:T(8,128)S(1)}, f32[256,1024]{1,0:T(8,128)}, u32[]{:S(2)}) copy-start(f32[256,1024]{1,0:T(8,128)} %get-tuple-element.20) | copy-start | bytes 3145732
  530.2 13.5 %slice-start = ((s8[8388608]{0:T(1024)(128)(4,1)}), s8[4194304]{0:T(1024)(128)(4,1)S(1)}, s32[]{:S(2)}) async-start(s8[8388608]{0:T(1024)(128)(4,1)} %bitcast.52), calls=%async_computation.4 | async-start | bytes 8388608
  537.0 5.4 copy-start.2
  537.0 5.4 copy-start.4
  537.0 6.6 %slice-start.1 = ((s8[8388608]{0:T(1024)(128)(4,1)}), s8[4194304]{0:T(1024)(128)(4,1)S(1)}, s32[]{:S(2)}) async-start(s8[8388608]{0:T(1024)(128)(4,1)} %bitcast.52), calls=%async_computation.5 | async-start | bytes 8388608
Sparse Core Ops, SparseCore 0:
  11.1 87.1 all-reduce.7
  102.4 127.2 all-reduce.13
  307.6 85.0 all-reduce.9
  395.9 130.3 all-reduce.11
where the time goes:
time: 563 us; the launch traced here: 560 us
  waiting for transfers between devices  408 us (72%)
  matrix products  67.3 us (12%)
  other arithmetic  63.2 us (11%)
  between operations  15.9 us (3%)
    psum x2, waiting for transfers between devices, broadcast(): return lax.psum(jnp.where(mine, array, jnp.zeros_like(array)), axis)  212 us
    psum x1, waiting for transfers between devices, body(): coupling = lax.psum(inner_product(basis_rows, product_rows), 'row')  131 us
    psum x1, waiting for transfers between devices, body(): product_rows = lax.psum(matmul(matrix, basis_columns), 'col')  64.7 us
    another operation x6, other arithmetic, body(): factor = jnp.linalg.cholesky(gram)  33.9 us
    dot_general x4, matrix products, inner_product(): lax.dot_general(left, right, (((0,), (0,)), ((), ())), preferred_element_...  23.1 us
    dot_general x4, matrix products, matmul(): jnp.dot(left, right, preferred_element_type=jnp.float32, precision=lax.Pr...  20.8 us
    another operation x3, other arithmetic, body(): lax.linalg.triangular_solve(factor, row_panel, left_side=False, lower=Tru...  19.7 us
    dot_general x2, matrix products, outer_product(): lax.dot_general(left, right, (((1,), (1,)), ((), ())), preferred_element_...  16.3 us
  transfers between devices with their start and end apart: 4, of which 4 were waited for; matrix products, arithmetic and copies ran while one was open for 4% of the time, Pallas kernels for 0%

commit v1 on v0

v1 whole, which is shorter than its diff:
```python
import jax
import jax.numpy as jnp
from jax import lax
from jax.experimental import pallas as pl
from jax.experimental.pallas import tpu as pltpu
from jax.sharding import Mesh
from jax.sharding import PartitionSpec as P

B = 256
ROW = ("y", "zl", "co")
CHIPS = ("y", "zl")
COL = ("x", "zh")
ALL = ("y", "zl", "co", "x", "zh")
HIGH = lax.Precision.HIGH
HIGHEST = lax.Precision.HIGHEST


def nn(left, right, precision=HIGH):
    return lax.dot_general(
        left, right, (((1,), (0,)), ((), ())), preferred_element_type=jnp.float32, precision=precision
    )


def tn(left, right, precision=HIGH):
    return lax.dot_general(
        left, right, (((0,), (0,)), ((), ())), preferred_element_type=jnp.float32, precision=precision
    )


def nt(left, right, precision=HIGH):
    return lax.dot_general(
        left, right, (((1,), (1,)), ((), ())), preferred_element_type=jnp.float32, precision=precision
    )


def sweep_all(block):
    n, group = 128, 16
    lane = lax.broadcasted_iota(jnp.int32, (1, n), 1)
    line = lax.broadcasted_iota(jnp.int32, (n, 1), 0)

    def step(_, s):
        for k in range(0, group, 2):
            r0, r1 = s[k : k + 1, :], s[k + 1 : k + 2, :]
            c0, c1 = s[:, k : k + 1], s[:, k + 1 : k + 2]
            a, b, d = r0[:, k : k + 1], r0[:, k + 1 : k + 2], r1[:, k + 1 : k + 2]
            scale = 1.0 / (a * d - b * b)
            ia, ib, id_ = d * scale, -b * scale, a * scale
            q0 = ia * r0 + ib * r1
            q1 = ib * r0 + id_ * r1
            q0 = jnp.where(lane == k, -ia, jnp.where(lane == k + 1, -ib, q0))
            q1 = jnp.where(lane == k, -ib, jnp.where(lane == k + 1, -id_, q1))
            c0 = jnp.where(line == k, -1.0, jnp.where(line == k + 1, 0.0, c0))
            c1 = jnp.where(line == k, 0.0, jnp.where(line == k + 1, -1.0, c1))
            keep = ((lane != k) & (lane != k + 1)) & ((line != k) & (line != k + 1))
            s = jnp.where(keep, s, 0.0) - c0 * q0 - c1 * q1
        s = jnp.concatenate([s[group:], s[:group]], axis=0)
        return pltpu.roll(s, n - group, 1)

    return lax.fori_loop(0, n // group, step, block)


def invert_kernel(gram_ref, out_ref):
    h = B // 2
    a, b, d = gram_ref[:h, :h], gram_ref[:h, h:], gram_ref[h:, h:]
    ai = -sweep_all(a)
    t = nn(ai, b, HIGHEST)
    si = -sweep_all(d - tn(b, t, HIGHEST))
    u = nn(t, si, HIGHEST)
    out_ref[:h, :h] = ai + nt(u, t, HIGHEST)
    out_ref[:h, h:] = -u
    out_ref[h:, :h] = -u.T
    out_ref[h:, h:] = si


def invert(gram):
    return pl.pallas_call(
        invert_kernel,
        out_shape=jax.ShapeDtypeStruct((B, B), jnp.float32),
        cost_estimate=pl.CostEstimate(flops=2 * B**3 * 20, bytes_accessed=8 * B * B, transcendentals=0),
    )(gram)


def repeat(block, n):
    return jnp.broadcast_to(block[None], (n,) + block.shape)


def exchange(blocks, axes):
    return lax.all_to_all(blocks, axes, 0, 0, tiled=True)


def swap_cores(array):
    return lax.ppermute(array, "co", [(0, 1), (1, 0)])


def flip_pairs():
    pairs = []
    for i in range(16):
        for k in range(8):
            pairs.append((i * 8 + k, (k * 2 + i % 2) * 8 + i // 2))
    return pairs


def body(matrix, vectors):
    rows_here = matrix.shape[0]
    row_index = lax.axis_index(ROW)
    col_index = lax.axis_index(COL)
    core = lax.axis_index("co")
    there = flip_pairs()
    back = [(b, a) for a, b in there]

    global_rows = row_index * rows_here + jnp.arange(rows_here, dtype=jnp.int32)
    panel = jnp.where(global_rows[:, None] >= B, matrix[:, :B], jnp.float32(0.0))
    mine = panel[:128]
    for k in range(1, 8):
        got = lax.ppermute(panel[k * 128 : (k + 1) * 128], COL, [(0, k)])
        mine = jnp.where(col_index == k, got, mine)
    mine_t = lax.ppermute(mine, ALL, there)

    panel_rows = exchange(repeat(mine, 8), COL).reshape(1024, B)
    half = exchange(repeat(mine_t, 8), CHIPS).reshape(1024, B)
    other = swap_cores(half)
    panel_cols = jnp.where(
        core == 0, jnp.concatenate([half, other]), jnp.concatenate([other, half])
    )

    product_t = tn(matrix, panel_rows)
    mixing_t = tn(vectors, panel_rows)
    gram = tn(panel_rows, panel_rows, HIGHEST)
    coupling = tn(panel_cols, product_t)
    parts = jnp.concatenate(
        [
            product_t.reshape(2, 8, 128, B),
            mixing_t.reshape(2, 8, 64, B),
            gram.reshape(2, 8, 16, B),
            coupling.reshape(2, 8, 16, B),
        ],
        axis=2,
    )
    keep = jnp.where(core == 0, parts[0], parts[1])
    give = jnp.where(core == 0, parts[1], parts[0])
    own = jnp.sum(exchange(keep + swap_cores(give), CHIPS), axis=0)

    coupling16 = jnp.sum(exchange(repeat(own[208:], 8), COL), axis=0)
    product_mine = lax.ppermute(own[:128], ALL, back)
    half = exchange(repeat(jnp.concatenate([own[:208], coupling16]), 8), CHIPS)
    product_rows = exchange(repeat(product_mine, 8), COL).reshape(1024, B)
    other = swap_cores(half)
    low = jnp.where(core == 0, half, other)
    high = jnp.where(core == 0, other, half)
    full = jnp.stack([low, high])
    product_cols = full[:, :, :128].reshape(2048, B)
    mixing_t = full[:, :, 128:192].reshape(1024, B)
    gram = full[:, :, 192:208].reshape(B, B)
    coupling = full[:, :, 208:].reshape(B, B)

    inverse = invert(gram)
    u1 = 2.0 * nn(panel_rows, inverse, HIGHEST)
    u2 = 2.0 * nn(product_rows, inverse, HIGHEST) - 2.0 * nn(u1, nn(coupling, inverse, HIGHEST), HIGHEST)
    rotated = vectors - nt(u1, mixing_t)
    updated = matrix - nt(jnp.concatenate([u1, u2], axis=1), jnp.concatenate([product_cols, panel_cols], axis=1))
    return (updated, rotated)


def solution(mesh):
    fine = Mesh(mesh.devices.reshape(4, 2, 2, 4, 2), ALL)
    placed = (P(ROW, COL), P(ROW, COL))
    return jax.shard_map(body, mesh=fine, in_specs=placed, out_specs=placed, check_vma=False)
```

time: 563 us -> 251 us (0.45)
  waiting for transfers between devices: 408 us -> 41.3 us
  starting transfers between devices: 0.9 us -> 60.3 us
  other arithmetic: 63.2 us -> 12.1 us
  blocking collectives: 0 us -> 49 us
  Pallas kernels: 0 us -> 33.3 us
  matrix products: 67.3 us -> 42.6 us
  between operations: 15.9 us -> 1.13 us
    psum x4 -> x0, waiting for transfers between devices: 408 us -> none  [the longest x2 212 us: broadcast(): return lax.psum(jnp.where(mine, array, jnp.zeros_like(array)), axis)]
    all_to_all x0 -> x2, blocking collectives: none -> 49 us  [exchange(): return lax.all_to_all(blocks, axes, 0, 0, tiled=True)]
    another operation x9 -> x3, other arithmetic: 53.7 us -> 6.16 us  [body(): full = jnp.stack([low, high])]
    all_to_all x0 -> x4, starting transfers between devices: none -> 35.5 us  [exchange(): return lax.all_to_all(blocks, axes, 0, 0, tiled=True)]
    pallas_call x0 -> x1, Pallas kernels: none -> 33.3 us  [invert(): pl.pallas_call(invert_kernel, out_shape=jax.ShapeDtypeStruct((B, B), jnp....]
    all_to_all x0 -> x4, waiting for transfers between devices: none -> 32.3 us  [exchange(): return lax.all_to_all(blocks, axes, 0, 0, tiled=True)]
    ppermute x0 -> x12, starting transfers between devices: none -> 24.8 us  [the longest x7 16.3 us: body(): got = lax.ppermute(panel[k * 128:(k + 1) * 128], COL, [(0, k)])]
    dot_general x10, matrix products: 60.3 us -> 42.6 us  [the longest x2 23.3 us: nt(): lax.dot_general(left, right, (((1,), (1,)), ((), ())), preferred_element_...]
  transfers between devices with their start and end apart: 4 -> 16, of which waited for: 4 -> 6; matrix products, arithmetic and copies ran while one was open for 4% -> 11% of each run, Pallas kernels for 0% -> 13%
where the time goes in v1:
time: 251 us
  starting transfers between devices  60.3 us (24%)
  blocking collectives  49 us (20%)
  matrix products  42.6 us (17%)
  waiting for transfers between devices  41.3 us (16%)
  Pallas kernels  33.3 us (13%)
  other arithmetic  12.1 us (5%)
  local copies, waits for them, and re-layouts  10.7 us (4%)
    all_to_all x2, blocking collectives, exchange(): return lax.all_to_all(blocks, axes, 0, 0, tiled=True)  49 us
    all_to_all x4, starting transfers between devices, exchange(): return lax.all_to_all(blocks, axes, 0, 0, tiled=True)  35.5 us
    pallas_call x1, Pallas kernels, invert(): pl.pallas_call(invert_kernel, out_shape=jax.ShapeDtypeStruct((B, B), jnp....  33.3 us
    all_to_all x4, waiting for transfers between devices, exchange(): return lax.all_to_all(blocks, axes, 0, 0, tiled=True)  32.3 us
    dot_general x2, matrix products, nt(): lax.dot_general(left, right, (((1,), (1,)), ((), ())), preferred_element_...  23.3 us
    ppermute x7, starting transfers between devices, body(): got = lax.ppermute(panel[k * 128:(k + 1) * 128], COL, [(0, k)])  16.3 us
    dot_general x4, matrix products, tn(): lax.dot_general(left, right, (((0,), (0,)), ((), ())), preferred_element_...  14.3 us
    ppermute x3, starting transfers between devices, swap_cores(): return lax.ppermute(array, 'co', [(0, 1), (1, 0)])  7.16 us
  transfers between devices with their start and end apart: 16, of which 6 were waited for; matrix products, arithmetic and copies ran while one was open for 11% of the time, Pallas kernels for 13%

profile of v1, /device:TPU:1, one launch (start us, length us, event | category | flops | bytes accessed | tf_op | source)
XLA Modules:
  0.0 250.6 jit_solution(16681010441458624504)
XLA Ops:
  0.7 1.4 slice_select_fusion
  2.2 8.5 %collective-permute-start = (f32[128,256]{1,0:T(8,128)S(1)}, f32[128,256]{1,0:T(8,128)S(1)}, u32[]{:S(2)}, u32[]{:S(2)}) collective-permute-start(f32[128,256]{1,0:T(8,128)S(1)} %get-tuple-element.12), channel_id=1, source_target_pairs={{0,7},{8,15},{16,23},{24,31},{32,39},{40,47},{48,55},{56,63},{64,7... | collective-permute-start | bytes 393224 | tf_op jit(solution)/shard_map/ppermute | solution.py:115
  10.7 1.3 collective-permute-start.1
  12.0 1.3 collective-permute-start.2
  13.3 1.3 collective-permute-start.3
  14.6 1.3 collective-permute-start.4
  15.9 1.3 collective-permute-start.5
  17.2 1.3 collective-permute-start.6
  18.6 2.5 collective-permute-done.4
  21.1 2.8 %collective-permute-done.5 = f32[128,256]{1,0:T(8,128)S(1)} collective-permute-done((f32[128,256]{1,0:T(8,128)S(1)}, f32[128,256]{1,0:T(8,128)S(1)}, u32[]{:S(2)}, u32[]{:S(2)}) %collective-permute-start.5) | collective-permute-done | bytes 131104 | tf_op jit(solution)/shard_map/ppermute | solution.py:115
  23.9 0.1 fusion.17
  23.9 1.1 broadcast_in_dim.24
  25.0 3.6 %all-to-all-start = ((f32[8,128,256]{2,1,0:T(8,128)}), f32[8,128,256]{2,1,0:T(8,128)S(1)}, u32[]{:S(2)}, u32[]{:S(2)}) async-start(f32[8,128,256]{2,1,0:T(8,128)} %broadcast_in_dim.24), calls=%async_computation | async-start | bytes 2097152 | tf_op jit(solution)/shard_map/all_to_all | solution.py:88
  28.6 0.7 collective-permute-start.7
  29.3 13.3 %all-to-all-done = f32[8,128,256]{2,1,0:T(8,128)S(1)} async-done(((f32[8,128,256]{2,1,0:T(8,128)}), f32[8,128,256]{2,1,0:T(8,128)S(1)}, u32[]{:S(2)}, u32[]{:S(2)}) %all-to-all-start) | async-done | bytes 1048608 | tf_op jit(solution)/shard_map/all_to_all | solution.py:88
  42.6 1.1 broadcast_in_dim.25
  43.6 10.4 %all-to-all-start.1 = ((f32[8,128,256]{2,1,0:T(8,128)}), f32[8,128,256]{2,1,0:T(8,128)}, u32[]{:S(2)}, u32[]{:S(2)}) async-start(f32[8,128,256]{2,1,0:T(8,128)} %broadcast_in_dim.25), calls=%async_computation.1 | async-start | bytes 2097152 | tf_op jit(solution)/shard_map/all_to_all | solution.py:88
  54.1 1.3 copy.28
  55.4 12.3 %all-to-all-done.1 = f32[8,128,256]{2,1,0:T(8,128)} async-done(((f32[8,128,256]{2,1,0:T(8,128)}), f32[8,128,256]{2,1,0:T(8,128)}, u32[]{:S(2)}, u32[]{:S(2)}) %all-to-all-start.1) | async-done | bytes 1048608 | tf_op jit(solution)/shard_map/all_to_all | solution.py:88
  67.6 3.1 %collective-permute-start.8 = (f32[1024,256]{1,0:T(8,128)}, f32[1024,256]{1,0:T(8,128)}, u32[]{:S(2)}, u32[]{:S(2)}) collective-permute-start(f32[1024,256]{1,0:T(8,128)} %bitcast.9), channel_id=1, source_target_pairs={{0,8},{8,0},{1,9},{9,1},{2,10},{10,2},{3,11},{11,3},{4,12},{12,4},... | collective-permute-start | bytes 3145736 | tf_op jit(solution)/shard_map/ppermute | solution.py:92
  70.7 4.1 %convolution_bitcast_fusion = f32[1024,256]{0,1:T(8,128)S(1)} fusion(f32[1024,256]{1,0:T(8,128)S(1)} %bitcast.49, f32[1024,1024]{1,0:T(8,128)} %param.3), kind=kOutput, calls=%fused_computation.18 | convolution fusion | flops 1610612736 | bytes 6291456 | tf_op jit(solution)/shard_map/dot_general | solution.py:25
  74.8 1.3 copy.27
  76.2 6.1 %fusion.20 = f32[256,2048]{1,0:T(8,128)S(1)} fusion(f32[1024,256]{1,0:T(8,128)S(1)} %bitcast.50, f32[1024,2048]{1,0:T(8,128)} %param.2), kind=kOutput, calls=%fused_computation.38 | convolution fusion | flops 3221225472 | bytes 11534336 | tf_op jit(solution)/shard_map/dot_general | solution.py:25
  82.3 1.8 copy.36
  84.1 2.2 fusion.21
  86.3 2.5 maximum_select_fusion
  88.9 1.9 fusion.22
  90.8 0.4 copy-done.4
  91.2 0.3 copy-done.7
  91.5 0.3 pad_maximum_fusion
  91.8 0.2 select_bitcast_fusion.2
  92.0 0.1 collective-permute-start.9
  92.1 3.8 %collective-permute-done.9 = f32[8,224,256]{2,1,0:T(8,128)S(1)} collective-permute-done((f32[8,224,256]{2,1,0:T(8,128)S(1)}, f32[8,224,256]{2,1,0:T(8,128)S(1)}, u32[]{:S(2)}, u32[]{:S(2)}) %collective-permute-start.9) | collective-permute-done | bytes 1835040 | tf_op jit(solution)/shard_map/ppermute | solution.py:92
  95.9 0.4 bitcast_add_fusion
  96.3 25.7 %all_to_all.30 = f32[8,224,256]{2,1,0:T(8,128)S(1)} all-to-all(f32[8,224,256]{2,1,0:T(8,128)S(1)} %bitcast_add_fusion), channel_id=1, replica_groups=mesh['y'=4,'zl'=2,'co'=2,'x'=4,'zh'=2] {'y','zl'}, dimensions={0} | all-to-all | bytes 3670016 | tf_op jit(solution)/shard_map/all_to_all | solution.py:88
  121.9 0.1 reduce_sum.18
  122.1 0.7 broadcast_in_dim.26
  122.7 4.6 %all-to-all-start.3 = ((f32[8,16,256]{2,1,0:T(8,128)}), f32[8,16,256]{2,1,0:T(8,128)S(1)}, u32[]{:S(2)}, u32[]{:S(2)}) async-start(f32[8,16,256]{2,1,0:T(8,128)} %broadcast_in_dim.26), calls=%async_computation.3 | async-start | bytes 262144 | tf_op jit(solution)/shard_map/all_to_all | solution.py:88
  127.4 0.1 copy.38
  127.5 6.7 %all-to-all-done.3 = f32[8,16,256]{2,1,0:T(8,128)S(1)} async-done(((f32[8,16,256]{2,1,0:T(8,128)}), f32[8,16,256]{2,1,0:T(8,128)S(1)}, u32[]{:S(2)}, u32[]{:S(2)}) %all-to-all-start.3) | async-done | bytes 131104 | tf_op jit(solution)/shard_map/all_to_all | solution.py:88
  134.2 0.1 copy.32
  134.3 0.1 pad_maximum_fusion.4
  134.5 0.1 copy.33
  134.6 0.2 broadcast_in_dim.27
  134.7 23.3 %all_to_all.31 = f32[8,224,256]{2,1,0:T(8,128)S(1)} all-to-all(f32[8,224,256]{2,1,0:T(8,128)S(1)} %broadcast_in_dim.27), channel_id=1, replica_groups=mesh['y'=4,'zl'=2,'co'=2,'x'=4,'zh'=2] {'y','zl'}, dimensions={0} | all-to-all | bytes 3670016 | tf_op jit(solution)/shard_map/all_to_all | solution.py:88
  158.1 4.0 %collective-permute-start.10 = (f32[8,224,256]{2,1,0:T(8,128)S(1)}, f32[8,224,256]{2,1,0:T(8,128)}, u32[]{:S(2)}, u32[]{:S(2)}) collective-permute-start(f32[8,224,256]{2,1,0:T(8,128)S(1)} %all_to_all.31), channel_id=1, source_target_pairs={{0,8},{8,0},{1,9},{9,1},{2,10},{10,2},{3,11},{11,3},{4,12},{12,4},... | collective-permute-start | bytes 5505032 | tf_op jit(solution)/shard_map/ppermute | solution.py:92
  162.1 0.1 copy.40
  162.2 0.7 collective-permute-start.11
  162.9 0.1 copy.34
  163.0 1.1 broadcast_in_dim.28
  164.0 16.8 %all-to-all-start.5 = ((f32[8,128,256]{2,1,0:T(8,128)}), f32[8,128,256]{2,1,0:T(8,128)}, u32[]{:S(2)}, u32[]{:S(2)}) async-start(f32[8,128,256]{2,1,0:T(8,128)} %broadcast_in_dim.28), calls=%async_computation.5 | async-start | bytes 2097152 | tf_op jit(solution)/shard_map/all_to_all | solution.py:88
  180.9 2.4 select_bitcast_fusion
  183.3 0.8 pad_maximum_fusion.2
  184.1 0.5 copy-done
  184.6 33.3 %shard_map.41 = f32[256,256]{1,0:T(8,128)} custom-call(f32[256,256]{1,0:T(8,128)} %bitcast.61), custom_call_target="tpu_custom_call" | custom-call | flops 671088640 | bytes 524288 | tf_op jit(solution)/shard_map/pallas_call | solution.py:76
  217.9 2.3 pad_maximum_fusion.1
  220.2 1.5 fusion.7
  221.7 1.1 convolution_multiply_fusion.2
  222.8 2.5 convolution_multiply_fusion.1
  225.3 0.4 fusion.23
  225.7 7.8 %convolution_subtract_fusion = f32[1024,1024]{1,0:T(8,128)} fusion(f32[1024,1024]{1,0:T(8,128)} %param.3, f32[1024,256]{0,1:T(8,128)S(1)} %convolution_multiply_fusion.2, f32[1024,256]{1,0:T(8,128)S(1)} %bitcast.57), kind=kOutput, calls=%fused_computation.8 | convolution fusion | flops 1611661312 | bytes 10485760 | tf_op jit(solution)/shard_map/dot_general | solution.py:31
  233.5 1.1 fusion.11
  234.7 0.4 copy-done.3
  235.1 15.5 %fusion.4 = f32[1024,2048]{1,0:T(8,128)} fusion(f32[1024,2048]{1,0:T(8,128)S(1)} %bitcast.47, f32[2048,256]{1,0:T(8,128)S(1)} %copy-done.3, f32[2048,256]{1,0:T(8,128)S(1)} %bitcast.55, f32[1024,256]{0,1:T(8,128)S(1)} %fusion.11, f32[1024,256]{0,1:T(8,128)S(1)} %convolution_multiply_fusion.2), kind=kOutput, calls=%fused_computation.4 | convolution fusion | flops 6446120960 | bytes 23068672 | tf_op jit(solution)/shard_map/dot_general | solution.py:31
  (37 shorter events, 0.2 us)
Async XLA Ops:
  2.2 13.8 %collective-permute-start = (f32[128,256]{1,0:T(8,128)S(1)}, f32[128,256]{1,0:T(8,128)S(1)}, u32[]{:S(2)}, u32[]{:S(2)}) collective-permute-start(f32[128,256]{1,0:T(8,128)S(1)} %get-tuple-element.12), channel_id=1, source_target_pairs={{0,7},{8,15},{16,23},{24,31},{32,39},{40,47},{48,55},{56,63},{64,7... | collective-permute-start | bytes 393224 | tf_op jit(solution)/shard_map/ppermute | solution.py:115
  10.7 6.5 %collective-permute-start.1 = (f32[128,256]{1,0:T(8,128)S(1)}, f32[128,256]{1,0:T(8,128)S(1)}, u32[]{:S(2)}, u32[]{:S(2)}) collective-permute-start(f32[128,256]{1,0:T(8,128)S(1)} %get-tuple-element.11), channel_id=1, source_target_pairs={{0,6},{8,14},{16,22},{24,30},{32,38},{40,46},{48,54},{56,62},{64,7... | collective-permute-start | bytes 393224 | tf_op jit(solution)/shard_map/ppermute | solution.py:115
  12.0 6.6 %collective-permute-start.2 = (f32[128,256]{1,0:T(8,128)S(1)}, f32[128,256]{1,0:T(8,128)S(1)}, u32[]{:S(2)}, u32[]{:S(2)}) collective-permute-start(f32[128,256]{1,0:T(8,128)S(1)} %get-tuple-element.10), channel_id=1, source_target_pairs={{0,5},{8,13},{16,21},{24,29},{32,37},{40,45},{48,53},{56,61},{64,6... | collective-permute-start | bytes 393224 | tf_op jit(solution)/shard_map/ppermute | solution.py:115
  13.3 5.3 %collective-permute-start.3 = (f32[128,256]{1,0:T(8,128)S(1)}, f32[128,256]{1,0:T(8,128)S(1)}, u32[]{:S(2)}, u32[]{:S(2)}) collective-permute-start(f32[128,256]{1,0:T(8,128)S(1)} %get-tuple-element.9), channel_id=1, source_target_pairs={{0,4},{8,12},{16,20},{24,28},{32,36},{40,44},{48,52},{56,60},{64,6... | collective-permute-start | bytes 393224 | tf_op jit(solution)/shard_map/ppermute | solution.py:115
  14.6 6.5 %collective-permute-start.4 = (f32[128,256]{1,0:T(8,128)S(1)}, f32[128,256]{1,0:T(8,128)S(1)}, u32[]{:S(2)}, u32[]{:S(2)}) collective-permute-start(f32[128,256]{1,0:T(8,128)S(1)} %get-tuple-element.8), channel_id=1, source_target_pairs={{0,3},{8,11},{16,19},{24,27},{32,35},{40,43},{48,51},{56,59},{64,6... | collective-permute-start | bytes 393224 | tf_op jit(solution)/shard_map/ppermute | solution.py:115
  15.9 7.9 %collective-permute-start.5 = (f32[128,256]{1,0:T(8,128)S(1)}, f32[128,256]{1,0:T(8,128)S(1)}, u32[]{:S(2)}, u32[]{:S(2)}) collective-permute-start(f32[128,256]{1,0:T(8,128)S(1)} %get-tuple-element.7), channel_id=1, source_target_pairs={{0,2},{8,10},{16,18},{24,26},{32,34},{40,42},{48,50},{56,58},{64,6... | collective-permute-start | bytes 393224 | tf_op jit(solution)/shard_map/ppermute | solution.py:115
  17.2 6.6 %collective-permute-start.6 = (f32[128,256]{1,0:T(8,128)S(1)}, f32[128,256]{1,0:T(8,128)S(1)}, u32[]{:S(2)}, u32[]{:S(2)}) collective-permute-start(f32[128,256]{1,0:T(8,128)S(1)} %get-tuple-element.6), channel_id=1, source_target_pairs={{0,1},{8,9},{16,17},{24,25},{32,33},{40,41},{48,49},{56,57},{64,65... | collective-permute-start | bytes 393224 | tf_op jit(solution)/shard_map/ppermute | solution.py:115
  25.0 17.5 %all-to-all-start = ((f32[8,128,256]{2,1,0:T(8,128)}), f32[8,128,256]{2,1,0:T(8,128)S(1)}, u32[]{:S(2)}, u32[]{:S(2)}) async-start(f32[8,128,256]{2,1,0:T(8,128)} %broadcast_in_dim.24), calls=%async_computation | async-start | bytes 2097152 | tf_op jit(solution)/shard_map/all_to_all | solution.py:88
  28.6 0.7 collective-permute-start.7
  43.6 24.0 %all-to-all-start.1 = ((f32[8,128,256]{2,1,0:T(8,128)}), f32[8,128,256]{2,1,0:T(8,128)}, u32[]{:S(2)}, u32[]{:S(2)}) async-start(f32[8,128,256]{2,1,0:T(8,128)} %broadcast_in_dim.25), calls=%async_computation.1 | async-start | bytes 2097152 | tf_op jit(solution)/shard_map/all_to_all | solution.py:88
  67.6 18.7 %collective-permute-start.8 = (f32[1024,256]{1,0:T(8,128)}, f32[1024,256]{1,0:T(8,128)}, u32[]{:S(2)}, u32[]{:S(2)}) collective-permute-start(f32[1024,256]{1,0:T(8,128)} %bitcast.9), channel_id=1, source_target_pairs={{0,8},{8,0},{1,9},{9,1},{2,10},{10,2},{3,11},{11,3},{4,12},{12,4},... | collective-permute-start | bytes 3145736 | tf_op jit(solution)/shard_map/ppermute | solution.py:92
  88.8 1.9 copy-start.2
  88.9 2.4 copy-start.4
  88.9 2.6 %copy-start.7 = (f32[1024,256]{1,0:T(8,128)S(1)}, f32[1024,256]{1,0:T(8,128)}, u32[]{:S(2)}) copy-start(f32[1024,256]{1,0:T(8,128)} %copy.27) | copy-start | bytes 3145732
  92.0 3.9 %collective-permute-start.9 = (f32[8,224,256]{2,1,0:T(8,128)S(1)}, f32[8,224,256]{2,1,0:T(8,128)S(1)}, u32[]{:S(2)}, u32[]{:S(2)}) collective-permute-start(f32[8,224,256]{2,1,0:T(8,128)S(1)} %select_bitcast_fusion.2), channel_id=1, source_target_pairs={{0,8},{8,0},{1,9},{9,1},{2,10},{10,2},{3,11},{11,3},{4,12},{12,4},... | collective-permute-start | bytes 5505032 | tf_op jit(solution)/shard_map/ppermute | solution.py:92
  122.7 11.5 %all-to-all-start.3 = ((f32[8,16,256]{2,1,0:T(8,128)}), f32[8,16,256]{2,1,0:T(8,128)S(1)}, u32[]{:S(2)}, u32[]{:S(2)}) async-start(f32[8,16,256]{2,1,0:T(8,128)} %broadcast_in_dim.26), calls=%async_computation.3 | async-start | bytes 262144 | tf_op jit(solution)/shard_map/all_to_all | solution.py:88
  158.1 22.8 %copy-start.6 = (f32[8,224,256]{2,1,0:T(8,128)}, f32[8,224,256]{2,1,0:T(8,128)S(1)}, u32[]{:S(2)}) copy-start(f32[8,224,256]{2,1,0:T(8,128)S(1)} %all_to_all.31) | copy-start | bytes 5505028
  158.1 22.8 %collective-permute-start.10 = (f32[8,224,256]{2,1,0:T(8,128)S(1)}, f32[8,224,256]{2,1,0:T(8,128)}, u32[]{:S(2)}, u32[]{:S(2)}) collective-permute-start(f32[8,224,256]{2,1,0:T(8,128)S(1)} %all_to_all.31), channel_id=1, source_target_pairs={{0,8},{8,0},{1,9},{9,1},{2,10},{10,2},{3,11},{11,3},{4,12},{12,4},... | collective-permute-start | bytes 5505032 | tf_op jit(solution)/shard_map/ppermute | solution.py:92
  162.2 0.7 collective-permute-start.11
  164.0 58.8 %all-to-all-start.5 = ((f32[8,128,256]{2,1,0:T(8,128)}), f32[8,128,256]{2,1,0:T(8,128)}, u32[]{:S(2)}, u32[]{:S(2)}) async-start(f32[8,128,256]{2,1,0:T(8,128)} %broadcast_in_dim.28), calls=%async_computation.5 | async-start | bytes 2097152 | tf_op jit(solution)/shard_map/all_to_all | solution.py:88
  183.3 1.3 copy-start
  217.9 2.3 copy-start.1
  220.2 1.5 copy-start.9
  222.8 2.9 %copy-start.8 = (f32[2,8,64,256]{3,2,1,0:T(8,128)S(1)}, f32[2,8,64,256]{3,2,1,0:T(8,128)}, u32[]{:S(2)}) copy-start(f32[2,8,64,256]{3,2,1,0:T(8,128)} %pad_maximum_fusion.1) | copy-start | bytes 3145732
  222.8 11.8 %slice-start = ((s8[8388608]{0:T(1024)(128)(4,1)}), s8[4194304]{0:T(1024)(128)(4,1)S(1)}, s32[]{:S(2)}) async-start(s8[8388608]{0:T(1024)(128)(4,1)} %bitcast.46), calls=%async_computation.6 | async-start | bytes 8388608
  225.7 9.0 %slice-start.1 = ((s8[8388608]{0:T(1024)(128)(4,1)}), s8[4194304]{0:T(1024)(128)(4,1)S(1)}, s32[]{:S(2)}) async-start(s8[8388608]{0:T(1024)(128)(4,1)} %bitcast.46), calls=%async_computation.7 | async-start | bytes 8388608
  225.7 9.0 %copy-start.5 = (f32[2,8,128,256]{3,2,1,0:T(8,128)S(1)}, f32[2,8,128,256]{3,2,1,0:T(8,128)}, u32[]{:S(2)}) copy-start(f32[2,8,128,256]{3,2,1,0:T(8,128)} %fusion.7) | copy-start | bytes 6291460
  233.5 1.6 copy-start.3

commit v2 on v1

v2 whole, which is shorter than its diff:
```python
import jax
import jax.numpy as jnp
from jax import lax
from jax.experimental import pallas as pl
from jax.experimental.pallas import tpu as pltpu
from jax.sharding import Mesh
from jax.sharding import PartitionSpec as P

B = 256
ROW = ("y", "zl", "co")
CHIPS = ("y", "zl")
COL = ("x", "zh")
COUPLED = ("co", "x", "zh")
ALL = ("y", "zl", "co", "x", "zh")
HIGHEST = lax.Precision.HIGHEST
F32 = jnp.float32
BF16 = jnp.bfloat16
NN = (((1,), (0,)), ((), ()))
NT = (((1,), (1,)), ((), ()))
TN = (((0,), (0,)), ((), ()))


def dot(left, right, dims=NN):
    return lax.dot_general(left, right, dims, preferred_element_type=F32, precision=HIGHEST)


def split(x):
    hi = x.astype(BF16)
    return hi, (x - hi.astype(F32)).astype(BF16)


def dot3(left, right, dims=NN):
    (ah, al), (bh, bl) = left, right
    f = lambda a, b: lax.dot_general(a, b, dims, preferred_element_type=F32)
    return f(ah, bh) + (f(ah, bl) + f(al, bh))


def call(kernel, out_shape, us, mib=8, **kw):
    cost = pl.CostEstimate(flops=int(us * 1e9), bytes_accessed=1024, transcendentals=0)
    params = pltpu.CompilerParams(vmem_limit_bytes=mib * 1024 * 1024)
    return pl.pallas_call(kernel, out_shape=out_shape, cost_estimate=cost, compiler_params=params, **kw)


def f32(*shape):
    return jax.ShapeDtypeStruct(shape, F32)


def sweep_all(block):
    n, group = 128, 16
    lane = lax.broadcasted_iota(jnp.int32, (8, n), 1)
    line = lax.broadcasted_iota(jnp.int32, (8, n), 0)
    tiles = n // 8

    def step(_, s):
        s = list(s)
        for k in range(0, group, 2):
            t, sub = k // 8, k % 8
            r0 = jnp.broadcast_to(s[t][sub : sub + 1, :], (8, n))
            r1 = jnp.broadcast_to(s[t][sub + 1 : sub + 2, :], (8, n))
            a = jnp.broadcast_to(r0[:, k : k + 1], (8, n))
            b = jnp.broadcast_to(r1[:, k : k + 1], (8, n))
            d = jnp.broadcast_to(r1[:, k + 1 : k + 2], (8, n))
            scale = 1.0 / (a * d - b * b)
            ia, ib, ic = d * scale, -b * scale, a * scale
            q0 = jnp.where(lane == k, -ia, jnp.where(lane == k + 1, -ib, ia * r0 + ib * r1))
            q1 = jnp.where(lane == k, -ib, jnp.where(lane == k + 1, -ic, ib * r0 + ic * r1))
            pivots = (lane == k) | (lane == k + 1)
            for u in range(tiles):
                c0 = jnp.broadcast_to(s[u][:, k : k + 1], (8, n))
                c1 = jnp.broadcast_to(s[u][:, k + 1 : k + 2], (8, n))
                new = jnp.where(pivots, 0.0, s[u]) - c0 * q0 - c1 * q1
                if u == t:
                    new = jnp.where(line == sub, q0, jnp.where(line == sub + 1, q1, new))
                s[u] = new
        s = s[group // 8 :] + s[: group // 8]
        return tuple(pltpu.roll(v, n - group, 1) for v in s)

    out = lax.fori_loop(0, n // group, step, tuple(block[8 * u : 8 * u + 8, :] for u in range(tiles)))
    return jnp.concatenate(out, axis=0)


def invert_first(gram_ref, ai_ref, t_ref, schur_ref):
    def part(lo, lanes):
        return jnp.concatenate([gram_ref[m, 32 * lanes : 32 * lanes + 32, :] for m in range(lo, lo + 4)], axis=0)

    b = part(0, 1)
    ai = -sweep_all(part(0, 0))
    t = dot(ai, b)
    ai_ref[...] = ai
    t_ref[...] = t
    schur_ref[...] = part(4, 1) - dot(b, t, TN)


def invert_second(ai_ref, t_ref, schur_ref, out_ref):
    h = B // 2
    t = t_ref[...]
    si = -sweep_all(schur_ref[...])
    u = dot(t, si)
    out_ref[:h, :h] = ai_ref[...] + dot(u, t, NT)
    out_ref[:h, h:] = -u
    out_ref[h:, :h] = -u.T
    out_ref[h:, h:] = si


def choose_kernel(col_ref, *refs):
    parts, (out_ref, turned_ref) = refs[:8], refs[8:]
    mine = parts[0][...]
    for k in range(1, 8):
        mine = jnp.where(col_ref[0] == k, parts[k][...], mine)
    for k in range(8):
        out_ref[k] = mine
    turned_ref[...] = mine.T


def gram_kernel(panel_ref, out_ref):
    gram = dot(panel_ref[...].T, panel_ref[...]).reshape(8, 32, B)
    out_ref[:, :32, :] = gram[:, :, :128]
    out_ref[:, 32:, :] = gram[:, :, 128:]


def product_kernel(core_ref, panel_ref, matrix_ref, vectors_ref, keep_ref, give_ref, hi_ref, lo_ref):
    step = pl.program_id(0)
    core = core_ref[0]

    def put(own, both, place):
        @pl.when(own == core)
        def _():
            keep_ref[:, place, :] = both[0]
            give_ref[:, place, :] = both[1]

        @pl.when(own != core)
        def _():
            keep_ref[:, place, :] = both[1]
            give_ref[:, place, :] = both[0]

    @pl.when(step == 0)
    def _():
        hi_ref[...], lo_ref[...] = split(panel_ref[...].T)

    panel = hi_ref[...], lo_ref[...]
    product = dot3(panel, split(matrix_ref[...]))
    mixing = dot3(panel, split(vectors_ref[...])).reshape(2, 8, 16, 128)
    m = (2 * step) % 8
    put(0, mixing, pl.ds(pl.multiple_of(256 + 16 * step, 16), 16))

    @pl.when(step // 4 == core)
    def _():
        keep_ref[m, :256, :] = product[:, :128]
        keep_ref[m + 1, :256, :] = product[:, 128:]

    @pl.when(step // 4 != core)
    def _():
        give_ref[m, :256, :] = product[:, :128]
        give_ref[m + 1, :256, :] = product[:, 128:]


def join_kernel(keep_ref, got_ref, gram_ref, other_ref, out_ref):
    out_ref[:, :384, :] = keep_ref[...] + got_ref[...]
    gram = gram_ref[...] + other_ref[...]
    for m in range(8):
        out_ref[m, 384:, :] = gram


def reduce_kernel(in_ref, turned_ref, product_ref, gram_ref, out_ref):
    own = in_ref[0, :384, :]
    for m in range(1, 8):
        own = own + in_ref[m, :384, :]
    product_ref[...] = own[:256].T
    gram_ref[...] = in_ref[:, 384:, :]
    for m in range(8):
        out_ref[m, :384, :] = own
        out_ref[m, 384:, :] = turned_ref[...]


def coupling_kernel(panel_ref, product_ref, out_ref):
    total = jnp.zeros((B, B), F32)
    for m in range(0, 8, 2):
        left = jnp.concatenate([panel_ref[m], panel_ref[m + 1]], axis=1)
        right = jnp.concatenate([product_ref[m], product_ref[m + 1]], axis=1)
        total = total + dot3(split(left), split(right), NT)
    out_ref[...] = total.reshape(16, 16, B)


def sum_kernel(in_ref, out_ref):
    total = jnp.sum(in_ref[...], axis=0)
    for m in range(out_ref.shape[0]):
        out_ref[m] = total


def rotate_kernel(core_ref, panel_ref, inverse_ref, mine_ref, other_ref, vectors_ref, out_ref, u_ref, left_ref):
    @pl.when(pl.program_id(0) == 0)
    def _():
        u = 2.0 * dot(panel_ref[...], inverse_ref[...])
        u_ref[...] = u
        hi, lo = split(u)
        left_ref[:, :256], left_ref[:, 256:512], left_ref[:, 512:] = hi, hi, lo

    core = core_ref[0]
    mine, other = mine_ref[...], other_ref[...]
    both = jnp.where(core == 0, mine, other), jnp.where(core == 0, other, mine)
    lanes = [jnp.concatenate([h[:, k : k + 16, :].reshape(128, 128) for h in both], axis=0) for k in (0, 16)]
    hi, lo = split(jnp.concatenate(lanes, axis=1))
    right = jnp.concatenate([hi, lo, hi], axis=0)
    out_ref[...] = vectors_ref[...] - lax.dot_general(left_ref[...], right, NN, preferred_element_type=F32)


def update_kernel(
    where_ref, u_ref, near_ref, far_ref, inverse_ref, coupling_ref,
    mine_ref, other_ref, pmine_ref, pother_ref, matrix_ref, out_ref, left_ref, product_ref,
):
    step = pl.program_id(0)

    @pl.when(step == 0)
    def _():
        for k in range(4):
            for piece_ref, zh in ((near_ref, where_ref[2]), (far_ref, 1 - where_ref[2])):
                place = (lax.rem(where_ref[1] + k, 4) * 2 + zh) * 128
                product_ref[pl.ds(pl.multiple_of(place, 128), 128), :] = piece_ref[k]
        small = dot(coupling_ref[...].reshape(B, B), inverse_ref[...])
        u1 = u_ref[...]
        u2 = 2.0 * dot(product_ref[...], inverse_ref[...]) - 2.0 * dot(u1, small)
        for k, u in ((0, u1), (256, u2)):
            hi, lo = split(u)
            left_ref[:, k : k + 256], left_ref[:, k + 512 : k + 768], left_ref[:, k + 1024 : k + 1280] = hi, hi, lo

    mine = step // 4 == where_ref[0]
    product = jnp.where(mine, mine_ref[...], other_ref[...])
    panel = jnp.where(mine, pmine_ref[...], pother_ref[...])
    hi, lo = split(
        jnp.concatenate(
            [jnp.concatenate([product[0], product[1]], axis=1), jnp.concatenate([panel[0], panel[1]], axis=1)], axis=0
        )
    )
    right = jnp.concatenate([hi, lo, hi], axis=0)
    out_ref[...] = matrix_ref[...] - lax.dot_general(left_ref[...], right, NN, preferred_element_type=F32)


def repeat(block, n=8):
    return jnp.broadcast_to(block[None], (n,) + block.shape)


def exchange(blocks, axes):
    return lax.all_to_all(blocks, axes, 0, 0, tiled=True)


def swap_cores(array):
    return lax.ppermute(array, "co", [(0, 1), (1, 0)])


def gather_x(block):
    return jnp.stack([block] + [lax.ppermute(block, "x", [((x + k) % 4, x) for x in range(4)]) for k in (1, 2, 3)])


def flip_pairs():
    pairs = []
    for i in range(16):
        for k in range(8):
            pairs.append((i * 8 + k, (k * 2 + i % 2) * 8 + i // 2))
    return pairs


VMEM = pl.BlockSpec(memory_space=pltpu.VMEM)
SMEM = pl.BlockSpec(memory_space=pltpu.SMEM)


def whole(*shape):
    return pl.BlockSpec(shape, lambda t: (0,) * len(shape))


def body(matrix, vectors):
    rows_here = matrix.shape[0]
    row_index = lax.axis_index(ROW)
    col_index = lax.axis_index(COL)
    core = lax.axis_index("co").astype(jnp.int32).reshape(1)
    where = jnp.stack([core[0], lax.axis_index("x").astype(jnp.int32), lax.axis_index("zh").astype(jnp.int32)])
    there = flip_pairs()
    back = [(b, a) for a, b in there]

    global_rows = row_index * rows_here + jnp.arange(rows_here, dtype=jnp.int32)
    panel = jnp.where(global_rows[:, None] >= B, matrix[:, :B], F32(0.0))
    parts = [panel[:128]]
    for k in range(1, 8):
        parts.append(lax.ppermute(panel[k * 128 : (k + 1) * 128], COL, [(0, k)]))
    sent, turned = call(
        choose_kernel, (f32(8, 128, 256), f32(256, 128)), 1, in_specs=[SMEM] + [VMEM] * 8
    )(col_index.astype(jnp.int32).reshape(1), *parts)
    panel_rows, turned = lax.optimization_barrier((exchange(sent, COL).reshape(1024, B), turned))
    turned = lax.ppermute(turned, ALL, there)
    wide = whole(8, 384, 128)
    gram = exchange(call(gram_kernel, f32(8, 64, 128), 1)(panel_rows), CHIPS)
    keep, give = call(
        product_kernel,
        (f32(8, 384, 128), f32(8, 384, 128)),
        12,
        60,
        grid=(8,),
        in_specs=[
            SMEM,
            whole(1024, 256),
            pl.BlockSpec((1024, 256), lambda t: (0, t)),
            pl.BlockSpec((1024, 128), lambda t: (0, t)),
        ],
        out_specs=(wide, wide),
        scratch_shapes=[pltpu.VMEM((256, 1024), BF16), pltpu.VMEM((256, 1024), BF16)],
    )(core, panel_rows, matrix, vectors)
    keep, give, turned, gram = lax.optimization_barrier((keep, give, turned, gram))
    gram = jnp.sum(gram, axis=0)
    came = exchange(
        call(join_kernel, f32(8, 448, 128), 1, 12)(keep, swap_cores(give), gram, swap_cores(gram)), CHIPS
    )

    product, gram, sent = call(reduce_kernel, (f32(128, 256), f32(8, 64, 128), f32(8, 640, 128)), 2, 12)(came, turned)
    final = exchange(sent, CHIPS)
    near = gather_x(lax.ppermute(product, ALL, back))
    ai, t, schur = call(invert_first, (f32(128, 128),) * 3, 9)(gram)
    inverse = call(invert_second, f32(B, B), 9)(ai, t, schur)
    final, near, inverse = lax.optimization_barrier((final, near, inverse))
    other = swap_cores(final)
    far = lax.ppermute(near, "zh", [(0, 1), (1, 0)])
    coupling = call(
        coupling_kernel,
        f32(16, 16, 256),
        2,
        grid=(1,),
        in_specs=[
            pl.BlockSpec((pl.Element(8), pl.Element(256), pl.Element(128)), lambda t: (0, 384, 0)),
            pl.BlockSpec((8, 256, 128), lambda t: (0, 0, 0)),
        ],
        out_specs=whole(16, 16, 256),
    )(final, final)
    coupling = call(sum_kernel, f32(16, 16, 256), 1)(exchange(coupling, COUPLED))
    coupling = exchange(coupling, COUPLED)

    mixing = pl.BlockSpec((8, 32, 128), lambda t: (0, 8 + t, 0))
    rotated, u = call(
        rotate_kernel,
        (f32(1024, 1024), f32(1024, 256)),
        6,
        60,
        grid=(4,),
        in_specs=[
            SMEM, whole(1024, 256), whole(256, 256), mixing, mixing, pl.BlockSpec((1024, 256), lambda t: (0, t)),
        ],
        out_specs=(pl.BlockSpec((1024, 256), lambda t: (0, t)), whole(1024, 256)),
        scratch_shapes=[pltpu.VMEM((1024, 768), BF16)],
    )(core, panel_rows, inverse, final, other, vectors)

    coupling, rotated, u = lax.optimization_barrier((coupling, rotated, u))
    pair = pl.BlockSpec((2, 256, 128), lambda t: (t % 4, 0, 0))
    piece = whole(4, 128, 256)
    panel_pair = pl.BlockSpec((pl.Element(2), pl.Element(256), pl.Element(128)), lambda t: (2 * (t % 4), 384, 0))
    updated = call(
        update_kernel,
        f32(1024, 2048),
        12,
        60,
        grid=(8,),
        in_specs=[
            SMEM, whole(1024, 256), piece, piece, whole(256, 256), whole(16, 16, 256), pair, pair, panel_pair,
            panel_pair, pl.BlockSpec((1024, 256), lambda t: (0, t)),
        ],
        out_specs=pl.BlockSpec((1024, 256), lambda t: (0, t)),
        scratch_shapes=[pltpu.VMEM((1024, 1536), BF16), pltpu.VMEM((1024, 256), F32)],
    )(where, u, near, far, inverse, coupling, final, other, final, other, matrix)
    return (updated, rotated)


def solution(mesh):
    fine = Mesh(mesh.devices.reshape(4, 2, 2, 4, 2), ALL)
    placed = (P(ROW, COL), P(ROW, COL))
    return jax.shard_map(body, mesh=fine, in_specs=placed, out_specs=placed, check_vma=False)
```

time: 251 us -> 197 us (0.78)
  matrix products: 42.6 us -> 0 us
  Pallas kernels: 33.3 us -> 61 us
  waiting for transfers between devices: 41.3 us -> 21.9 us
  other arithmetic: 12.1 us -> 2.06 us
  local copies, waits for them, and re-layouts: 10.7 us -> 4.41 us
  blocking collectives: 49 us -> 44.7 us
    dot_general x10 -> x0, matrix products: 42.6 us -> none  [the longest x2 23.3 us: nt(): lax.dot_general(left, right, (((1,), (1,)), ((), ())), preferred_element_...]
    pallas_call x1 -> x11, Pallas kernels: 33.3 us -> 61 us  [the longest x1 17 us: body(): call(update_kernel, f32(1024, 2048), 12, 60, grid=(8,), in_specs=[SMEM, w...]
    all_to_all x4, waiting for transfers between devices: 32.3 us -> 13.4 us  [exchange(): return lax.all_to_all(blocks, axes, 0, 0, tiled=True)]
    ppermute x9 -> x13, starting transfers between devices: 17.7 us -> 29.5 us  [the longest x7 16.3 us: body(): parts.append(lax.ppermute(panel[k * 128:(k + 1) * 128], COL, [(0, k)]))]
    all_to_all x4, starting transfers between devices: 35.5 us -> 24.6 us  [exchange(): return lax.all_to_all(blocks, axes, 0, 0, tiled=True)]
    another operation x3 -> x2, other arithmetic: 6.16 us -> 0.61 us  [the longest x1 0.58 us: body(): jnp.stack([core[0], lax.axis_index('x').astype(jnp.int32), lax.axis_index...]
    all_to_all x2, blocking collectives: 49 us -> 44.7 us  [exchange(): return lax.all_to_all(blocks, axes, 0, 0, tiled=True)]
    broadcast_in_dim x5 -> x0, local copies, waits for them, and re-layouts: 3.98 us -> none  [repeat(): return jnp.broadcast_to(block[None], (n,) + block.shape)]
  transfers between devices with their start and end apart: 16 -> 20, of which waited for: 6 -> 7; matrix products, arithmetic and copies ran while one was open for 11% -> 0% of each run, Pallas kernels for 13% -> 22%
where the time goes in v2:
time: 197 us; the launch traced here: 196 us
  Pallas kernels  61 us (31%)
  starting transfers between devices  60.8 us (31%)
  blocking collectives  44.7 us (23%)
  waiting for transfers between devices  21.9 us (11%)
  local copies, waits for them, and re-layouts  4.41 us (2%)
  other arithmetic  2.06 us (1%)
    all_to_all x2, blocking collectives, exchange(): return lax.all_to_all(blocks, axes, 0, 0, tiled=True)  44.7 us
    all_to_all x4, starting transfers between devices, exchange(): return lax.all_to_all(blocks, axes, 0, 0, tiled=True)  24.6 us
    pallas_call x1, Pallas kernels, body(): call(update_kernel, f32(1024, 2048), 12, 60, grid=(8,), in_specs=[SMEM, w...  17 us
    ppermute x7, starting transfers between devices, body(): parts.append(lax.ppermute(panel[k * 128:(k + 1) * 128], COL, [(0, k)]))  16.3 us
    pallas_call x1, Pallas kernels, body(): call(product_kernel, (f32(8, 384, 128), f32(8, 384, 128)), 12, 60, grid=(...  13.6 us
    all_to_all x4, waiting for transfers between devices, exchange(): return lax.all_to_all(blocks, axes, 0, 0, tiled=True)  13.4 us
    pallas_call x1, Pallas kernels, body(): inverse = call(invert_second, f32(B, B), 9)(ai, t, schur)  9.09 us
    pallas_call x1, Pallas kernels, body(): ai, t, schur = call(invert_first, (f32(128, 128),) * 3, 9)(gram)  9.04 us
  transfers between devices with their start and end apart: 20, of which 7 were waited for; matrix products, arithmetic and copies ran while one was open for 0% of the time, Pallas kernels for 22%

profile of v2, /device:TPU:1, one launch (start us, length us, event | category | flops | bytes accessed | tf_op | source)
XLA Modules:
  0.0 195.8 jit_solution(11872503749988916652)
XLA Ops:
  0.7 1.4 slice_select_fusion
  2.1 0.1 fusion
  2.2 8.5 %collective-permute-start.6 = (f32[128,256]{1,0:T(8,128)S(1)}, f32[128,256]{1,0:T(8,128)S(1)}, u32[]{:S(2)}, u32[]{:S(2)}) collective-permute-start(f32[128,256]{1,0:T(8,128)S(1)} %get-tuple-element.50), channel_id=1, source_target_pairs={{0,7},{8,15},{16,23},{24,31},{32,39},{40,47},{48,55},{56,63},{64,7... | collective-permute-start | bytes 393224 | tf_op jit(solution)/shard_map/ppermute | solution.py:283
  10.7 1.3 collective-permute-start.5
  12.0 1.3 collective-permute-start.4
  13.3 1.3 collective-permute-start.3
  14.6 1.3 collective-permute-start.2
  15.9 0.0 collective-permute-done.6.refs_7_
  16.0 1.3 collective-permute-start.1
  17.3 0.0 collective-permute-done.5.refs_6_
  17.3 1.3 collective-permute-start
  18.6 0.0 collective-permute-done.4.refs_5_
  18.6 0.0 collective-permute-done.3.refs_4_
  18.6 2.5 %collective-permute-done.2.refs_3_ = f32[128,256]{1,0:T(8,128)S(1)} collective-permute-done((f32[128,256]{1,0:T(8,128)S(1)}, f32[128,256]{1,0:T(8,128)S(1)}, u32[]{:S(2)}, u32[]{:S(2)}) %collective-permute-start.2) | collective-permute-done | bytes 131104 | tf_op jit(solution)/shard_map/ppermute | solution.py:283
  21.1 2.8 %collective-permute-done.1.refs_2_ = f32[128,256]{1,0:T(8,128)S(1)} collective-permute-done((f32[128,256]{1,0:T(8,128)S(1)}, f32[128,256]{1,0:T(8,128)S(1)}, u32[]{:S(2)}, u32[]{:S(2)}) %collective-permute-start.1) | collective-permute-done | bytes 131104 | tf_op jit(solution)/shard_map/ppermute | solution.py:283
  23.9 0.0 collective-permute-done.refs_1_
  23.9 0.1 shard_map.41
  24.0 16.9 %all_to_all.30 = f32[8,128,256]{2,1,0:T(8,128)S(1)} all-to-all(f32[8,128,256]{2,1,0:T(8,128)S(1)} %get-tuple-element.26), channel_id=1, replica_groups=mesh['y'=4,'zl'=2,'co'=2,'x'=4,'zh'=2] {'x','zh'}, dimensions={0} | all-to-all | bytes 2097152 | tf_op jit(solution)/shard_map/all_to_all | solution.py:243
  40.9 0.7 collective-permute-start.7
  41.6 1.9 shard_map.43
  43.5 6.7 %all-to-all-start.1 = ((f32[8,64,128]{2,1,0:T(8,128)}), f32[8,64,128]{2,1,0:T(8,128)S(1)}, u32[]{:S(2)}, u32[]{:S(2)}) async-start(f32[8,64,128]{2,1,0:T(8,128)} %shard_map.43), calls=%async_computation.1 | async-start | bytes 524288 | tf_op jit(solution)/shard_map/all_to_all | solution.py:243
  50.2 0.0 copy-done.3
  50.2 13.6 %shard_map.42 = (f32[8,384,128]{2,1,0:T(8,128)}, f32[8,384,128]{2,1,0:T(8,128)}) custom-call(s32[1]{0:T(128)} %bitcast.core_ref, f32[1024,256]{1,0:T(8,128)} %bitcast.10, f32[1024,2048]{1,0:T(8,128)} %matrix_ref.3, f32[1024,1024]{1,0:T(8,128)} %vectors_ref.3), custom_call_target="tpu_custom_call" | custom-call | flops 12000000000 | bytes 1024 | tf_op jit(solution)/shard_map/pallas_call | solution.py:291
  63.8 0.0 collective-permute-done.7.turned_ref
  63.8 0.0 all-to-all-done.1
  63.8 4.5 %collective-permute-start.8 = (f32[8,384,128]{2,1,0:T(8,128)}, f32[8,384,128]{2,1,0:T(8,128)S(1)}, u32[]{:S(2)}, u32[]{:S(2)}) collective-permute-start(f32[8,384,128]{2,1,0:T(8,128)} %get-tuple-element.33), channel_id=1, source_target_pairs={{0,8},{8,0},{1,9},{9,1},{2,10},{10,2},{3,11},{11,3},{4,12},{12,4},... | collective-permute-start | bytes 4718600 | tf_op jit(solution)/shard_map/ppermute | solution.py:247
  68.3 0.1 collective-permute-start.9
  68.4 2.8 %collective-permute-done.9.other_ref = f32[64,128]{1,0:T(8,128)S(1)} collective-permute-done((f32[64,128]{1,0:T(8,128)S(1)}, f32[64,128]{1,0:T(8,128)S(1)}, u32[]{:S(2)}, u32[]{:S(2)}) %collective-permute-start.9) | collective-permute-done | bytes 32800 | tf_op jit(solution)/shard_map/ppermute | solution.py:247
  71.2 0.3 collective-permute-done.8.got_ref
  71.5 1.4 copy-done.2
  72.9 0.2 shard_map.44
  73.1 27.9 %all_to_all.31.in_ref = f32[8,448,128]{2,1,0:T(8,128)S(1)} all-to-all(f32[8,448,128]{2,1,0:T(8,128)S(1)} %shard_map.44), channel_id=1, replica_groups=mesh['y'=4,'zl'=2,'co'=2,'x'=4,'zh'=2] {'y','zl'}, dimensions={0} | all-to-all | bytes 3670016 | tf_op jit(solution)/shard_map/all_to_all | solution.py:243
  101.0 0.3 shard_map.45
  101.3 0.0 copy-start.1
  101.3 1.5 copy-done.1
  102.8 3.7 %all-to-all-start.3 = ((f32[8,640,128]{2,1,0:T(8,128)}), f32[8,640,128]{2,1,0:T(8,128)S(1)}, u32[]{:S(2)}, u32[]{:S(2)}) async-start(f32[8,640,128]{2,1,0:T(8,128)} %copy-done.1), calls=%async_computation.3 | async-start | bytes 5242880 | tf_op jit(solution)/shard_map/all_to_all | solution.py:243
  106.5 0.7 collective-permute-start.10
  107.1 9.0 %shard_map.46 = (f32[128,128]{1,0:T(8,128)S(1)}, f32[128,128]{1,0:T(8,128)S(1)}, f32[128,128]{1,0:T(8,128)S(1)}) custom-call(f32[8,64,128]{2,1,0:T(8,128)S(1)} %get-tuple-element.38.gram_ref), custom_call_target="tpu_custom_call" | custom-call | flops 8999999488 | bytes 1024 | tf_op jit(solution)/shard_map/pallas_call | solution.py:315
  116.2 0.0 collective-permute-done.10
  116.2 4.0 %collective-permute-start.13 = (f32[128,256]{1,0:T(8,128)S(1)}, f32[128,256]{1,0:T(8,128)S(1)}, u32[]{:S(2)}, u32[]{:S(2)}) collective-permute-start(f32[128,256]{1,0:T(8,128)S(1)} %collective-permute-done.10), channel_id=1, source_target_pairs={{6,0},{0,2},{2,4},{4,6},{7,1},{1,3},{3,5},{5,7},{14,8},{8,10},{10,... | collective-permute-start | bytes 393224 | tf_op jit(solution)/shard_map/ppermute | solution.py:251
  120.2 3.6 %collective-permute-start.12 = (f32[128,256]{1,0:T(8,128)S(1)}, f32[128,256]{1,0:T(8,128)S(1)}, u32[]{:S(2)}, u32[]{:S(2)}) collective-permute-start(f32[128,256]{1,0:T(8,128)S(1)} %collective-permute-done.10), channel_id=1, source_target_pairs={{4,0},{6,2},{0,4},{2,6},{5,1},{7,3},{1,5},{3,7},{12,8},{14,10},{8,... | collective-permute-start | bytes 393224 | tf_op jit(solution)/shard_map/ppermute | solution.py:251
  123.8 1.5 collective-permute-start.11
  125.2 9.1 %shard_map.47.inverse_ref = f32[256,256]{1,0:T(8,128)S(1)} custom-call(f32[128,128]{1,0:T(8,128)S(1)} %get-tuple-element.39.ai_ref, f32[128,128]{1,0:T(8,128)S(1)} %get-tuple-element.40.t_ref, f32[128,128]{1,0:T(8,128)S(1)} %get-tuple-element.41.schur_ref), custom_call_target="tpu_custom_call" | custom-call | flops 8999999488 | bytes 1024 | tf_op jit(solution)/shard_map/pallas_call | solution.py:316
  134.3 0.0 copy-start.4
  134.3 0.7 copy-done.4
  135.0 0.0 collective-permute-done.13
  135.0 0.0 collective-permute-done.12
  135.0 0.0 collective-permute-done.11
  135.1 7.2 %all-to-all-done.3.panel_ref.product_ref.mine_ref.pmine_ref = f32[8,640,128]{2,1,0:T(8,128)S(1)} async-done(((f32[8,640,128]{2,1,0:T(8,128)}), f32[8,640,128]{2,1,0:T(8,128)S(1)}, u32[]{:S(2)}, u32[]{:S(2)}) %all-to-all-start.3) | async-done | bytes 2621472 | tf_op jit(solution)/shard_map/all_to_all | solution.py:243
  142.3 2.1 %collective-permute-start.14 = (f32[8,640,128]{2,1,0:T(8,128)S(1)}, f32[8,640,128]{2,1,0:T(8,128)}, u32[]{:S(2)}, u32[]{:S(2)}) collective-permute-start(f32[8,640,128]{2,1,0:T(8,128)S(1)} %all-to-all-done.3.panel_ref.product_ref.mine_ref.pmine_ref), channel_id=1, source_target_pairs={{0,8},{8,0},{1,9},{9,1},{2,10},{10,2},{3,11},{11,3},{4,12},{12,4},... | collective-permute-start | bytes 7864328 | tf_op jit(solution)/shard_map/ppermute | solution.py:247
  144.5 1.3 shard_map.48
  145.8 0.0 copy-done
  145.8 9.7 %all-to-all-start.4 = ((f32[16,16,256]{2,1,0:T(8,128)}), f32[16,16,256]{2,1,0:T(8,128)S(1)}, u32[]{:S(2)}, u32[]{:S(2)}) async-start(f32[16,16,256]{2,1,0:T(8,128)} %shard_map.48), calls=%async_computation.4 | async-start | bytes 524288 | tf_op jit(solution)/shard_map/all_to_all | solution.py:243
  155.5 0.6 pad_add_fusion.where_ref
  156.1 2.9 %collective-permute-start.15 = (f32[4,128,256]{2,1,0:T(8,128)S(1)}, f32[4,128,256]{2,1,0:T(8,128)}, u32[]{:S(2)}, u32[]{:S(2)}) collective-permute-start(f32[4,128,256]{2,1,0:T(8,128)S(1)} %pad_maximum_fusion.near_ref), channel_id=1, source_target_pairs={{0,1},{1,0},{2,3},{3,2},{4,5},{5,4},{6,7},{7,6},{8,9},{9,8},{10,11... | collective-permute-start | bytes 1572872 | tf_op jit(solution)/shard_map/ppermute | solution.py:319
  159.0 5.2 %all-to-all-done.4.in_ref = f32[16,16,256]{2,1,0:T(8,128)S(1)} async-done(((f32[16,16,256]{2,1,0:T(8,128)}), f32[16,16,256]{2,1,0:T(8,128)S(1)}, u32[]{:S(2)}, u32[]{:S(2)}) %all-to-all-start.4) | async-done | bytes 262176 | tf_op jit(solution)/shard_map/all_to_all | solution.py:243
  164.2 0.7 shard_map.49
  164.9 4.5 %all-to-all-start.5 = ((f32[16,16,256]{2,1,0:T(8,128)}), f32[16,16,256]{2,1,0:T(8,128)S(1)}, u32[]{:S(2)}, u32[]{:S(2)}) async-start(f32[16,16,256]{2,1,0:T(8,128)} %shard_map.49), calls=%async_computation.5 | async-start | bytes 524288 | tf_op jit(solution)/shard_map/all_to_all | solution.py:243
  169.4 0.0 collective-permute-done.14.other_ref.pother_ref
  169.4 7.7 %shard_map.50 = (f32[1024,1024]{1,0:T(8,128)}, f32[1024,256]{1,0:T(8,128)}) custom-call(s32[1]{0:T(128)} %bitcast.core_ref, f32[1024,256]{1,0:T(8,128)} %bitcast.11, f32[256,256]{1,0:T(8,128)} %copy-done.4, f32[8,640,128]{2,1,0:T(8,128)} %copy-done, f32[8,640,128]{2,1,0:T(8,128)} %collective-permute-done.14.other_ref.pother_ref, f32[1024,1024]{1,0:T(8,128)} %vectors_ref.3), custom_call_target="tpu_custom_call" | custom-call | flops 6000000000 | bytes 1024 | tf_op jit(solution)/shard_map/pallas_call | solution.py:335
  177.1 0.9 all-to-all-done.5.coupling_ref
  178.0 0.0 collective-permute-done.15.far_ref
  178.0 0.7 copy-done.6
  178.8 17.0 %shard_map.51 = f32[1024,2048]{1,0:T(8,128)} custom-call(s32[3]{0:T(128)} %pad_add_fusion.where_ref, f32[1024,256]{1,0:T(8,128)} %get-tuple-element.46.u_ref, f32[4,128,256]{2,1,0:T(8,128)} %copy-done.5, f32[4,128,256]{2,1,0:T(8,128)} %collective-permute-done.15.far_ref, f32[256,256]{1,0:T(8,128)} %copy-done.4, f32[16,16,256]{2,1,0:T(8,128)} %copy-done.6, ...), custom_call_target="tpu_custom_call" | custom-call | flops 12000000000 | bytes 1024 | tf_op jit(solution)/shard_map/pallas_call | solution.py:352
  (9 shorter events, 0.1 us)
Async XLA Ops:
  2.2 13.8 %collective-permute-start.6 = (f32[128,256]{1,0:T(8,128)S(1)}, f32[128,256]{1,0:T(8,128)S(1)}, u32[]{:S(2)}, u32[]{:S(2)}) collective-permute-start(f32[128,256]{1,0:T(8,128)S(1)} %get-tuple-element.50), channel_id=1, source_target_pairs={{0,7},{8,15},{16,23},{24,31},{32,39},{40,47},{48,55},{56,63},{64,7... | collective-permute-start | bytes 393224 | tf_op jit(solution)/shard_map/ppermute | solution.py:283
  10.7 6.5 %collective-permute-start.5 = (f32[128,256]{1,0:T(8,128)S(1)}, f32[128,256]{1,0:T(8,128)S(1)}, u32[]{:S(2)}, u32[]{:S(2)}) collective-permute-start(f32[128,256]{1,0:T(8,128)S(1)} %get-tuple-element.51), channel_id=1, source_target_pairs={{0,6},{8,14},{16,22},{24,30},{32,38},{40,46},{48,54},{56,62},{64,7... | collective-permute-start | bytes 393224 | tf_op jit(solution)/shard_map/ppermute | solution.py:283
  12.0 6.6 %collective-permute-start.4 = (f32[128,256]{1,0:T(8,128)S(1)}, f32[128,256]{1,0:T(8,128)S(1)}, u32[]{:S(2)}, u32[]{:S(2)}) collective-permute-start(f32[128,256]{1,0:T(8,128)S(1)} %get-tuple-element.52), channel_id=1, source_target_pairs={{0,5},{8,13},{16,21},{24,29},{32,37},{40,45},{48,53},{56,61},{64,6... | collective-permute-start | bytes 393224 | tf_op jit(solution)/shard_map/ppermute | solution.py:283
  13.3 5.3 %collective-permute-start.3 = (f32[128,256]{1,0:T(8,128)S(1)}, f32[128,256]{1,0:T(8,128)S(1)}, u32[]{:S(2)}, u32[]{:S(2)}) collective-permute-start(f32[128,256]{1,0:T(8,128)S(1)} %get-tuple-element.53), channel_id=1, source_target_pairs={{0,4},{8,12},{16,20},{24,28},{32,36},{40,44},{48,52},{56,60},{64,6... | collective-permute-start | bytes 393224 | tf_op jit(solution)/shard_map/ppermute | solution.py:283
  14.6 6.5 %collective-permute-start.2 = (f32[128,256]{1,0:T(8,128)S(1)}, f32[128,256]{1,0:T(8,128)S(1)}, u32[]{:S(2)}, u32[]{:S(2)}) collective-permute-start(f32[128,256]{1,0:T(8,128)S(1)} %get-tuple-element.54), channel_id=1, source_target_pairs={{0,3},{8,11},{16,19},{24,27},{32,35},{40,43},{48,51},{56,59},{64,6... | collective-permute-start | bytes 393224 | tf_op jit(solution)/shard_map/ppermute | solution.py:283
  16.0 7.9 %collective-permute-start.1 = (f32[128,256]{1,0:T(8,128)S(1)}, f32[128,256]{1,0:T(8,128)S(1)}, u32[]{:S(2)}, u32[]{:S(2)}) collective-permute-start(f32[128,256]{1,0:T(8,128)S(1)} %get-tuple-element.55), channel_id=1, source_target_pairs={{0,2},{8,10},{16,18},{24,26},{32,34},{40,42},{48,50},{56,58},{64,6... | collective-permute-start | bytes 393224 | tf_op jit(solution)/shard_map/ppermute | solution.py:283
  17.3 6.6 %collective-permute-start = (f32[128,256]{1,0:T(8,128)S(1)}, f32[128,256]{1,0:T(8,128)S(1)}, u32[]{:S(2)}, u32[]{:S(2)}) collective-permute-start(f32[128,256]{1,0:T(8,128)S(1)} %get-tuple-element.56), channel_id=1, source_target_pairs={{0,1},{8,9},{16,17},{24,25},{32,33},{40,41},{48,49},{56,57},{64,65... | collective-permute-start | bytes 393224 | tf_op jit(solution)/shard_map/ppermute | solution.py:283
  40.9 9.3 %copy-start.3 = (f32[8,128,256]{2,1,0:T(8,128)}, f32[8,128,256]{2,1,0:T(8,128)S(1)}, u32[]{:S(2)}) copy-start(f32[8,128,256]{2,1,0:T(8,128)S(1)} %all_to_all.30) | copy-start | bytes 3145732
  40.9 22.9 %collective-permute-start.7 = (f32[256,128]{1,0:T(8,128)S(1)}, f32[256,128]{1,0:T(8,128)S(1)}, u32[]{:S(2)}, u32[]{:S(2)}) collective-permute-start(f32[256,128]{1,0:T(8,128)S(1)} %get-tuple-element.31), channel_id=1, source_target_pairs={{0,0},{1,16},{2,32},{3,48},{4,64},{5,80},{6,96},{7,112},{8,8},{9,2... | collective-permute-start | bytes 393224 | tf_op jit(solution)/shard_map/ppermute | solution.py:288
  43.5 20.3 %all-to-all-start.1 = ((f32[8,64,128]{2,1,0:T(8,128)}), f32[8,64,128]{2,1,0:T(8,128)S(1)}, u32[]{:S(2)}, u32[]{:S(2)}) async-start(f32[8,64,128]{2,1,0:T(8,128)} %shard_map.43), calls=%async_computation.1 | async-start | bytes 524288 | tf_op jit(solution)/shard_map/all_to_all | solution.py:243
  63.8 7.7 %collective-permute-start.8 = (f32[8,384,128]{2,1,0:T(8,128)}, f32[8,384,128]{2,1,0:T(8,128)S(1)}, u32[]{:S(2)}, u32[]{:S(2)}) collective-permute-start(f32[8,384,128]{2,1,0:T(8,128)} %get-tuple-element.33), channel_id=1, source_target_pairs={{0,8},{8,0},{1,9},{9,1},{2,10},{10,2},{3,11},{11,3},{4,12},{12,4},... | collective-permute-start | bytes 4718600 | tf_op jit(solution)/shard_map/ppermute | solution.py:247
  68.3 2.9 %collective-permute-start.9 = (f32[64,128]{1,0:T(8,128)S(1)}, f32[64,128]{1,0:T(8,128)S(1)}, u32[]{:S(2)}, u32[]{:S(2)}) collective-permute-start(f32[64,128]{1,0:T(8,128)S(1)} %reduce_sum.9.gram_ref), channel_id=1, source_target_pairs={{0,8},{8,0},{1,9},{9,1},{2,10},{10,2},{3,11},{11,3},{4,12},{12,4},... | collective-permute-start | bytes 98312 | tf_op jit(solution)/shard_map/ppermute | solution.py:247
  71.5 1.4 copy-start.2
  101.3 1.5 copy-start.1
  102.8 39.6 %all-to-all-start.3 = ((f32[8,640,128]{2,1,0:T(8,128)}), f32[8,640,128]{2,1,0:T(8,128)S(1)}, u32[]{:S(2)}, u32[]{:S(2)}) async-start(f32[8,640,128]{2,1,0:T(8,128)} %copy-done.1), calls=%async_computation.3 | async-start | bytes 5242880 | tf_op jit(solution)/shard_map/all_to_all | solution.py:243
  106.5 9.7 %collective-permute-start.10 = (f32[128,256]{1,0:T(8,128)S(1)}, f32[128,256]{1,0:T(8,128)S(1)}, u32[]{:S(2)}, u32[]{:S(2)}) collective-permute-start(f32[128,256]{1,0:T(8,128)S(1)} %get-tuple-element.37), channel_id=1, source_target_pairs={{0,0},{16,1},{32,2},{48,3},{64,4},{80,5},{96,6},{112,7},{8,8},{24,... | collective-permute-start | bytes 393224 | tf_op jit(solution)/shard_map/ppermute | solution.py:314
  116.2 18.8 %collective-permute-start.13 = (f32[128,256]{1,0:T(8,128)S(1)}, f32[128,256]{1,0:T(8,128)S(1)}, u32[]{:S(2)}, u32[]{:S(2)}) collective-permute-start(f32[128,256]{1,0:T(8,128)S(1)} %collective-permute-done.10), channel_id=1, source_target_pairs={{6,0},{0,2},{2,4},{4,6},{7,1},{1,3},{3,5},{5,7},{14,8},{8,10},{10,... | collective-permute-start | bytes 393224 | tf_op jit(solution)/shard_map/ppermute | solution.py:251
  120.2 14.9 %collective-permute-start.12 = (f32[128,256]{1,0:T(8,128)S(1)}, f32[128,256]{1,0:T(8,128)S(1)}, u32[]{:S(2)}, u32[]{:S(2)}) collective-permute-start(f32[128,256]{1,0:T(8,128)S(1)} %collective-permute-done.10), channel_id=1, source_target_pairs={{4,0},{6,2},{0,4},{2,6},{5,1},{7,3},{1,5},{3,7},{12,8},{14,10},{8,... | collective-permute-start | bytes 393224 | tf_op jit(solution)/shard_map/ppermute | solution.py:251
  123.8 11.3 %collective-permute-start.11 = (f32[128,256]{1,0:T(8,128)S(1)}, f32[128,256]{1,0:T(8,128)S(1)}, u32[]{:S(2)}, u32[]{:S(2)}) collective-permute-start(f32[128,256]{1,0:T(8,128)S(1)} %collective-permute-done.10), channel_id=1, source_target_pairs={{2,0},{4,2},{6,4},{0,6},{3,1},{5,3},{7,5},{1,7},{10,8},{12,10},{14... | collective-permute-start | bytes 393224 | tf_op jit(solution)/shard_map/ppermute | solution.py:251
  134.3 0.7 copy-start.4
  135.1 21.0 %copy-start.5 = (f32[4,128,256]{2,1,0:T(8,128)}, f32[4,128,256]{2,1,0:T(8,128)S(1)}, u32[]{:S(2)}) copy-start(f32[4,128,256]{2,1,0:T(8,128)S(1)} %pad_maximum_fusion.near_ref) | copy-start | bytes 1572868
  142.3 3.4 %copy-start = (f32[8,640,128]{2,1,0:T(8,128)}, f32[8,640,128]{2,1,0:T(8,128)S(1)}, u32[]{:S(2)}) copy-start(f32[8,640,128]{2,1,0:T(8,128)S(1)} %all-to-all-done.3.panel_ref.product_ref.mine_ref.pmine_ref) | copy-start | bytes 7864324
  142.3 27.1 %collective-permute-start.14 = (f32[8,640,128]{2,1,0:T(8,128)S(1)}, f32[8,640,128]{2,1,0:T(8,128)}, u32[]{:S(2)}, u32[]{:S(2)}) collective-permute-start(f32[8,640,128]{2,1,0:T(8,128)S(1)} %all-to-all-done.3.panel_ref.product_ref.mine_ref.pmine_ref), channel_id=1, source_target_pairs={{0,8},{8,0},{1,9},{9,1},{2,10},{10,2},{3,11},{11,3},{4,12},{12,4},... | collective-permute-start | bytes 7864328 | tf_op jit(solution)/shard_map/ppermute | solution.py:247
  145.8 18.4 %all-to-all-start.4 = ((f32[16,16,256]{2,1,0:T(8,128)}), f32[16,16,256]{2,1,0:T(8,128)S(1)}, u32[]{:S(2)}, u32[]{:S(2)}) async-start(f32[16,16,256]{2,1,0:T(8,128)} %shard_map.48), calls=%async_computation.4 | async-start | bytes 524288 | tf_op jit(solution)/shard_map/all_to_all | solution.py:243
  156.1 22.0 %collective-permute-start.15 = (f32[4,128,256]{2,1,0:T(8,128)S(1)}, f32[4,128,256]{2,1,0:T(8,128)}, u32[]{:S(2)}, u32[]{:S(2)}) collective-permute-start(f32[4,128,256]{2,1,0:T(8,128)S(1)} %pad_maximum_fusion.near_ref), channel_id=1, source_target_pairs={{0,1},{1,0},{2,3},{3,2},{4,5},{5,4},{6,7},{7,6},{8,9},{9,8},{10,11... | collective-permute-start | bytes 1572872 | tf_op jit(solution)/shard_map/ppermute | solution.py:319
  164.9 13.1 %all-to-all-start.5 = ((f32[16,16,256]{2,1,0:T(8,128)}), f32[16,16,256]{2,1,0:T(8,128)S(1)}, u32[]{:S(2)}, u32[]{:S(2)}) async-start(f32[16,16,256]{2,1,0:T(8,128)} %shard_map.49), calls=%async_computation.5 | async-start | bytes 524288 | tf_op jit(solution)/shard_map/all_to_all | solution.py:243
  178.0 0.7 copy-start.6

commit v3 on v2

--- a/solution.py
+++ b/solution.py
@@ -112,50 +112,44 @@
     turned_ref[...] = mine.T
 
 
-def gram_kernel(panel_ref, out_ref):
-    gram = dot(panel_ref[...].T, panel_ref[...]).reshape(8, 32, B)
+def gram_kernel(panel_ref, out_ref, turned_ref):
+    turned = panel_ref[...].T
+    gram = dot(turned, panel_ref[...]).reshape(8, 32, B)
     out_ref[:, :32, :] = gram[:, :, :128]
     out_ref[:, 32:, :] = gram[:, :, 128:]
-
-
-def product_kernel(core_ref, panel_ref, matrix_ref, vectors_ref, keep_ref, give_ref, hi_ref, lo_ref):
+    turned_ref[:256], turned_ref[256:] = split(turned)
+
+
+def panel_product(turned_ref, right):
+    hi, lo = split(right)
+    both = lax.dot_general(turned_ref[...], hi, NN, preferred_element_type=F32)
+    return both[:256] + (both[256:] + lax.dot_general(turned_ref[:256], lo, NN, preferred_element_type=F32))
+
+
+def give_kernel(core_ref, turned_ref, matrix_ref, vectors_ref, give_ref, keep_ref):
     step = pl.program_id(0)
-    core = core_ref[0]
-
-    def put(own, both, place):
-        @pl.when(own == core)
-        def _():
-            keep_ref[:, place, :] = both[0]
-            give_ref[:, place, :] = both[1]
-
-        @pl.when(own != core)
-        def _():
-            keep_ref[:, place, :] = both[1]
-            give_ref[:, place, :] = both[0]
-
-    @pl.when(step == 0)
-    def _():
-        hi_ref[...], lo_ref[...] = split(panel_ref[...].T)
-
-    panel = hi_ref[...], lo_ref[...]
-    product = dot3(panel, split(matrix_ref[...]))
-    mixing = dot3(panel, split(vectors_ref[...])).reshape(2, 8, 16, 128)
-    m = (2 * step) % 8
-    put(0, mixing, pl.ds(pl.multiple_of(256 + 16 * step, 16), 16))
-
-    @pl.when(step // 4 == core)
-    def _():
-        keep_ref[m, :256, :] = product[:, :128]
-        keep_ref[m + 1, :256, :] = product[:, 128:]
-
-    @pl.when(step // 4 != core)
-    def _():
-        give_ref[m, :256, :] = product[:, :128]
-        give_ref[m + 1, :256, :] = product[:, 128:]
-
-
-def join_kernel(keep_ref, got_ref, gram_ref, other_ref, out_ref):
-    out_ref[:, :384, :] = keep_ref[...] + got_ref[...]
+    product = panel_product(turned_ref, matrix_ref[...])
+    give_ref[2 * step, :256, :] = product[:, :128]
+    give_ref[2 * step + 1, :256, :] = product[:, 128:]
+    mixing = panel_product(turned_ref, vectors_ref[...])
+    for b in range(2):
+        first, last = mixing[:128, 128 * b : 128 * b + 128], mixing[128:, 128 * b : 128 * b + 128]
+        first, last = first.reshape(8, 16, 128), last.reshape(8, 16, 128)
+        place = pl.multiple_of(32 * step + 16 * b, 16)
+        keep_ref[:, pl.ds(place, 16), :] = jnp.where(core_ref[0] == 0, first, last)
+        give_ref[:, pl.ds(256 + place, 16), :] = jnp.where(core_ref[0] == 0, last, first)
+
+
+def keep_kernel(core_ref, turned_ref, matrix_ref, keep_ref):
+    step = pl.program_id(0)
+    product = panel_product(turned_ref, matrix_ref[...])
+    keep_ref[2 * step] = product[:, :128]
+    keep_ref[2 * step + 1] = product[:, 128:]
+
+
+def join_kernel(keep_ref, mixing_ref, got_ref, gram_ref, other_ref, out_ref):
+    out_ref[:, :256, :] = keep_ref[...] + got_ref[:, :256, :]
+    out_ref[:, 256:384, :] = mixing_ref[...] + got_ref[:, 256:, :]
     gram = gram_ref[...] + other_ref[...]
     for m in range(8):
         out_ref[m, 384:, :] = gram
@@ -187,14 +181,15 @@
         out_ref[m] = total
 
 
-def rotate_kernel(core_ref, panel_ref, inverse_ref, mine_ref, other_ref, vectors_ref, out_ref, u_ref, left_ref):
-    @pl.when(pl.program_id(0) == 0)
-    def _():
-        u = 2.0 * dot(panel_ref[...], inverse_ref[...])
-        u_ref[...] = u
-        hi, lo = split(u)
-        left_ref[:, :256], left_ref[:, 256:512], left_ref[:, 512:] = hi, hi, lo
-
+def scale_kernel(panel_ref, product_ref, inverse_ref, left_ref, out_ref):
+    inverse = inverse_ref[...]
+    hi, lo = split(2.0 * dot(panel_ref[...], inverse))
+    left_ref[:, :256], left_ref[:, 256:512], left_ref[:, 512:] = hi, hi, lo
+    for k in range(4):
+        out_ref[k] = 2.0 * dot(product_ref[k], inverse)
+
+
+def rotate_kernel(core_ref, left_ref, mine_ref, other_ref, vectors_ref, out_ref):
     core = core_ref[0]
     mine, other = mine_ref[...], other_ref[...]
     both = jnp.where(core == 0, mine, other), jnp.where(core == 0, other, mine)
@@ -205,7 +200,7 @@
 
 
 def update_kernel(
-    where_ref, u_ref, near_ref, far_ref, inverse_ref, coupling_ref,
+    where_ref, first_ref, near_ref, far_ref, inverse_ref, coupling_ref,
     mine_ref, other_ref, pmine_ref, pother_ref, matrix_ref, out_ref, left_ref, product_ref,
 ):
     step = pl.program_id(0)
@@ -217,21 +212,18 @@
                 place = (lax.rem(where_ref[1] + k, 4) * 2 + zh) * 128
                 product_ref[pl.ds(pl.multiple_of(place, 128), 128), :] = piece_ref[k]
         small = dot(coupling_ref[...].reshape(B, B), inverse_ref[...])
-        u1 = u_ref[...]
-        u2 = 2.0 * dot(product_ref[...], inverse_ref[...]) - 2.0 * dot(u1, small)
-        for k, u in ((0, u1), (256, u2)):
-            hi, lo = split(u)
-            left_ref[:, k : k + 256], left_ref[:, k + 512 : k + 768], left_ref[:, k + 1024 : k + 1280] = hi, hi, lo
+        hi, lo = split(small)
+        right = jnp.concatenate([hi, lo, hi], axis=0)
+        u = product_ref[...] - 2.0 * lax.dot_general(first_ref[...], right, NN, preferred_element_type=F32)
+        hi, lo = split(u)
+        left_ref[:, :768] = first_ref[...]
+        left_ref[:, 768:1024], left_ref[:, 1024:1280], left_ref[:, 1280:] = hi, hi, lo
 
     mine = step // 4 == where_ref[0]
     product = jnp.where(mine, mine_ref[...], other_ref[...])
     panel = jnp.where(mine, pmine_ref[...], pother_ref[...])
-    hi, lo = split(
-        jnp.concatenate(
-            [jnp.concatenate([product[0], product[1]], axis=1), jnp.concatenate([panel[0], panel[1]], axis=1)], axis=0
-        )
-    )
-    right = jnp.concatenate([hi, lo, hi], axis=0)
+    halves = [split(jnp.concatenate([a[0], a[1]], axis=1)) for a in (product, panel)]
+    right = jnp.concatenate([x for hi, lo in halves for x in (hi, lo, hi)], axis=0)
     out_ref[...] = matrix_ref[...] - lax.dot_general(left_ref[...], right, NN, preferred_element_type=F32)
 
 
@@ -286,35 +278,56 @@
     )(col_index.astype(jnp.int32).reshape(1), *parts)
     panel_rows, turned = lax.optimization_barrier((exchange(sent, COL).reshape(1024, B), turned))
     turned = lax.ppermute(turned, ALL, there)
-    wide = whole(8, 384, 128)
-    gram = exchange(call(gram_kernel, f32(8, 64, 128), 1)(panel_rows), CHIPS)
-    keep, give = call(
-        product_kernel,
-        (f32(8, 384, 128), f32(8, 384, 128)),
-        12,
+    gram, stacked = call(gram_kernel, (f32(8, 64, 128), jax.ShapeDtypeStruct((512, 1024), BF16)), 2, 12)(panel_rows)
+    gram = exchange(gram, CHIPS)
+    give, mixing = call(
+        give_kernel,
+        (f32(8, 384, 128), f32(8, 128, 128)),
+        8,
         60,
-        grid=(8,),
-        in_specs=[
-            SMEM,
-            whole(1024, 256),
-            pl.BlockSpec((1024, 256), lambda t: (0, t)),
-            pl.BlockSpec((1024, 128), lambda t: (0, t)),
-        ],
-        out_specs=(wide, wide),
-        scratch_shapes=[pltpu.VMEM((256, 1024), BF16), pltpu.VMEM((256, 1024), BF16)],
-    )(core, panel_rows, matrix, vectors)
-    keep, give, turned, gram = lax.optimization_barrier((keep, give, turned, gram))
+        grid_spec=pltpu.PrefetchScalarGridSpec(
+            num_scalar_prefetch=1,
+            grid=(4,),
+            in_specs=[
+                pl.BlockSpec((512, 1024), lambda t, core: (0, 0)),
+                pl.BlockSpec((1024, 256), lambda t, core: (0, (1 - core[0]) * 4 + t)),
+                pl.BlockSpec((1024, 256), lambda t, core: (0, t)),
+            ],
+            out_specs=(
+                pl.BlockSpec((8, 384, 128), lambda t, core: (0, 0, 0)),
+                pl.BlockSpec((8, 128, 128), lambda t, core: (0, 0, 0)),
+            ),
+        ),
+    )(core, stacked, matrix, vectors)
+    give, mixing, turned, gram, stacked = lax.optimization_barrier((give, mixing, turned, gram, stacked))
     gram = jnp.sum(gram, axis=0)
-    came = exchange(
-        call(join_kernel, f32(8, 448, 128), 1, 12)(keep, swap_cores(give), gram, swap_cores(gram)), CHIPS
-    )
+    keep = call(
+        keep_kernel,
+        f32(8, 256, 128),
+        5,
+        60,
+        grid_spec=pltpu.PrefetchScalarGridSpec(
+            num_scalar_prefetch=1,
+            grid=(4,),
+            in_specs=[
+                pl.BlockSpec((512, 1024), lambda t, core: (0, 0)),
+                pl.BlockSpec((1024, 256), lambda t, core: (0, core[0] * 4 + t)),
+            ],
+            out_specs=pl.BlockSpec((8, 256, 128), lambda t, core: (0, 0, 0)),
+        ),
+    )(core, stacked, matrix)
+    got, other_gram, keep = lax.optimization_barrier((swap_cores(give), swap_cores(gram), keep))
+    came = exchange(call(join_kernel, f32(8, 448, 128), 1, 12)(keep, mixing, got, gram, other_gram), CHIPS)
 
     product, gram, sent = call(reduce_kernel, (f32(128, 256), f32(8, 64, 128), f32(8, 640, 128)), 2, 12)(came, turned)
     final = exchange(sent, CHIPS)
     near = gather_x(lax.ppermute(product, ALL, back))
     ai, t, schur = call(invert_first, (f32(128, 128),) * 3, 9)(gram)
     inverse = call(invert_second, f32(B, B), 9)(ai, t, schur)
-    final, near, inverse = lax.optimization_barrier((final, near, inverse))
+    first, near = call(
+        scale_kernel, (jax.ShapeDtypeStruct((1024, 768), BF16), f32(4, 128, 256)), 4, 20
+    )(panel_rows, near, inverse)
+    final, near, first, inverse = lax.optimization_barrier((final, near, first, inverse))
     other = swap_cores(final)
     far = lax.ppermute(near, "zh", [(0, 1), (1, 0)])
     coupling = call(
@@ -328,24 +341,20 @@
         ],
         out_specs=whole(16, 16, 256),
     )(final, final)
-    coupling = call(sum_kernel, f32(16, 16, 256), 1)(exchange(coupling, COUPLED))
     coupling = exchange(coupling, COUPLED)
-
     mixing = pl.BlockSpec((8, 32, 128), lambda t: (0, 8 + t, 0))
-    rotated, u = call(
+    rotated = call(
         rotate_kernel,
-        (f32(1024, 1024), f32(1024, 256)),
+        f32(1024, 1024),
         6,
         60,
         grid=(4,),
-        in_specs=[
-            SMEM, whole(1024, 256), whole(256, 256), mixing, mixing, pl.BlockSpec((1024, 256), lambda t: (0, t)),
-        ],
-        out_specs=(pl.BlockSpec((1024, 256), lambda t: (0, t)), whole(1024, 256)),
-        scratch_shapes=[pltpu.VMEM((1024, 768), BF16)],
-    )(core, panel_rows, inverse, final, other, vectors)
-
-    coupling, rotated, u = lax.optimization_barrier((coupling, rotated, u))
+        in_specs=[SMEM, whole(1024, 768), mixing, mixing, pl.BlockSpec((1024, 256), lambda t: (0, t))],
+        out_specs=pl.BlockSpec((1024, 256), lambda t: (0, t)),
+    )(core, first, final, other, vectors)
+    coupling, rotated = lax.optimization_barrier((coupling, rotated))
+    coupling = exchange(call(sum_kernel, f32(16, 16, 256), 1)(coupling), COUPLED)
+
     pair = pl.BlockSpec((2, 256, 128), lambda t: (t % 4, 0, 0))
     piece = whole(4, 128, 256)
     panel_pair = pl.BlockSpec((pl.Element(2), pl.Element(256), pl.Element(128)), lambda t: (2 * (t % 4), 384, 0))
@@ -356,12 +365,12 @@
         60,
         grid=(8,),
         in_specs=[
-            SMEM, whole(1024, 256), piece, piece, whole(256, 256), whole(16, 16, 256), pair, pair, panel_pair,
+            SMEM, whole(1024, 768), piece, piece, whole(256, 256), whole(16, 16, 256), pair, pair, panel_pair,
             panel_pair, pl.BlockSpec((1024, 256), lambda t: (0, t)),
         ],
         out_specs=pl.BlockSpec((1024, 256), lambda t: (0, t)),
         scratch_shapes=[pltpu.VMEM((1024, 1536), BF16), pltpu.VMEM((1024, 256), F32)],
-    )(where, u, near, far, inverse, coupling, final, other, final, other, matrix)
+    )(where, first, near, far, inverse, coupling, final, other, final, other, matrix)
     return (updated, rotated)
 
 

time: 197 us -> 195 us (0.990)
  waiting for transfers between devices: 21.9 us -> 18.6 us
    ppermute x3, waiting for transfers between devices: 3.18 us -> 0.01 us  [swap_cores(): return lax.ppermute(array, 'co', [(0, 1), (1, 0)])]
    all_to_all x4, waiting for transfers between devices: 13.4 us -> 11.4 us  [exchange(): return lax.all_to_all(blocks, axes, 0, 0, tiled=True)]
    unnamed x14 -> x22, local copies, waits for them, and re-layouts: 4.32 us -> 5.58 us
    pallas_call x4 -> x6, Pallas kernels: 23.9 us -> 24.4 us  [the longest x1 7.91 us: body(): call(give_kernel, (f32(8, 384, 128), f32(8, 128, 128)), 8, 60, grid_spec=...]
  transfers between devices with their start and end apart: 20 -> 20, of which waited for: 7 -> 5; matrix products, arithmetic and copies ran while one was open for 0% -> 0% of each run, Pallas kernels for 22% -> 23%
where the time goes in v3:
time: 195 us; the launch traced here: 194 us
  starting transfers between devices  61.5 us (32%)
  Pallas kernels  60.7 us (31%)
  blocking collectives  44.7 us (23%)
  waiting for transfers between devices  18.6 us (10%)
  local copies, waits for them, and re-layouts  5.66 us (3%)
  other arithmetic  2.15 us (1%)
    all_to_all x2, blocking collectives, exchange(): return lax.all_to_all(blocks, axes, 0, 0, tiled=True)  44.7 us
    all_to_all x4, starting transfers between devices, exchange(): return lax.all_to_all(blocks, axes, 0, 0, tiled=True)  25.1 us
    ppermute x7, starting transfers between devices, body(): parts.append(lax.ppermute(panel[k * 128:(k + 1) * 128], COL, [(0, k)]))  16.3 us
    pallas_call x1, Pallas kernels, body(): call(update_kernel, f32(1024, 2048), 12, 60, grid=(8,), in_specs=[SMEM, w...  16.2 us
    all_to_all x4, waiting for transfers between devices, exchange(): return lax.all_to_all(blocks, axes, 0, 0, tiled=True)  11.4 us
    pallas_call x1, Pallas kernels, body(): inverse = call(invert_second, f32(B, B), 9)(ai, t, schur)  9.09 us
    pallas_call x1, Pallas kernels, body(): ai, t, schur = call(invert_first, (f32(128, 128),) * 3, 9)(gram)  9.05 us
    ppermute x3, starting transfers between devices, gather_x(): lax.ppermute(block, 'x', [((x + k) % 4, x) for x in range(4)])  9.03 us
  transfers between devices with their start and end apart: 20, of which 5 were waited for; matrix products, arithmetic and copies ran while one was open for 0% of the time, Pallas kernels for 23%

profile of v3, /device:TPU:1, one launch (start us, length us, event | category | flops | bytes accessed | tf_op | source)
XLA Modules:
  0.0 194.2 jit_solution(5518722264130891785)
XLA Ops:
  0.7 1.4 slice_select_fusion
  2.1 0.1 fusion
  2.2 8.5 %collective-permute-start.6 = (f32[128,256]{1,0:T(8,128)S(1)}, f32[128,256]{1,0:T(8,128)S(1)}, u32[]{:S(2)}, u32[]{:S(2)}) collective-permute-start(f32[128,256]{1,0:T(8,128)S(1)} %get-tuple-element.62), channel_id=1, source_target_pairs={{0,7},{8,15},{16,23},{24,31},{32,39},{40,47},{48,55},{56,63},{64,7... | collective-permute-start | bytes 393224 | tf_op jit(solution)/shard_map/ppermute | solution.py:275
  10.7 1.3 collective-permute-start.5
  12.0 1.3 collective-permute-start.4
  13.3 1.3 collective-permute-start.3
  14.6 1.3 collective-permute-start.2
  15.9 0.0 collective-permute-done.6.refs_7_
  16.0 1.3 collective-permute-start.1
  17.3 0.0 collective-permute-done.5.refs_6_
  17.3 1.3 collective-permute-start
  18.6 0.0 collective-permute-done.4.refs_5_
  18.6 0.0 collective-permute-done.3.refs_4_
  18.6 2.5 %collective-permute-done.2.refs_3_ = f32[128,256]{1,0:T(8,128)S(1)} collective-permute-done((f32[128,256]{1,0:T(8,128)S(1)}, f32[128,256]{1,0:T(8,128)S(1)}, u32[]{:S(2)}, u32[]{:S(2)}) %collective-permute-start.2) | collective-permute-done | bytes 131104 | tf_op jit(solution)/shard_map/ppermute | solution.py:275
  21.1 2.8 %collective-permute-done.1.refs_2_ = f32[128,256]{1,0:T(8,128)S(1)} collective-permute-done((f32[128,256]{1,0:T(8,128)S(1)}, f32[128,256]{1,0:T(8,128)S(1)}, u32[]{:S(2)}, u32[]{:S(2)}) %collective-permute-start.1) | collective-permute-done | bytes 131104 | tf_op jit(solution)/shard_map/ppermute | solution.py:275
  23.9 0.0 collective-permute-done.refs_1_
  23.9 0.1 shard_map.41
  24.0 16.9 %all_to_all.30 = f32[8,128,256]{2,1,0:T(8,128)S(1)} all-to-all(f32[8,128,256]{2,1,0:T(8,128)S(1)} %get-tuple-element.32), channel_id=1, replica_groups=mesh['y'=4,'zl'=2,'co'=2,'x'=4,'zh'=2] {'x','zh'}, dimensions={0} | all-to-all | bytes 2097152 | tf_op jit(solution)/shard_map/all_to_all | solution.py:235
  40.9 0.7 collective-permute-start.7
  41.6 1.9 shard_map.42
  43.5 1.0 copy-done.8
  44.5 6.7 %all-to-all-start.1 = ((f32[8,64,128]{2,1,0:T(8,128)}), f32[8,64,128]{2,1,0:T(8,128)S(1)}, u32[]{:S(2)}, u32[]{:S(2)}) async-start(f32[8,64,128]{2,1,0:T(8,128)} %get-tuple-element.39), calls=%async_computation.1 | async-start | bytes 524288 | tf_op jit(solution)/shard_map/all_to_all | solution.py:235
  51.2 7.9 %shard_map.43 = (f32[8,384,128]{2,1,0:T(8,128)}, f32[8,128,128]{2,1,0:T(8,128)}) custom-call(s32[1]{0:T(128)} %bitcast.core_ref, bf16[512,1024]{1,0:T(8,128)(2,1)} %copy-done.8, f32[1024,2048]{1,0:T(8,128)} %matrix_ref.5, f32[1024,1024]{1,0:T(8,128)} %vectors_ref.3), custom_call_target="tpu_custom_call" | custom-call | flops 8000000000 | bytes 1024 | tf_op jit(solution)/shard_map/pallas_call | solution.py:283
  59.2 0.0 collective-permute-done.7.turned_ref
  59.2 0.0 all-to-all-done.1
  59.2 4.5 %collective-permute-start.8 = (f32[8,384,128]{2,1,0:T(8,128)}, f32[8,384,128]{2,1,0:T(8,128)S(1)}, u32[]{:S(2)}, u32[]{:S(2)}) collective-permute-start(f32[8,384,128]{2,1,0:T(8,128)} %get-tuple-element.40), channel_id=1, source_target_pairs={{0,8},{8,0},{1,9},{9,1},{2,10},{10,2},{3,11},{11,3},{4,12},{12,4},... | collective-permute-start | bytes 4718600 | tf_op jit(solution)/shard_map/ppermute | solution.py:239
  63.7 0.1 collective-permute-start.9
  63.8 5.6 %shard_map.44.keep_ref = f32[8,256,128]{2,1,0:T(8,128)} custom-call(s32[1]{0:T(128)} %bitcast.core_ref, bf16[512,1024]{1,0:T(8,128)(2,1)} %copy-done.8, f32[1024,2048]{1,0:T(8,128)} %matrix_ref.5), custom_call_target="tpu_custom_call" | custom-call | flops 5000000000 | bytes 1024 | tf_op jit(solution)/shard_map/pallas_call | solution.py:304
  69.4 0.0 collective-permute-done.9.other_ref
  69.4 0.0 collective-permute-done.8.got_ref
  69.4 1.2 copy-done.2
  70.7 0.2 shard_map.45
  70.8 27.8 %all_to_all.31.in_ref = f32[8,448,128]{2,1,0:T(8,128)S(1)} all-to-all(f32[8,448,128]{2,1,0:T(8,128)S(1)} %shard_map.45), channel_id=1, replica_groups=mesh['y'=4,'zl'=2,'co'=2,'x'=4,'zh'=2] {'y','zl'}, dimensions={0} | all-to-all | bytes 3670016 | tf_op jit(solution)/shard_map/all_to_all | solution.py:235
  98.6 0.3 shard_map.46
  98.9 0.0 copy-start.1
  98.9 1.5 copy-done.1
  100.4 3.8 %all-to-all-start.3 = ((f32[8,640,128]{2,1,0:T(8,128)}), f32[8,640,128]{2,1,0:T(8,128)S(1)}, u32[]{:S(2)}, u32[]{:S(2)}) async-start(f32[8,640,128]{2,1,0:T(8,128)} %copy-done.1), calls=%async_computation.3 | async-start | bytes 5242880 | tf_op jit(solution)/shard_map/all_to_all | solution.py:235
  104.2 0.7 collective-permute-start.10
  104.8 9.0 %shard_map.47 = (f32[128,128]{1,0:T(8,128)S(1)}, f32[128,128]{1,0:T(8,128)S(1)}, f32[128,128]{1,0:T(8,128)S(1)}) custom-call(f32[8,64,128]{2,1,0:T(8,128)S(1)} %get-tuple-element.50.gram_ref), custom_call_target="tpu_custom_call" | custom-call | flops 8999999488 | bytes 1024 | tf_op jit(solution)/shard_map/pallas_call | solution.py:325
  113.9 0.0 collective-permute-done.10
  113.9 4.0 %collective-permute-start.13 = (f32[128,256]{1,0:T(8,128)S(1)}, f32[128,256]{1,0:T(8,128)S(1)}, u32[]{:S(2)}, u32[]{:S(2)}) collective-permute-start(f32[128,256]{1,0:T(8,128)S(1)} %collective-permute-done.10), channel_id=1, source_target_pairs={{6,0},{0,2},{2,4},{4,6},{7,1},{1,3},{3,5},{5,7},{14,8},{8,10},{10,... | collective-permute-start | bytes 393224 | tf_op jit(solution)/shard_map/ppermute | solution.py:243
  117.9 3.6 %collective-permute-start.12 = (f32[128,256]{1,0:T(8,128)S(1)}, f32[128,256]{1,0:T(8,128)S(1)}, u32[]{:S(2)}, u32[]{:S(2)}) collective-permute-start(f32[128,256]{1,0:T(8,128)S(1)} %collective-permute-done.10), channel_id=1, source_target_pairs={{4,0},{6,2},{0,4},{2,6},{5,1},{7,3},{1,5},{3,7},{12,8},{14,10},{8,... | collective-permute-start | bytes 393224 | tf_op jit(solution)/shard_map/ppermute | solution.py:243
  121.5 1.5 collective-permute-start.11
  122.9 9.1 %shard_map.48.inverse_ref = f32[256,256]{1,0:T(8,128)S(1)} custom-call(f32[128,128]{1,0:T(8,128)S(1)} %get-tuple-element.51.ai_ref, f32[128,128]{1,0:T(8,128)S(1)} %get-tuple-element.52.t_ref, f32[128,128]{1,0:T(8,128)S(1)} %get-tuple-element.53.schur_ref), custom_call_target="tpu_custom_call" | custom-call | flops 8999999488 | bytes 1024 | tf_op jit(solution)/shard_map/pallas_call | solution.py:326
  132.0 0.0 collective-permute-done.13
  132.1 0.0 collective-permute-done.12
  132.1 0.0 collective-permute-done.11
  132.1 1.4 shard_map.49
  133.6 1.2 copy-done.7
  134.8 5.3 %all-to-all-done.3.panel_ref.product_ref.mine_ref.pmine_ref = f32[8,640,128]{2,1,0:T(8,128)S(1)} async-done(((f32[8,640,128]{2,1,0:T(8,128)}), f32[8,640,128]{2,1,0:T(8,128)S(1)}, u32[]{:S(2)}, u32[]{:S(2)}) %all-to-all-start.3) | async-done | bytes 2621472 | tf_op jit(solution)/shard_map/all_to_all | solution.py:235
  140.1 2.1 %collective-permute-start.15 = (f32[8,640,128]{2,1,0:T(8,128)S(1)}, f32[8,640,128]{2,1,0:T(8,128)}, u32[]{:S(2)}, u32[]{:S(2)}) collective-permute-start(f32[8,640,128]{2,1,0:T(8,128)S(1)} %all-to-all-done.3.panel_ref.product_ref.mine_ref.pmine_ref), channel_id=1, source_target_pairs={{0,8},{8,0},{1,9},{9,1},{2,10},{10,2},{3,11},{11,3},{4,12},{12,4},... | collective-permute-start | bytes 7864328 | tf_op jit(solution)/shard_map/ppermute | solution.py:239
  142.2 1.3 shard_map.50
  143.5 9.7 %all-to-all-start.4 = ((f32[16,16,256]{2,1,0:T(8,128)}), f32[16,16,256]{2,1,0:T(8,128)S(1)}, u32[]{:S(2)}, u32[]{:S(2)}) async-start(f32[16,16,256]{2,1,0:T(8,128)} %shard_map.50), calls=%async_computation.4 | async-start | bytes 524288 | tf_op jit(solution)/shard_map/all_to_all | solution.py:235
  153.2 3.0 %collective-permute-start.14 = (f32[4,128,256]{2,1,0:T(8,128)S(1)}, f32[4,128,256]{2,1,0:T(8,128)}, u32[]{:S(2)}, u32[]{:S(2)}) collective-permute-start(f32[4,128,256]{2,1,0:T(8,128)S(1)} %get-tuple-element.57.near_ref), channel_id=1, source_target_pairs={{0,1},{1,0},{2,3},{3,2},{4,5},{5,4},{6,7},{7,6},{8,9},{9,8},{10,11... | collective-permute-start | bytes 1572872 | tf_op jit(solution)/shard_map/ppermute | solution.py:332
  156.2 0.0 collective-permute-done.15.other_ref.pother_ref
  156.2 6.8 %shard_map.51 = f32[1024,1024]{1,0:T(8,128)} custom-call(s32[1]{0:T(128)} %bitcast.core_ref, bf16[1024,768]{1,0:T(8,128)(2,1)} %copy-done.7, f32[8,640,128]{2,1,0:T(8,128)} %copy-done, f32[8,640,128]{2,1,0:T(8,128)} %collective-permute-done.15.other_ref.pother_ref, f32[1024,1024]{1,0:T(8,128)} %vectors_ref.3), custom_call_target="tpu_custom_call" | custom-call | flops 6000000000 | bytes 1024 | tf_op jit(solution)/shard_map/pallas_call | solution.py:346
  163.0 0.0 all-to-all-done.4.in_ref
  163.0 0.7 shard_map.52
  163.7 4.9 %all-to-all-start.5 = ((f32[16,16,256]{2,1,0:T(8,128)}), f32[16,16,256]{2,1,0:T(8,128)S(1)}, u32[]{:S(2)}, u32[]{:S(2)}) async-start(f32[16,16,256]{2,1,0:T(8,128)} %shard_map.52), calls=%async_computation.5 | async-start | bytes 524288 | tf_op jit(solution)/shard_map/all_to_all | solution.py:235
  168.6 0.7 pad_add_fusion.where_ref
  169.3 1.9 collective-permute-done.14.far_ref
  171.2 6.1 %all-to-all-done.5.coupling_ref = f32[16,16,256]{2,1,0:T(8,128)S(1)} async-done(((f32[16,16,256]{2,1,0:T(8,128)}), f32[16,16,256]{2,1,0:T(8,128)S(1)}, u32[]{:S(2)}, u32[]{:S(2)}) %all-to-all-start.5) | async-done | bytes 262176 | tf_op jit(solution)/shard_map/all_to_all | solution.py:235
  177.3 0.7 copy-done.10
  178.0 16.2 %shard_map.53 = f32[1024,2048]{1,0:T(8,128)} custom-call(s32[3]{0:T(128)} %pad_add_fusion.where_ref, bf16[1024,768]{1,0:T(8,128)(2,1)} %copy-done.7, f32[4,128,256]{2,1,0:T(8,128)} %copy-done.6, f32[4,128,256]{2,1,0:T(8,128)} %collective-permute-done.14.far_ref, f32[256,256]{1,0:T(8,128)} %copy-done.9, f32[16,16,256]{2,1,0:T(8,128)} %copy-done.10, ...), custom_call_target="tpu_custom_call" | custom-call | flops 12000000000 | bytes 1024 | tf_op jit(solution)/shard_map/pallas_call | solution.py:361
  (19 shorter events, 0.1 us)
Async XLA Ops:
  2.2 13.8 %collective-permute-start.6 = (f32[128,256]{1,0:T(8,128)S(1)}, f32[128,256]{1,0:T(8,128)S(1)}, u32[]{:S(2)}, u32[]{:S(2)}) collective-permute-start(f32[128,256]{1,0:T(8,128)S(1)} %get-tuple-element.62), channel_id=1, source_target_pairs={{0,7},{8,15},{16,23},{24,31},{32,39},{40,47},{48,55},{56,63},{64,7... | collective-permute-start | bytes 393224 | tf_op jit(solution)/shard_map/ppermute | solution.py:275
  10.7 6.5 %collective-permute-start.5 = (f32[128,256]{1,0:T(8,128)S(1)}, f32[128,256]{1,0:T(8,128)S(1)}, u32[]{:S(2)}, u32[]{:S(2)}) collective-permute-start(f32[128,256]{1,0:T(8,128)S(1)} %get-tuple-element.63), channel_id=1, source_target_pairs={{0,6},{8,14},{16,22},{24,30},{32,38},{40,46},{48,54},{56,62},{64,7... | collective-permute-start | bytes 393224 | tf_op jit(solution)/shard_map/ppermute | solution.py:275
  12.0 6.6 %collective-permute-start.4 = (f32[128,256]{1,0:T(8,128)S(1)}, f32[128,256]{1,0:T(8,128)S(1)}, u32[]{:S(2)}, u32[]{:S(2)}) collective-permute-start(f32[128,256]{1,0:T(8,128)S(1)} %get-tuple-element.64), channel_id=1, source_target_pairs={{0,5},{8,13},{16,21},{24,29},{32,37},{40,45},{48,53},{56,61},{64,6... | collective-permute-start | bytes 393224 | tf_op jit(solution)/shard_map/ppermute | solution.py:275
  13.3 5.3 %collective-permute-start.3 = (f32[128,256]{1,0:T(8,128)S(1)}, f32[128,256]{1,0:T(8,128)S(1)}, u32[]{:S(2)}, u32[]{:S(2)}) collective-permute-start(f32[128,256]{1,0:T(8,128)S(1)} %get-tuple-element.65), channel_id=1, source_target_pairs={{0,4},{8,12},{16,20},{24,28},{32,36},{40,44},{48,52},{56,60},{64,6... | collective-permute-start | bytes 393224 | tf_op jit(solution)/shard_map/ppermute | solution.py:275
  14.6 6.5 %collective-permute-start.2 = (f32[128,256]{1,0:T(8,128)S(1)}, f32[128,256]{1,0:T(8,128)S(1)}, u32[]{:S(2)}, u32[]{:S(2)}) collective-permute-start(f32[128,256]{1,0:T(8,128)S(1)} %get-tuple-element.66), channel_id=1, source_target_pairs={{0,3},{8,11},{16,19},{24,27},{32,35},{40,43},{48,51},{56,59},{64,6... | collective-permute-start | bytes 393224 | tf_op jit(solution)/shard_map/ppermute | solution.py:275
  16.0 7.9 %collective-permute-start.1 = (f32[128,256]{1,0:T(8,128)S(1)}, f32[128,256]{1,0:T(8,128)S(1)}, u32[]{:S(2)}, u32[]{:S(2)}) collective-permute-start(f32[128,256]{1,0:T(8,128)S(1)} %get-tuple-element.67), channel_id=1, source_target_pairs={{0,2},{8,10},{16,18},{24,26},{32,34},{40,42},{48,50},{56,58},{64,6... | collective-permute-start | bytes 393224 | tf_op jit(solution)/shard_map/ppermute | solution.py:275
  17.3 6.6 %collective-permute-start = (f32[128,256]{1,0:T(8,128)S(1)}, f32[128,256]{1,0:T(8,128)S(1)}, u32[]{:S(2)}, u32[]{:S(2)}) collective-permute-start(f32[128,256]{1,0:T(8,128)S(1)} %get-tuple-element.68), channel_id=1, source_target_pairs={{0,1},{8,9},{16,17},{24,25},{32,33},{40,41},{48,49},{56,57},{64,65... | collective-permute-start | bytes 393224 | tf_op jit(solution)/shard_map/ppermute | solution.py:275
  40.9 2.6 %copy-start.3 = (f32[8,128,256]{2,1,0:T(8,128)}, f32[8,128,256]{2,1,0:T(8,128)S(1)}, u32[]{:S(2)}) copy-start(f32[8,128,256]{2,1,0:T(8,128)S(1)} %all_to_all.30) | copy-start | bytes 3145732
  40.9 18.2 %collective-permute-start.7 = (f32[256,128]{1,0:T(8,128)S(1)}, f32[256,128]{1,0:T(8,128)S(1)}, u32[]{:S(2)}, u32[]{:S(2)}) collective-permute-start(f32[256,128]{1,0:T(8,128)S(1)} %get-tuple-element.38), channel_id=1, source_target_pairs={{0,0},{1,16},{2,32},{3,48},{4,64},{5,80},{6,96},{7,112},{8,8},{9,2... | collective-permute-start | bytes 393224 | tf_op jit(solution)/shard_map/ppermute | solution.py:280
  43.5 1.0 copy-start.8
  44.5 14.7 %all-to-all-start.1 = ((f32[8,64,128]{2,1,0:T(8,128)}), f32[8,64,128]{2,1,0:T(8,128)S(1)}, u32[]{:S(2)}, u32[]{:S(2)}) async-start(f32[8,64,128]{2,1,0:T(8,128)} %get-tuple-element.39), calls=%async_computation.1 | async-start | bytes 524288 | tf_op jit(solution)/shard_map/all_to_all | solution.py:235
  59.2 10.3 %collective-permute-start.8 = (f32[8,384,128]{2,1,0:T(8,128)}, f32[8,384,128]{2,1,0:T(8,128)S(1)}, u32[]{:S(2)}, u32[]{:S(2)}) collective-permute-start(f32[8,384,128]{2,1,0:T(8,128)} %get-tuple-element.40), channel_id=1, source_target_pairs={{0,8},{8,0},{1,9},{9,1},{2,10},{10,2},{3,11},{11,3},{4,12},{12,4},... | collective-permute-start | bytes 4718600 | tf_op jit(solution)/shard_map/ppermute | solution.py:239
  63.7 5.8 %copy-start.5 = (f32[8,128,128]{2,1,0:T(8,128)S(1)}, f32[8,128,128]{2,1,0:T(8,128)}, u32[]{:S(2)}) copy-start(f32[8,128,128]{2,1,0:T(8,128)} %get-tuple-element.44.mixing_ref) | copy-start | bytes 1572868
  63.7 5.7 %collective-permute-start.9 = (f32[64,128]{1,0:T(8,128)S(1)}, f32[64,128]{1,0:T(8,128)S(1)}, u32[]{:S(2)}, u32[]{:S(2)}) collective-permute-start(f32[64,128]{1,0:T(8,128)S(1)} %reduce_sum.9.gram_ref), channel_id=1, source_target_pairs={{0,8},{8,0},{1,9},{9,1},{2,10},{10,2},{3,11},{11,3},{4,12},{12,4},... | collective-permute-start | bytes 98312 | tf_op jit(solution)/shard_map/ppermute | solution.py:239
  69.4 1.2 copy-start.2
  98.9 1.5 copy-start.1
  100.4 39.6 %all-to-all-start.3 = ((f32[8,640,128]{2,1,0:T(8,128)}), f32[8,640,128]{2,1,0:T(8,128)S(1)}, u32[]{:S(2)}, u32[]{:S(2)}) async-start(f32[8,640,128]{2,1,0:T(8,128)} %copy-done.1), calls=%async_computation.3 | async-start | bytes 5242880 | tf_op jit(solution)/shard_map/all_to_all | solution.py:235
  104.2 9.7 %collective-permute-start.10 = (f32[128,256]{1,0:T(8,128)S(1)}, f32[128,256]{1,0:T(8,128)S(1)}, u32[]{:S(2)}, u32[]{:S(2)}) collective-permute-start(f32[128,256]{1,0:T(8,128)S(1)} %get-tuple-element.49), channel_id=1, source_target_pairs={{0,0},{16,1},{32,2},{48,3},{64,4},{80,5},{96,6},{112,7},{8,8},{24,... | collective-permute-start | bytes 393224 | tf_op jit(solution)/shard_map/ppermute | solution.py:324
  113.9 18.1 %collective-permute-start.13 = (f32[128,256]{1,0:T(8,128)S(1)}, f32[128,256]{1,0:T(8,128)S(1)}, u32[]{:S(2)}, u32[]{:S(2)}) collective-permute-start(f32[128,256]{1,0:T(8,128)S(1)} %collective-permute-done.10), channel_id=1, source_target_pairs={{6,0},{0,2},{2,4},{4,6},{7,1},{1,3},{3,5},{5,7},{14,8},{8,10},{10,... | collective-permute-start | bytes 393224 | tf_op jit(solution)/shard_map/ppermute | solution.py:243
  117.9 14.2 %collective-permute-start.12 = (f32[128,256]{1,0:T(8,128)S(1)}, f32[128,256]{1,0:T(8,128)S(1)}, u32[]{:S(2)}, u32[]{:S(2)}) collective-permute-start(f32[128,256]{1,0:T(8,128)S(1)} %collective-permute-done.10), channel_id=1, source_target_pairs={{4,0},{6,2},{0,4},{2,6},{5,1},{7,3},{1,5},{3,7},{12,8},{14,10},{8,... | collective-permute-start | bytes 393224 | tf_op jit(solution)/shard_map/ppermute | solution.py:243
  121.5 10.6 %collective-permute-start.11 = (f32[128,256]{1,0:T(8,128)S(1)}, f32[128,256]{1,0:T(8,128)S(1)}, u32[]{:S(2)}, u32[]{:S(2)}) collective-permute-start(f32[128,256]{1,0:T(8,128)S(1)} %collective-permute-done.10), channel_id=1, source_target_pairs={{2,0},{4,2},{6,4},{0,6},{3,1},{5,3},{7,5},{1,7},{10,8},{12,10},{14... | collective-permute-start | bytes 393224 | tf_op jit(solution)/shard_map/ppermute | solution.py:243
  122.9 9.2 %copy-start.4 = (f32[8,128,256]{2,1,0:T(8,128)S(1)}, f32[8,128,256]{2,1,0:T(8,128)}, u32[]{:S(2)}) copy-start(f32[8,128,256]{2,1,0:T(8,128)} %copy-done.3) | copy-start | bytes 3145732
  132.0 1.5 copy-start.9
  133.6 1.2 copy-start.7
  134.8 18.5 %copy-start.6 = (f32[4,128,256]{2,1,0:T(8,128)}, f32[4,128,256]{2,1,0:T(8,128)S(1)}, u32[]{:S(2)}) copy-start(f32[4,128,256]{2,1,0:T(8,128)S(1)} %get-tuple-element.57.near_ref) | copy-start | bytes 1572868
  140.1 3.5 %copy-start = (f32[8,640,128]{2,1,0:T(8,128)}, f32[8,640,128]{2,1,0:T(8,128)S(1)}, u32[]{:S(2)}) copy-start(f32[8,640,128]{2,1,0:T(8,128)S(1)} %all-to-all-done.3.panel_ref.product_ref.mine_ref.pmine_ref) | copy-start | bytes 7864324
  140.1 16.1 %collective-permute-start.15 = (f32[8,640,128]{2,1,0:T(8,128)S(1)}, f32[8,640,128]{2,1,0:T(8,128)}, u32[]{:S(2)}, u32[]{:S(2)}) collective-permute-start(f32[8,640,128]{2,1,0:T(8,128)S(1)} %all-to-all-done.3.panel_ref.product_ref.mine_ref.pmine_ref), channel_id=1, source_target_pairs={{0,8},{8,0},{1,9},{9,1},{2,10},{10,2},{3,11},{11,3},{4,12},{12,4},... | collective-permute-start | bytes 7864328 | tf_op jit(solution)/shard_map/ppermute | solution.py:239
  143.5 19.5 %all-to-all-start.4 = ((f32[16,16,256]{2,1,0:T(8,128)}), f32[16,16,256]{2,1,0:T(8,128)S(1)}, u32[]{:S(2)}, u32[]{:S(2)}) async-start(f32[16,16,256]{2,1,0:T(8,128)} %shard_map.50), calls=%async_computation.4 | async-start | bytes 524288 | tf_op jit(solution)/shard_map/all_to_all | solution.py:235
  153.2 18.0 %collective-permute-start.14 = (f32[4,128,256]{2,1,0:T(8,128)S(1)}, f32[4,128,256]{2,1,0:T(8,128)}, u32[]{:S(2)}, u32[]{:S(2)}) collective-permute-start(f32[4,128,256]{2,1,0:T(8,128)S(1)} %get-tuple-element.57.near_ref), channel_id=1, source_target_pairs={{0,1},{1,0},{2,3},{3,2},{4,5},{5,4},{6,7},{7,6},{8,9},{9,8},{10,11... | collective-permute-start | bytes 1572872 | tf_op jit(solution)/shard_map/ppermute | solution.py:332
  163.7 13.6 %all-to-all-start.5 = ((f32[16,16,256]{2,1,0:T(8,128)}), f32[16,16,256]{2,1,0:T(8,128)S(1)}, u32[]{:S(2)}, u32[]{:S(2)}) async-start(f32[16,16,256]{2,1,0:T(8,128)} %shard_map.52), calls=%async_computation.5 | async-start | bytes 524288 | tf_op jit(solution)/shard_map/all_to_all | solution.py:235
  177.3 0.7 copy-start.10

commit v4 on v3

--- a/solution.py
+++ b/solution.py
@@ -112,11 +112,13 @@
     turned_ref[...] = mine.T
 
 
-def gram_kernel(panel_ref, out_ref, turned_ref):
+def gram_kernel(panel_ref, block_ref, out_ref, turned_ref):
     turned = panel_ref[...].T
     gram = dot(turned, panel_ref[...]).reshape(8, 32, B)
-    out_ref[:, :32, :] = gram[:, :, :128]
-    out_ref[:, 32:, :] = gram[:, :, 128:]
+    for m in range(8):
+        out_ref[m, :256, :] = block_ref[...]
+    out_ref[:, 256:288, :] = gram[:, :, :128]
+    out_ref[:, 288:, :] = gram[:, :, 128:]
     turned_ref[:256], turned_ref[256:] = split(turned)
 
 
@@ -126,44 +128,36 @@
     return both[:256] + (both[256:] + lax.dot_general(turned_ref[:256], lo, NN, preferred_element_type=F32))
 
 
-def give_kernel(core_ref, turned_ref, matrix_ref, vectors_ref, give_ref, keep_ref):
+def product_kernel(core_ref, turned_ref, theirs_ref, mine_ref, vectors_ref, give_ref, keep_ref):
     step = pl.program_id(0)
-    product = panel_product(turned_ref, matrix_ref[...])
-    give_ref[2 * step, :256, :] = product[:, :128]
-    give_ref[2 * step + 1, :256, :] = product[:, 128:]
+    for matrix_ref, out_ref in ((theirs_ref, give_ref), (mine_ref, keep_ref)):
+        product = panel_product(turned_ref, matrix_ref[...])
+        out_ref[2 * step, :256, :] = product[:, :128]
+        out_ref[2 * step + 1, :256, :] = product[:, 128:]
     mixing = panel_product(turned_ref, vectors_ref[...])
     for b in range(2):
         first, last = mixing[:128, 128 * b : 128 * b + 128], mixing[128:, 128 * b : 128 * b + 128]
         first, last = first.reshape(8, 16, 128), last.reshape(8, 16, 128)
         place = pl.multiple_of(32 * step + 16 * b, 16)
-        keep_ref[:, pl.ds(place, 16), :] = jnp.where(core_ref[0] == 0, first, last)
+        keep_ref[:, pl.ds(256 + place, 16), :] = jnp.where(core_ref[0] == 0, first, last)
         give_ref[:, pl.ds(256 + place, 16), :] = jnp.where(core_ref[0] == 0, last, first)
 
 
-def keep_kernel(core_ref, turned_ref, matrix_ref, keep_ref):
-    step = pl.program_id(0)
-    product = panel_product(turned_ref, matrix_ref[...])
-    keep_ref[2 * step] = product[:, :128]
-    keep_ref[2 * step + 1] = product[:, 128:]
-
-
-def join_kernel(keep_ref, mixing_ref, got_ref, gram_ref, other_ref, out_ref):
-    out_ref[:, :256, :] = keep_ref[...] + got_ref[:, :256, :]
-    out_ref[:, 256:384, :] = mixing_ref[...] + got_ref[:, 256:, :]
+def join_kernel(keep_ref, got_ref, gram_ref, other_ref, out_ref):
+    out_ref[:, :384, :] = keep_ref[...] + got_ref[...]
     gram = gram_ref[...] + other_ref[...]
     for m in range(8):
         out_ref[m, 384:, :] = gram
 
 
-def reduce_kernel(in_ref, turned_ref, product_ref, gram_ref, out_ref):
+def reduce_kernel(in_ref, product_ref, gram_ref, out_ref):
     own = in_ref[0, :384, :]
     for m in range(1, 8):
         own = own + in_ref[m, :384, :]
     product_ref[...] = own[:256].T
     gram_ref[...] = in_ref[:, 384:, :]
     for m in range(8):
-        out_ref[m, :384, :] = own
-        out_ref[m, 384:, :] = turned_ref[...]
+        out_ref[m] = own
 
 
 def coupling_kernel(panel_ref, product_ref, out_ref):
@@ -259,6 +253,10 @@
     return pl.BlockSpec(shape, lambda t: (0,) * len(shape))
 
 
+def fixed(*shape):
+    return pl.BlockSpec(shape, lambda t, w: (0,) * len(shape))
+
+
 def body(matrix, vectors):
     rows_here = matrix.shape[0]
     row_index = lax.axis_index(ROW)
@@ -269,21 +267,24 @@
     back = [(b, a) for a, b in there]
 
     global_rows = row_index * rows_here + jnp.arange(rows_here, dtype=jnp.int32)
-    panel = jnp.where(global_rows[:, None] >= B, matrix[:, :B], F32(0.0))
-    parts = [panel[:128]]
+    columns = jnp.where(global_rows[:, None] >= B, matrix[:, :B], F32(0.0))
+    parts = [columns[:128]]
     for k in range(1, 8):
-        parts.append(lax.ppermute(panel[k * 128 : (k + 1) * 128], COL, [(0, k)]))
+        parts.append(lax.ppermute(columns[k * 128 : (k + 1) * 128], COL, [(0, k)]))
     sent, turned = call(
         choose_kernel, (f32(8, 128, 256), f32(256, 128)), 1, in_specs=[SMEM] + [VMEM] * 8
     )(col_index.astype(jnp.int32).reshape(1), *parts)
-    panel_rows, turned = lax.optimization_barrier((exchange(sent, COL).reshape(1024, B), turned))
     turned = lax.ppermute(turned, ALL, there)
-    gram, stacked = call(gram_kernel, (f32(8, 64, 128), jax.ShapeDtypeStruct((512, 1024), BF16)), 2, 12)(panel_rows)
-    gram = exchange(gram, CHIPS)
-    give, mixing = call(
-        give_kernel,
-        (f32(8, 384, 128), f32(8, 128, 128)),
-        8,
+    panel_rows = exchange(sent, COL).reshape(1024, B)
+    sent, stacked = call(gram_kernel, (f32(8, 320, 128), jax.ShapeDtypeStruct((512, 1024), BF16)), 2, 12)(
+        panel_rows, turned
+    )
+    panel = exchange(sent, CHIPS)
+    half = pl.BlockSpec((8, 384, 128), lambda t, core: (0, 0, 0))
+    give, keep = call(
+        product_kernel,
+        (f32(8, 384, 128), f32(8, 384, 128)),
+        12,
         60,
         grid_spec=pltpu.PrefetchScalarGridSpec(
             num_scalar_prefetch=1,
@@ -291,35 +292,20 @@
             in_specs=[
                 pl.BlockSpec((512, 1024), lambda t, core: (0, 0)),
                 pl.BlockSpec((1024, 256), lambda t, core: (0, (1 - core[0]) * 4 + t)),
+                pl.BlockSpec((1024, 256), lambda t, core: (0, core[0] * 4 + t)),
                 pl.BlockSpec((1024, 256), lambda t, core: (0, t)),
             ],
-            out_specs=(
-                pl.BlockSpec((8, 384, 128), lambda t, core: (0, 0, 0)),
-                pl.BlockSpec((8, 128, 128), lambda t, core: (0, 0, 0)),
-            ),
+            out_specs=(half, half),
         ),
-    )(core, stacked, matrix, vectors)
-    give, mixing, turned, gram, stacked = lax.optimization_barrier((give, mixing, turned, gram, stacked))
-    gram = jnp.sum(gram, axis=0)
-    keep = call(
-        keep_kernel,
-        f32(8, 256, 128),
-        5,
-        60,
-        grid_spec=pltpu.PrefetchScalarGridSpec(
-            num_scalar_prefetch=1,
-            grid=(4,),
-            in_specs=[
-                pl.BlockSpec((512, 1024), lambda t, core: (0, 0)),
-                pl.BlockSpec((1024, 256), lambda t, core: (0, core[0] * 4 + t)),
-            ],
-            out_specs=pl.BlockSpec((8, 256, 128), lambda t, core: (0, 0, 0)),
-        ),
-    )(core, stacked, matrix)
-    got, other_gram, keep = lax.optimization_barrier((swap_cores(give), swap_cores(gram), keep))
-    came = exchange(call(join_kernel, f32(8, 448, 128), 1, 12)(keep, mixing, got, gram, other_gram), CHIPS)
-
-    product, gram, sent = call(reduce_kernel, (f32(128, 256), f32(8, 64, 128), f32(8, 640, 128)), 2, 12)(came, turned)
+    )(core, stacked, matrix, matrix, vectors)
+    give, keep, panel = lax.optimization_barrier((give, keep, panel))
+    got = swap_cores(give)
+    gram = jnp.sum(panel[:, 256:], axis=0)
+    other_gram = swap_cores(gram)
+    other_panel = swap_cores(panel)
+    came = exchange(call(join_kernel, f32(8, 448, 128), 1, 12)(keep, got, gram, other_gram), CHIPS)
+
+    product, gram, sent = call(reduce_kernel, (f32(128, 256), f32(8, 64, 128), f32(8, 384, 128)), 2, 12)(came)
     final = exchange(sent, CHIPS)
     near = gather_x(lax.ppermute(product, ALL, back))
     ai, t, schur = call(invert_first, (f32(128, 128),) * 3, 9)(gram)
@@ -336,11 +322,11 @@
         2,
         grid=(1,),
         in_specs=[
-            pl.BlockSpec((pl.Element(8), pl.Element(256), pl.Element(128)), lambda t: (0, 384, 0)),
+            pl.BlockSpec((8, 256, 128), lambda t: (0, 0, 0)),
             pl.BlockSpec((8, 256, 128), lambda t: (0, 0, 0)),
         ],
         out_specs=whole(16, 16, 256),
-    )(final, final)
+    )(panel, final)
     coupling = exchange(coupling, COUPLED)
     mixing = pl.BlockSpec((8, 32, 128), lambda t: (0, 8 + t, 0))
     rotated = call(
@@ -355,22 +341,25 @@
     coupling, rotated = lax.optimization_barrier((coupling, rotated))
     coupling = exchange(call(sum_kernel, f32(16, 16, 256), 1)(coupling), COUPLED)
 
-    pair = pl.BlockSpec((2, 256, 128), lambda t: (t % 4, 0, 0))
-    piece = whole(4, 128, 256)
-    panel_pair = pl.BlockSpec((pl.Element(2), pl.Element(256), pl.Element(128)), lambda t: (2 * (t % 4), 384, 0))
+    mine = pl.BlockSpec((2, 256, 128), lambda t, w: (jnp.clip(t - 4 * w[0], 0, 3), 0, 0))
+    theirs = pl.BlockSpec((2, 256, 128), lambda t, w: (jnp.clip(t - 4 * (1 - w[0]), 0, 3), 0, 0))
+    piece = fixed(4, 128, 256)
     updated = call(
         update_kernel,
         f32(1024, 2048),
         12,
         60,
-        grid=(8,),
-        in_specs=[
-            SMEM, whole(1024, 768), piece, piece, whole(256, 256), whole(16, 16, 256), pair, pair, panel_pair,
-            panel_pair, pl.BlockSpec((1024, 256), lambda t: (0, t)),
-        ],
-        out_specs=pl.BlockSpec((1024, 256), lambda t: (0, t)),
-        scratch_shapes=[pltpu.VMEM((1024, 1536), BF16), pltpu.VMEM((1024, 256), F32)],
-    )(where, first, near, far, inverse, coupling, final, other, final, other, matrix)
+        grid_spec=pltpu.PrefetchScalarGridSpec(
+            num_scalar_prefetch=1,
+            grid=(8,),
+            in_specs=[
+                fixed(1024, 768), piece, piece, fixed(256, 256), fixed(16, 16, 256), mine, theirs, mine, theirs,
+                pl.BlockSpec((1024, 256), lambda t, w: (0, t)),
+            ],
+            out_specs=pl.BlockSpec((1024, 256), lambda t, w: (0, t)),
+            scratch_shapes=[pltpu.VMEM((1024, 1536), BF16), pltpu.VMEM((1024, 256), F32)],
+        ),
+    )(where, first, near, far, inverse, coupling, final, other, panel, other_panel, matrix)
     return (updated, rotated)
 
 

time: 195 us -> 194 us (level)
  blocking collectives: 44.7 us -> 25.6 us
  waiting for transfers between devices: 18.6 us -> 36.4 us
    all_to_all x2 -> x1, blocking collectives: 44.7 us -> 25.6 us  [exchange(): return lax.all_to_all(blocks, axes, 0, 0, tiled=True)]
    all_to_all x4 -> x5, waiting for transfers between devices: 11.4 us -> 25.8 us  [exchange(): return lax.all_to_all(blocks, axes, 0, 0, tiled=True)]
    ppermute x3 -> x4, waiting for transfers between devices: 0.01 us -> 3.19 us  [swap_cores(): return lax.ppermute(array, 'co', [(0, 1), (1, 0)])]
    pallas_call x6 -> x5, Pallas kernels: 32.2 us -> 29.5 us  [the longest x1 16.4 us: body(): call(update_kernel, f32(1024, 2048), 12, 60, grid_spec=pltpu.PrefetchScal...]
    all_to_all x4 -> x5, starting transfers between devices: 25.1 us -> 27.2 us  [exchange(): return lax.all_to_all(blocks, axes, 0, 0, tiled=True)]
    ppermute x3 -> x4, starting transfers between devices: 6.7 us -> 5.82 us  [swap_cores(): return lax.ppermute(array, 'co', [(0, 1), (1, 0)])]
  transfers between devices with their start and end apart: 20 -> 22, of which waited for: 5 -> 8; matrix products, arithmetic and copies ran while one was open for 0% -> 0% of each run, Pallas kernels for 23% -> 20%
where the time goes in v4:
time: 194 us; the launch traced here: 193 us
  starting transfers between devices  62.5 us (32%)
  Pallas kernels  59 us (30%)
  waiting for transfers between devices  36.4 us (19%)
  blocking collectives  25.6 us (13%)
  local copies, waits for them, and re-layouts  6.36 us (3%)
  other arithmetic  2.07 us (1%)
    all_to_all x5, starting transfers between devices, exchange(): return lax.all_to_all(blocks, axes, 0, 0, tiled=True)  27.2 us
    all_to_all x5, waiting for transfers between devices, exchange(): return lax.all_to_all(blocks, axes, 0, 0, tiled=True)  25.8 us
    all_to_all x1, blocking collectives, exchange(): return lax.all_to_all(blocks, axes, 0, 0, tiled=True)  25.6 us
    pallas_call x1, Pallas kernels, body(): call(update_kernel, f32(1024, 2048), 12, 60, grid_spec=pltpu.PrefetchScal...  16.4 us
    ppermute x7, starting transfers between devices, body(): parts.append(lax.ppermute(columns[k * 128:(k + 1) * 128], COL, [(0, k)]))  16.3 us
    pallas_call x1, Pallas kernels, body(): call(product_kernel, (f32(8, 384, 128), f32(8, 384, 128)), 12, 60, grid_s...  10.4 us
    pallas_call x1, Pallas kernels, body(): inverse = call(invert_second, f32(B, B), 9)(ai, t, schur)  9.09 us
    pallas_call x1, Pallas kernels, body(): ai, t, schur = call(invert_first, (f32(128, 128),) * 3, 9)(gram)  9.05 us
  transfers between devices with their start and end apart: 22, of which 8 were waited for; matrix products, arithmetic and copies ran while one was open for 0% of the time, Pallas kernels for 20%

profile of v4, /device:TPU:1, one launch (start us, length us, event | category | flops | bytes accessed | tf_op | source)
XLA Modules:
  0.0 192.9 jit_solution(13122006482314553717)
XLA Ops:
  0.7 1.4 slice_select_fusion
  2.1 0.1 fusion
  2.2 8.5 %collective-permute-start.6 = (f32[128,256]{1,0:T(8,128)S(1)}, f32[128,256]{1,0:T(8,128)S(1)}, u32[]{:S(2)}, u32[]{:S(2)}) collective-permute-start(f32[128,256]{1,0:T(8,128)S(1)} %get-tuple-element.48), channel_id=1, source_target_pairs={{0,7},{8,15},{16,23},{24,31},{32,39},{40,47},{48,55},{56,63},{64,7... | collective-permute-start | bytes 393224 | tf_op jit(solution)/shard_map/ppermute | solution.py:273
  10.7 1.3 collective-permute-start.5
  12.0 1.3 collective-permute-start.4
  13.3 1.3 collective-permute-start.3
  14.6 1.3 collective-permute-start.2
  15.9 0.0 collective-permute-done.6.refs_7_
  16.0 1.3 collective-permute-start.1
  17.3 0.0 collective-permute-done.5.refs_6_
  17.3 1.3 collective-permute-start
  18.6 0.0 collective-permute-done.4.refs_5_
  18.6 0.0 collective-permute-done.3.refs_4_
  18.6 2.5 %collective-permute-done.2.refs_3_ = f32[128,256]{1,0:T(8,128)S(1)} collective-permute-done((f32[128,256]{1,0:T(8,128)S(1)}, f32[128,256]{1,0:T(8,128)S(1)}, u32[]{:S(2)}, u32[]{:S(2)}) %collective-permute-start.2) | collective-permute-done | bytes 131104 | tf_op jit(solution)/shard_map/ppermute | solution.py:273
  21.1 2.8 %collective-permute-done.1.refs_2_ = f32[128,256]{1,0:T(8,128)S(1)} collective-permute-done((f32[128,256]{1,0:T(8,128)S(1)}, f32[128,256]{1,0:T(8,128)S(1)}, u32[]{:S(2)}, u32[]{:S(2)}) %collective-permute-start.1) | collective-permute-done | bytes 131104 | tf_op jit(solution)/shard_map/ppermute | solution.py:273
  23.9 0.0 collective-permute-done.refs_1_
  23.9 1.0 shard_map.41
  24.9 3.6 %all-to-all-start = ((f32[8,128,256]{2,1,0:T(8,128)}), f32[8,128,256]{2,1,0:T(8,128)S(1)}, u32[]{:S(2)}, u32[]{:S(2)}) async-start(f32[8,128,256]{2,1,0:T(8,128)} %get-tuple-element.25), calls=%async_computation | async-start | bytes 2097152 | tf_op jit(solution)/shard_map/all_to_all | solution.py:229
  28.5 0.7 collective-permute-start.7
  29.2 0.0 collective-permute-done.7.block_ref
  29.2 13.3 %all-to-all-done = f32[8,128,256]{2,1,0:T(8,128)S(1)} async-done(((f32[8,128,256]{2,1,0:T(8,128)}), f32[8,128,256]{2,1,0:T(8,128)S(1)}, u32[]{:S(2)}, u32[]{:S(2)}) %all-to-all-start) | async-done | bytes 1048608 | tf_op jit(solution)/shard_map/all_to_all | solution.py:229
  42.5 2.3 %shard_map.42 = (f32[8,320,128]{2,1,0:T(8,128)}, bf16[512,1024]{1,0:T(8,128)(2,1)S(1)}) custom-call(f32[1024,256]{1,0:T(8,128)S(1)} %bitcast.9, f32[256,128]{1,0:T(8,128)S(1)} %collective-permute-done.7.block_ref), custom_call_target="tpu_custom_call" | custom-call | flops 2000000000 | bytes 1024 | tf_op jit(solution)/shard_map/pallas_call | solution.py:279
  44.8 1.0 copy-done.7
  45.8 10.4 %all-to-all-start.1 = ((f32[8,320,128]{2,1,0:T(8,128)}), f32[8,320,128]{2,1,0:T(8,128)S(1)}, u32[]{:S(2)}, u32[]{:S(2)}) async-start(f32[8,320,128]{2,1,0:T(8,128)} %get-tuple-element.30), calls=%async_computation.1 | async-start | bytes 2621440 | tf_op jit(solution)/shard_map/all_to_all | solution.py:229
  56.3 10.4 %shard_map.43 = (f32[8,384,128]{2,1,0:T(8,128)}, f32[8,384,128]{2,1,0:T(8,128)}) custom-call(s32[1]{0:T(128)} %bitcast.core_ref, bf16[512,1024]{1,0:T(8,128)(2,1)} %copy-done.7, f32[1024,2048]{1,0:T(8,128)} %matrix_ref.1, f32[1024,2048]{1,0:T(8,128)} %matrix_ref.1, f32[1024,1024]{1,0:T(8,128)} %vectors_ref.3), custom_call_target="tpu_custom_call" | custom-call | flops 12000000000 | bytes 1024 | tf_op jit(solution)/shard_map/pallas_call | solution.py:284
  66.7 6.5 %all-to-all-done.1.panel_ref.pmine_ref = f32[8,320,128]{2,1,0:T(8,128)S(1)} async-done(((f32[8,320,128]{2,1,0:T(8,128)}), f32[8,320,128]{2,1,0:T(8,128)S(1)}, u32[]{:S(2)}, u32[]{:S(2)}) %all-to-all-start.1) | async-done | bytes 1310752 | tf_op jit(solution)/shard_map/all_to_all | solution.py:229
  73.2 2.7 %collective-permute-start.8 = (f32[8,384,128]{2,1,0:T(8,128)}, f32[8,384,128]{2,1,0:T(8,128)S(1)}, u32[]{:S(2)}, u32[]{:S(2)}) collective-permute-start(f32[8,384,128]{2,1,0:T(8,128)} %get-tuple-element.32), channel_id=1, source_target_pairs={{0,8},{8,0},{1,9},{9,1},{2,10},{10,2},{3,11},{11,3},{4,12},{12,4},... | collective-permute-start | bytes 4718600 | tf_op jit(solution)/shard_map/ppermute | solution.py:233
  76.0 0.1 collective-permute-start.9
  76.1 2.8 %collective-permute-done.9.other_ref = f32[64,128]{1,0:T(8,128)S(1)} collective-permute-done((f32[64,128]{1,0:T(8,128)S(1)}, f32[64,128]{1,0:T(8,128)S(1)}, u32[]{:S(2)}, u32[]{:S(2)}) %collective-permute-start.9) | collective-permute-done | bytes 32800 | tf_op jit(solution)/shard_map/ppermute | solution.py:233
  78.9 0.3 collective-permute-done.8.got_ref
  79.3 1.4 copy-done.1
  80.7 0.2 shard_map.44
  80.9 25.6 %all_to_all.30.in_ref = f32[8,448,128]{2,1,0:T(8,128)S(1)} all-to-all(f32[8,448,128]{2,1,0:T(8,128)S(1)} %shard_map.44), channel_id=1, replica_groups=mesh['y'=4,'zl'=2,'co'=2,'x'=4,'zh'=2] {'y','zl'}, dimensions={0} | all-to-all | bytes 3670016 | tf_op jit(solution)/shard_map/all_to_all | solution.py:229
  106.5 0.2 shard_map.45
  106.7 0.0 copy-start.3
  106.7 1.1 copy-done.3
  107.9 3.6 %all-to-all-start.3 = ((f32[8,384,128]{2,1,0:T(8,128)}), f32[8,384,128]{2,1,0:T(8,128)S(1)}, u32[]{:S(2)}, u32[]{:S(2)}) async-start(f32[8,384,128]{2,1,0:T(8,128)} %copy-done.3), calls=%async_computation.3 | async-start | bytes 3145728 | tf_op jit(solution)/shard_map/all_to_all | solution.py:229
  111.4 0.7 collective-permute-start.10
  112.1 9.0 %shard_map.46 = (f32[128,128]{1,0:T(8,128)S(1)}, f32[128,128]{1,0:T(8,128)S(1)}, f32[128,128]{1,0:T(8,128)S(1)}) custom-call(f32[8,64,128]{2,1,0:T(8,128)S(1)} %get-tuple-element.36.gram_ref), custom_call_target="tpu_custom_call" | custom-call | flops 8999999488 | bytes 1024 | tf_op jit(solution)/shard_map/pallas_call | solution.py:311
  121.2 0.0 collective-permute-done.10
  121.2 3.8 %collective-permute-start.13 = (f32[128,256]{1,0:T(8,128)S(1)}, f32[128,256]{1,0:T(8,128)S(1)}, u32[]{:S(2)}, u32[]{:S(2)}) collective-permute-start(f32[128,256]{1,0:T(8,128)S(1)} %collective-permute-done.10), channel_id=1, source_target_pairs={{6,0},{0,2},{2,4},{4,6},{7,1},{1,3},{3,5},{5,7},{14,8},{8,10},{10,... | collective-permute-start | bytes 393224 | tf_op jit(solution)/shard_map/ppermute | solution.py:237
  125.0 3.6 %collective-permute-start.12 = (f32[128,256]{1,0:T(8,128)S(1)}, f32[128,256]{1,0:T(8,128)S(1)}, u32[]{:S(2)}, u32[]{:S(2)}) collective-permute-start(f32[128,256]{1,0:T(8,128)S(1)} %collective-permute-done.10), channel_id=1, source_target_pairs={{4,0},{6,2},{0,4},{2,6},{5,1},{7,3},{1,5},{3,7},{12,8},{14,10},{8,... | collective-permute-start | bytes 393224 | tf_op jit(solution)/shard_map/ppermute | solution.py:237
  128.7 1.5 collective-permute-start.11
  130.1 9.1 %shard_map.47.inverse_ref = f32[256,256]{1,0:T(8,128)S(1)} custom-call(f32[128,128]{1,0:T(8,128)S(1)} %get-tuple-element.37.ai_ref, f32[128,128]{1,0:T(8,128)S(1)} %get-tuple-element.38.t_ref, f32[128,128]{1,0:T(8,128)S(1)} %get-tuple-element.39.schur_ref), custom_call_target="tpu_custom_call" | custom-call | flops 8999999488 | bytes 1024 | tf_op jit(solution)/shard_map/pallas_call | solution.py:312
  139.2 0.0 collective-permute-done.13
  139.2 0.0 collective-permute-done.12
  139.3 1.4 shard_map.48
  140.8 0.8 copy-done.6
  141.6 1.2 copy-done.8
  142.8 2.9 %collective-permute-start.15 = (f32[8,384,128]{2,1,0:T(8,128)S(1)}, f32[8,384,128]{2,1,0:T(8,128)}, u32[]{:S(2)}, u32[]{:S(2)}) collective-permute-start(f32[8,384,128]{2,1,0:T(8,128)S(1)} %all-to-all-done.3.product_ref.mine_ref), channel_id=1, source_target_pairs={{0,8},{8,0},{1,9},{9,1},{2,10},{10,2},{3,11},{11,3},{4,12},{12,4},... | collective-permute-start | bytes 4718600 | tf_op jit(solution)/shard_map/ppermute | solution.py:233
  145.7 0.1 collective-permute-start.16
  145.8 1.3 shard_map.49
  147.2 4.7 %all-to-all-start.4 = ((f32[16,16,256]{2,1,0:T(8,128)}), f32[16,16,256]{2,1,0:T(8,128)S(1)}, u32[]{:S(2)}, u32[]{:S(2)}) async-start(f32[16,16,256]{2,1,0:T(8,128)} %shard_map.49), calls=%async_computation.4 | async-start | bytes 524288 | tf_op jit(solution)/shard_map/all_to_all | solution.py:229
  151.9 2.9 %collective-permute-start.14 = (f32[4,128,256]{2,1,0:T(8,128)}, f32[4,128,256]{2,1,0:T(8,128)}, u32[]{:S(2)}, u32[]{:S(2)}) collective-permute-start(f32[4,128,256]{2,1,0:T(8,128)} %copy-done.6), channel_id=1, source_target_pairs={{0,1},{1,0},{2,3},{3,2},{4,5},{5,4},{6,7},{7,6},{8,9},{9,8},{10,11... | collective-permute-start | bytes 1572872 | tf_op jit(solution)/shard_map/ppermute | solution.py:318
  154.7 6.8 %shard_map.50 = f32[1024,1024]{1,0:T(8,128)} custom-call(s32[1]{0:T(128)} %bitcast.core_ref, bf16[1024,768]{1,0:T(8,128)(2,1)} %copy-done.8, f32[8,384,128]{2,1,0:T(8,128)} %copy-done.2, f32[8,384,128]{2,1,0:T(8,128)} %collective-permute-done.15.other_ref, f32[1024,1024]{1,0:T(8,128)} %vectors_ref.3), custom_call_target="tpu_custom_call" | custom-call | flops 6000000000 | bytes 1024 | tf_op jit(solution)/shard_map/pallas_call | solution.py:332
  161.5 0.0 all-to-all-done.4.in_ref
  161.5 0.7 shard_map.51
  162.3 4.9 %all-to-all-start.5 = ((f32[16,16,256]{2,1,0:T(8,128)}), f32[16,16,256]{2,1,0:T(8,128)S(1)}, u32[]{:S(2)}, u32[]{:S(2)}) async-start(f32[16,16,256]{2,1,0:T(8,128)} %shard_map.51), calls=%async_computation.5 | async-start | bytes 524288 | tf_op jit(solution)/shard_map/all_to_all | solution.py:229
  167.2 0.6 pad_add_fusion.where_ref
  167.8 0.0 collective-permute-done.16.pother_ref
  167.8 2.1 %collective-permute-done.14.far_ref = f32[4,128,256]{2,1,0:T(8,128)} collective-permute-done((f32[4,128,256]{2,1,0:T(8,128)}, f32[4,128,256]{2,1,0:T(8,128)}, u32[]{:S(2)}, u32[]{:S(2)}) %collective-permute-start.14) | collective-permute-done | bytes 524320 | tf_op jit(solution)/shard_map/ppermute | solution.py:318
  169.9 6.0 %all-to-all-done.5.coupling_ref = f32[16,16,256]{2,1,0:T(8,128)S(1)} async-done(((f32[16,16,256]{2,1,0:T(8,128)}), f32[16,16,256]{2,1,0:T(8,128)S(1)}, u32[]{:S(2)}, u32[]{:S(2)}) %all-to-all-start.5) | async-done | bytes 262176 | tf_op jit(solution)/shard_map/all_to_all | solution.py:229
  175.9 0.7 copy-done.10
  176.6 16.4 %shard_map.52 = f32[1024,2048]{1,0:T(8,128)} custom-call(s32[3]{0:T(128)} %pad_add_fusion.where_ref, bf16[1024,768]{1,0:T(8,128)(2,1)} %copy-done.8, f32[4,128,256]{2,1,0:T(8,128)} %copy-done.6, f32[4,128,256]{2,1,0:T(8,128)} %collective-permute-done.14.far_ref, f32[256,256]{1,0:T(8,128)} %copy-done.9, f32[16,16,256]{2,1,0:T(8,128)} %copy-done.10, ...), custom_call_target="tpu_custom_call" | custom-call | flops 12000000000 | bytes 1024 | tf_op jit(solution)/shard_map/pallas_call | solution.py:347
  (21 shorter events, 0.1 us)
Async XLA Ops:
  2.2 13.8 %collective-permute-start.6 = (f32[128,256]{1,0:T(8,128)S(1)}, f32[128,256]{1,0:T(8,128)S(1)}, u32[]{:S(2)}, u32[]{:S(2)}) collective-permute-start(f32[128,256]{1,0:T(8,128)S(1)} %get-tuple-element.48), channel_id=1, source_target_pairs={{0,7},{8,15},{16,23},{24,31},{32,39},{40,47},{48,55},{56,63},{64,7... | collective-permute-start | bytes 393224 | tf_op jit(solution)/shard_map/ppermute | solution.py:273
  10.7 6.5 %collective-permute-start.5 = (f32[128,256]{1,0:T(8,128)S(1)}, f32[128,256]{1,0:T(8,128)S(1)}, u32[]{:S(2)}, u32[]{:S(2)}) collective-permute-start(f32[128,256]{1,0:T(8,128)S(1)} %get-tuple-element.49), channel_id=1, source_target_pairs={{0,6},{8,14},{16,22},{24,30},{32,38},{40,46},{48,54},{56,62},{64,7... | collective-permute-start | bytes 393224 | tf_op jit(solution)/shard_map/ppermute | solution.py:273
  12.0 6.6 %collective-permute-start.4 = (f32[128,256]{1,0:T(8,128)S(1)}, f32[128,256]{1,0:T(8,128)S(1)}, u32[]{:S(2)}, u32[]{:S(2)}) collective-permute-start(f32[128,256]{1,0:T(8,128)S(1)} %get-tuple-element.50), channel_id=1, source_target_pairs={{0,5},{8,13},{16,21},{24,29},{32,37},{40,45},{48,53},{56,61},{64,6... | collective-permute-start | bytes 393224 | tf_op jit(solution)/shard_map/ppermute | solution.py:273
  13.3 5.3 %collective-permute-start.3 = (f32[128,256]{1,0:T(8,128)S(1)}, f32[128,256]{1,0:T(8,128)S(1)}, u32[]{:S(2)}, u32[]{:S(2)}) collective-permute-start(f32[128,256]{1,0:T(8,128)S(1)} %get-tuple-element.51), channel_id=1, source_target_pairs={{0,4},{8,12},{16,20},{24,28},{32,36},{40,44},{48,52},{56,60},{64,6... | collective-permute-start | bytes 393224 | tf_op jit(solution)/shard_map/ppermute | solution.py:273
  14.6 6.5 %collective-permute-start.2 = (f32[128,256]{1,0:T(8,128)S(1)}, f32[128,256]{1,0:T(8,128)S(1)}, u32[]{:S(2)}, u32[]{:S(2)}) collective-permute-start(f32[128,256]{1,0:T(8,128)S(1)} %get-tuple-element.52), channel_id=1, source_target_pairs={{0,3},{8,11},{16,19},{24,27},{32,35},{40,43},{48,51},{56,59},{64,6... | collective-permute-start | bytes 393224 | tf_op jit(solution)/shard_map/ppermute | solution.py:273
  16.0 7.9 %collective-permute-start.1 = (f32[128,256]{1,0:T(8,128)S(1)}, f32[128,256]{1,0:T(8,128)S(1)}, u32[]{:S(2)}, u32[]{:S(2)}) collective-permute-start(f32[128,256]{1,0:T(8,128)S(1)} %get-tuple-element.53), channel_id=1, source_target_pairs={{0,2},{8,10},{16,18},{24,26},{32,34},{40,42},{48,50},{56,58},{64,6... | collective-permute-start | bytes 393224 | tf_op jit(solution)/shard_map/ppermute | solution.py:273
  17.3 6.6 %collective-permute-start = (f32[128,256]{1,0:T(8,128)S(1)}, f32[128,256]{1,0:T(8,128)S(1)}, u32[]{:S(2)}, u32[]{:S(2)}) collective-permute-start(f32[128,256]{1,0:T(8,128)S(1)} %get-tuple-element.54), channel_id=1, source_target_pairs={{0,1},{8,9},{16,17},{24,25},{32,33},{40,41},{48,49},{56,57},{64,65... | collective-permute-start | bytes 393224 | tf_op jit(solution)/shard_map/ppermute | solution.py:273
  24.9 17.5 %all-to-all-start = ((f32[8,128,256]{2,1,0:T(8,128)}), f32[8,128,256]{2,1,0:T(8,128)S(1)}, u32[]{:S(2)}, u32[]{:S(2)}) async-start(f32[8,128,256]{2,1,0:T(8,128)} %get-tuple-element.25), calls=%async_computation | async-start | bytes 2097152 | tf_op jit(solution)/shard_map/all_to_all | solution.py:229
  28.5 0.7 collective-permute-start.7
  42.5 2.3 %copy-start.4 = (f32[8,128,256]{2,1,0:T(8,128)}, f32[8,128,256]{2,1,0:T(8,128)S(1)}, u32[]{:S(2)}) copy-start(f32[8,128,256]{2,1,0:T(8,128)S(1)} %all-to-all-done) | copy-start | bytes 3145732
  44.8 1.0 copy-start.7
  45.8 27.4 %all-to-all-start.1 = ((f32[8,320,128]{2,1,0:T(8,128)}), f32[8,320,128]{2,1,0:T(8,128)S(1)}, u32[]{:S(2)}, u32[]{:S(2)}) async-start(f32[8,320,128]{2,1,0:T(8,128)} %get-tuple-element.30), calls=%async_computation.1 | async-start | bytes 2621440 | tf_op jit(solution)/shard_map/all_to_all | solution.py:229
  73.2 72.6 %copy-start = (f32[8,320,128]{2,1,0:T(8,128)}, f32[8,320,128]{2,1,0:T(8,128)S(1)}, u32[]{:S(2)}) copy-start(f32[8,320,128]{2,1,0:T(8,128)S(1)} %all-to-all-done.1.panel_ref.pmine_ref) | copy-start | bytes 3932164
  73.2 6.0 %collective-permute-start.8 = (f32[8,384,128]{2,1,0:T(8,128)}, f32[8,384,128]{2,1,0:T(8,128)S(1)}, u32[]{:S(2)}, u32[]{:S(2)}) collective-permute-start(f32[8,384,128]{2,1,0:T(8,128)} %get-tuple-element.32), channel_id=1, source_target_pairs={{0,8},{8,0},{1,9},{9,1},{2,10},{10,2},{3,11},{11,3},{4,12},{12,4},... | collective-permute-start | bytes 4718600 | tf_op jit(solution)/shard_map/ppermute | solution.py:233
  76.0 2.9 %collective-permute-start.9 = (f32[64,128]{1,0:T(8,128)S(1)}, f32[64,128]{1,0:T(8,128)S(1)}, u32[]{:S(2)}, u32[]{:S(2)}) collective-permute-start(f32[64,128]{1,0:T(8,128)S(1)} %slice_reduce_fusion.gram_ref), channel_id=1, source_target_pairs={{0,8},{8,0},{1,9},{9,1},{2,10},{10,2},{3,11},{11,3},{4,12},{12,4},... | collective-permute-start | bytes 98312 | tf_op jit(solution)/shard_map/ppermute | solution.py:233
  79.3 1.4 copy-start.1
  106.7 1.1 copy-start.3
  107.9 35.0 %all-to-all-start.3 = ((f32[8,384,128]{2,1,0:T(8,128)}), f32[8,384,128]{2,1,0:T(8,128)S(1)}, u32[]{:S(2)}, u32[]{:S(2)}) async-start(f32[8,384,128]{2,1,0:T(8,128)} %copy-done.3), calls=%async_computation.3 | async-start | bytes 3145728 | tf_op jit(solution)/shard_map/all_to_all | solution.py:229
  111.4 9.7 %collective-permute-start.10 = (f32[128,256]{1,0:T(8,128)S(1)}, f32[128,256]{1,0:T(8,128)S(1)}, u32[]{:S(2)}, u32[]{:S(2)}) collective-permute-start(f32[128,256]{1,0:T(8,128)S(1)} %get-tuple-element.35), channel_id=1, source_target_pairs={{0,0},{16,1},{32,2},{48,3},{64,4},{80,5},{96,6},{112,7},{8,8},{24,... | collective-permute-start | bytes 393224 | tf_op jit(solution)/shard_map/ppermute | solution.py:310
  121.2 18.1 %collective-permute-start.13 = (f32[128,256]{1,0:T(8,128)S(1)}, f32[128,256]{1,0:T(8,128)S(1)}, u32[]{:S(2)}, u32[]{:S(2)}) collective-permute-start(f32[128,256]{1,0:T(8,128)S(1)} %collective-permute-done.10), channel_id=1, source_target_pairs={{6,0},{0,2},{2,4},{4,6},{7,1},{1,3},{3,5},{5,7},{14,8},{8,10},{10,... | collective-permute-start | bytes 393224 | tf_op jit(solution)/shard_map/ppermute | solution.py:237
  125.0 14.2 %collective-permute-start.12 = (f32[128,256]{1,0:T(8,128)S(1)}, f32[128,256]{1,0:T(8,128)S(1)}, u32[]{:S(2)}, u32[]{:S(2)}) collective-permute-start(f32[128,256]{1,0:T(8,128)S(1)} %collective-permute-done.10), channel_id=1, source_target_pairs={{4,0},{6,2},{0,4},{2,6},{5,1},{7,3},{1,5},{3,7},{12,8},{14,10},{8,... | collective-permute-start | bytes 393224 | tf_op jit(solution)/shard_map/ppermute | solution.py:237
  128.7 10.6 %collective-permute-start.11 = (f32[128,256]{1,0:T(8,128)S(1)}, f32[128,256]{1,0:T(8,128)S(1)}, u32[]{:S(2)}, u32[]{:S(2)}) collective-permute-start(f32[128,256]{1,0:T(8,128)S(1)} %collective-permute-done.10), channel_id=1, source_target_pairs={{2,0},{4,2},{6,4},{0,6},{3,1},{5,3},{7,5},{1,7},{10,8},{12,10},{14... | collective-permute-start | bytes 393224 | tf_op jit(solution)/shard_map/ppermute | solution.py:237
  130.1 9.2 %copy-start.5 = (f32[8,128,256]{2,1,0:T(8,128)S(1)}, f32[8,128,256]{2,1,0:T(8,128)}, u32[]{:S(2)}) copy-start(f32[8,128,256]{2,1,0:T(8,128)} %copy-done.4) | copy-start | bytes 3145732
  139.2 1.5 copy-start.9
  140.8 0.9 copy-start.6
  141.6 1.2 copy-start.8
  142.8 4.4 %copy-start.2 = (f32[8,384,128]{2,1,0:T(8,128)}, f32[8,384,128]{2,1,0:T(8,128)S(1)}, u32[]{:S(2)}) copy-start(f32[8,384,128]{2,1,0:T(8,128)S(1)} %all-to-all-done.3.product_ref.mine_ref) | copy-start | bytes 4718596
  142.8 11.9 %collective-permute-start.15 = (f32[8,384,128]{2,1,0:T(8,128)S(1)}, f32[8,384,128]{2,1,0:T(8,128)}, u32[]{:S(2)}, u32[]{:S(2)}) collective-permute-start(f32[8,384,128]{2,1,0:T(8,128)S(1)} %all-to-all-done.3.product_ref.mine_ref), channel_id=1, source_target_pairs={{0,8},{8,0},{1,9},{9,1},{2,10},{10,2},{3,11},{11,3},{4,12},{12,4},... | collective-permute-start | bytes 4718600 | tf_op jit(solution)/shard_map/ppermute | solution.py:233
  145.7 22.0 %collective-permute-start.16 = (f32[8,320,128]{2,1,0:T(8,128)S(1)}, f32[8,320,128]{2,1,0:T(8,128)}, u32[]{:S(2)}, u32[]{:S(2)}) collective-permute-start(f32[8,320,128]{2,1,0:T(8,128)S(1)} %all-to-all-done.1.panel_ref.pmine_ref), channel_id=1, source_target_pairs={{0,8},{8,0},{1,9},{9,1},{2,10},{10,2},{3,11},{11,3},{4,12},{12,4},... | collective-permute-start | bytes 3932168 | tf_op jit(solution)/shard_map/ppermute | solution.py:233
  147.2 14.4 %all-to-all-start.4 = ((f32[16,16,256]{2,1,0:T(8,128)}), f32[16,16,256]{2,1,0:T(8,128)S(1)}, u32[]{:S(2)}, u32[]{:S(2)}) async-start(f32[16,16,256]{2,1,0:T(8,128)} %shard_map.49), calls=%async_computation.4 | async-start | bytes 524288 | tf_op jit(solution)/shard_map/all_to_all | solution.py:229
  151.9 18.0 %collective-permute-start.14 = (f32[4,128,256]{2,1,0:T(8,128)}, f32[4,128,256]{2,1,0:T(8,128)}, u32[]{:S(2)}, u32[]{:S(2)}) collective-permute-start(f32[4,128,256]{2,1,0:T(8,128)} %copy-done.6), channel_id=1, source_target_pairs={{0,1},{1,0},{2,3},{3,2},{4,5},{5,4},{6,7},{7,6},{8,9},{9,8},{10,11... | collective-permute-start | bytes 1572872 | tf_op jit(solution)/shard_map/ppermute | solution.py:318
  162.3 13.6 %all-to-all-start.5 = ((f32[16,16,256]{2,1,0:T(8,128)}), f32[16,16,256]{2,1,0:T(8,128)S(1)}, u32[]{:S(2)}, u32[]{:S(2)}) async-start(f32[16,16,256]{2,1,0:T(8,128)} %shard_map.51), calls=%async_computation.5 | async-start | bytes 524288 | tf_op jit(solution)/shard_map/all_to_all | solution.py:229
  175.9 0.7 copy-start.10

commit v5 on v4

--- a/solution.py
+++ b/solution.py
@@ -45,32 +45,60 @@
     return jax.ShapeDtypeStruct(shape, F32)
 
 
+def invert2(a, b, d):
+    scale = 1.0 / (a * d - b * b)
+    return d * scale, -(b * scale), a * scale
+
+
+def invert4(d):
+    a00, a01, a11 = invert2(d[0][0], d[0][1], d[1][1])
+    a = ((a00, a01), (a01, a11))
+    t = [[a[i][0] * d[0][j] + a[i][1] * d[1][j] for j in (2, 3)] for i in (0, 1)]
+    s = lambda i, j: d[i][j] - (d[0][i] * t[0][j - 2] + d[1][i] * t[1][j - 2])
+    s00, s01, s11 = invert2(s(2, 2), s(2, 3), s(3, 3))
+    c = ((s00, s01), (s01, s11))
+    u = [[t[i][0] * c[0][j] + t[i][1] * c[1][j] for j in (0, 1)] for i in (0, 1)]
+    top = [[a[i][j] + (u[i][0] * t[j][0] + u[i][1] * t[j][1]) for j in (0, 1)] for i in (0, 1)]
+    top[1][0] = top[0][1]
+    return [
+        [top[0][0], top[0][1], -u[0][0], -u[0][1]],
+        [top[1][0], top[1][1], -u[1][0], -u[1][1]],
+        [-u[0][0], -u[1][0], s00, s01],
+        [-u[0][1], -u[1][1], s01, s11],
+    ]
+
+
 def sweep_all(block):
-    n, group = 128, 16
+    n, group, size = 128, 16, 4
     lane = lax.broadcasted_iota(jnp.int32, (8, n), 1)
     line = lax.broadcasted_iota(jnp.int32, (8, n), 0)
     tiles = n // 8
 
+    def column(tile, k):
+        return jnp.broadcast_to(tile[:, k : k + 1], (8, n))
+
     def step(_, s):
         s = list(s)
-        for k in range(0, group, 2):
-            t, sub = k // 8, k % 8
-            r0 = jnp.broadcast_to(s[t][sub : sub + 1, :], (8, n))
-            r1 = jnp.broadcast_to(s[t][sub + 1 : sub + 2, :], (8, n))
-            a = jnp.broadcast_to(r0[:, k : k + 1], (8, n))
-            b = jnp.broadcast_to(r1[:, k : k + 1], (8, n))
-            d = jnp.broadcast_to(r1[:, k + 1 : k + 2], (8, n))
-            scale = 1.0 / (a * d - b * b)
-            ia, ib, ic = d * scale, -b * scale, a * scale
-            q0 = jnp.where(lane == k, -ia, jnp.where(lane == k + 1, -ib, ia * r0 + ib * r1))
-            q1 = jnp.where(lane == k, -ib, jnp.where(lane == k + 1, -ic, ib * r0 + ic * r1))
-            pivots = (lane == k) | (lane == k + 1)
+        for k in range(0, group, size):
+            own, sub = k // 8, k % 8
+            rows = [jnp.broadcast_to(s[own][sub + i : sub + i + 1, :], (8, n)) for i in range(size)]
+            d = [[column(rows[i], k + j) if j >= i else None for j in range(size)] for i in range(size)]
+            inverse = invert4(d)
+            scaled = []
+            for i in range(size):
+                e = inverse[i]
+                q = (e[0] * rows[0] + e[1] * rows[1]) + (e[2] * rows[2] + e[3] * rows[3])
+                for j in range(size):
+                    q = jnp.where(lane == k + j, -e[j], q)
+                scaled.append(q)
+            pivots = (lane >= k) & (lane < k + size)
             for u in range(tiles):
-                c0 = jnp.broadcast_to(s[u][:, k : k + 1], (8, n))
-                c1 = jnp.broadcast_to(s[u][:, k + 1 : k + 2], (8, n))
-                new = jnp.where(pivots, 0.0, s[u]) - c0 * q0 - c1 * q1
-                if u == t:
-                    new = jnp.where(line == sub, q0, jnp.where(line == sub + 1, q1, new))
+                c = [column(s[u], k + i) for i in range(size)]
+                change = (c[0] * scaled[0] + c[1] * scaled[1]) + (c[2] * scaled[2] + c[3] * scaled[3])
+                new = jnp.where(pivots, 0.0, s[u]) - change
+                if u == own:
+                    for i in range(size):
+                        new = jnp.where(line == sub + i, scaled[i], new)
                 s[u] = new
         s = s[group // 8 :] + s[: group // 8]
         return tuple(pltpu.roll(v, n - group, 1) for v in s)
@@ -150,14 +178,13 @@
         out_ref[m, 384:, :] = gram
 
 
-def reduce_kernel(in_ref, product_ref, gram_ref, out_ref):
+def reduce_kernel(in_ref, product_ref, own_ref, gram_ref):
     own = in_ref[0, :384, :]
     for m in range(1, 8):
         own = own + in_ref[m, :384, :]
     product_ref[...] = own[:256].T
+    own_ref[...] = own
     gram_ref[...] = in_ref[:, 384:, :]
-    for m in range(8):
-        out_ref[m] = own
 
 
 def coupling_kernel(panel_ref, product_ref, out_ref):
@@ -213,10 +240,10 @@
         left_ref[:, :768] = first_ref[...]
         left_ref[:, 768:1024], left_ref[:, 1024:1280], left_ref[:, 1280:] = hi, hi, lo
 
-    mine = step // 4 == where_ref[0]
+    mine = step // 2 == where_ref[0]
     product = jnp.where(mine, mine_ref[...], other_ref[...])
     panel = jnp.where(mine, pmine_ref[...], pother_ref[...])
-    halves = [split(jnp.concatenate([a[0], a[1]], axis=1)) for a in (product, panel)]
+    halves = [split(jnp.concatenate([a[m] for m in range(4)], axis=1)) for a in (product, panel)]
     right = jnp.concatenate([x for hi, lo in halves for x in (hi, lo, hi)], axis=0)
     out_ref[...] = matrix_ref[...] - lax.dot_general(left_ref[...], right, NN, preferred_element_type=F32)
 
@@ -305,8 +332,8 @@
     other_panel = swap_cores(panel)
     came = exchange(call(join_kernel, f32(8, 448, 128), 1, 12)(keep, got, gram, other_gram), CHIPS)
 
-    product, gram, sent = call(reduce_kernel, (f32(128, 256), f32(8, 64, 128), f32(8, 384, 128)), 2, 12)(came)
-    final = exchange(sent, CHIPS)
+    product, own, gram = call(reduce_kernel, (f32(128, 256), f32(384, 128), f32(8, 64, 128)), 2, 12)(came)
+    final = exchange(repeat(own), CHIPS)
     near = gather_x(lax.ppermute(product, ALL, back))
     ai, t, schur = call(invert_first, (f32(128, 128),) * 3, 9)(gram)
     inverse = call(invert_second, f32(B, B), 9)(ai, t, schur)
@@ -327,7 +354,7 @@
         ],
         out_specs=whole(16, 16, 256),
     )(panel, final)
-    coupling = exchange(coupling, COUPLED)
+    coupling = exchange(call(sum_kernel, f32(16, 16, 256), 1)(exchange(coupling, COUPLED)), COUPLED)
     mixing = pl.BlockSpec((8, 32, 128), lambda t: (0, 8 + t, 0))
     rotated = call(
         rotate_kernel,
@@ -339,10 +366,9 @@
         out_specs=pl.BlockSpec((1024, 256), lambda t: (0, t)),
     )(core, first, final, other, vectors)
     coupling, rotated = lax.optimization_barrier((coupling, rotated))
-    coupling = exchange(call(sum_kernel, f32(16, 16, 256), 1)(coupling), COUPLED)
-
-    mine = pl.BlockSpec((2, 256, 128), lambda t, w: (jnp.clip(t - 4 * w[0], 0, 3), 0, 0))
-    theirs = pl.BlockSpec((2, 256, 128), lambda t, w: (jnp.clip(t - 4 * (1 - w[0]), 0, 3), 0, 0))
+
+    mine = pl.BlockSpec((4, 256, 128), lambda t, w: (jnp.clip(t - 2 * w[0], 0, 1), 0, 0))
+    theirs = pl.BlockSpec((4, 256, 128), lambda t, w: (jnp.clip(t - 2 * (1 - w[0]), 0, 1), 0, 0))
     piece = fixed(4, 128, 256)
     updated = call(
         update_kernel,
@@ -351,12 +377,12 @@
         60,
         grid_spec=pltpu.PrefetchScalarGridSpec(
             num_scalar_prefetch=1,
-            grid=(8,),
+            grid=(4,),
             in_specs=[
                 fixed(1024, 768), piece, piece, fixed(256, 256), fixed(16, 16, 256), mine, theirs, mine, theirs,
-                pl.BlockSpec((1024, 256), lambda t, w: (0, t)),
+                pl.BlockSpec((1024, 512), lambda t, w: (0, t)),
             ],
-            out_specs=pl.BlockSpec((1024, 256), lambda t, w: (0, t)),
+            out_specs=pl.BlockSpec((1024, 512), lambda t, w: (0, t)),
             scratch_shapes=[pltpu.VMEM((1024, 1536), BF16), pltpu.VMEM((1024, 256), F32)],
         ),
     )(where, first, near, far, inverse, coupling, final, other, panel, other_panel, matrix)

time: 194 us -> 186 us (0.959)
  Pallas kernels: 59 us -> 53.4 us
    ppermute x3, starting transfers between devices: 8.94 us -> 3.89 us  [gather_x(): lax.ppermute(block, 'x', [((x + k) % 4, x) for x in range(4)])]
    all_to_all x5, starting transfers between devices: 27.2 us -> 31.4 us  [exchange(): return lax.all_to_all(blocks, axes, 0, 0, tiled=True)]
    ppermute x1, waiting for transfers between devices: 2.1 us -> 0.01 us  [body(): far = lax.ppermute(near, 'zh', [(0, 1), (1, 0)])]
    pallas_call x1, Pallas kernels: 9.05 us -> 6.99 us  [body(): ai, t, schur = call(invert_first, (f32(128, 128),) * 3, 9)(gram)]
    pallas_call x1, Pallas kernels: 9.09 us -> 7.03 us  [body(): inverse = call(invert_second, f32(B, B), 9)(ai, t, schur)]
    unnamed x22 -> x20, local copies, waits for them, and re-layouts: 6.27 us -> 5.12 us
  transfers between devices with their start and end apart: 22 -> 22, of which waited for: 8 -> 8; matrix products, arithmetic and copies ran while one was open for 0% -> 1% of each run, Pallas kernels for 20% -> 19%
where the time goes in v5:
time: 186 us; the launch traced here: 185 us
  starting transfers between devices  61.6 us (33%)
  Pallas kernels  53.4 us (29%)
  waiting for transfers between devices  35.4 us (19%)
  blocking collectives  25.6 us (14%)
  local copies, waits for them, and re-layouts  6.45 us (3%)
  other arithmetic  2.09 us (1%)
    all_to_all x5, starting transfers between devices, exchange(): return lax.all_to_all(blocks, axes, 0, 0, tiled=True)  31.4 us
    all_to_all x5, waiting for transfers between devices, exchange(): return lax.all_to_all(blocks, axes, 0, 0, tiled=True)  26.8 us
    all_to_all x1, blocking collectives, exchange(): return lax.all_to_all(blocks, axes, 0, 0, tiled=True)  25.6 us
    ppermute x7, starting transfers between devices, body(): parts.append(lax.ppermute(columns[k * 128:(k + 1) * 128], COL, [(0, k)]))  16.3 us
    pallas_call x1, Pallas kernels, body(): call(update_kernel, f32(1024, 2048), 12, 60, grid_spec=pltpu.PrefetchScal...  14.9 us
    pallas_call x1, Pallas kernels, body(): call(product_kernel, (f32(8, 384, 128), f32(8, 384, 128)), 12, 60, grid_s...  10.4 us
    pallas_call x1, Pallas kernels, body(): inverse = call(invert_second, f32(B, B), 9)(ai, t, schur)  7.03 us
    pallas_call x1, Pallas kernels, body(): ai, t, schur = call(invert_first, (f32(128, 128),) * 3, 9)(gram)  6.99 us
  transfers between devices with their start and end apart: 22, of which 8 were waited for; matrix products, arithmetic and copies ran while one was open for 1% of the time, Pallas kernels for 19%

profile of v5, /device:TPU:1, one launch (start us, length us, event | category | flops | bytes accessed | tf_op | source)
XLA Modules:
  0.0 185.5 jit_solution(3004035694720727777)
XLA Ops:
  0.7 1.4 slice_select_fusion
  2.1 0.1 fusion
  2.2 8.5 %collective-permute-start.6 = (f32[128,256]{1,0:T(8,128)S(1)}, f32[128,256]{1,0:T(8,128)S(1)}, u32[]{:S(2)}, u32[]{:S(2)}) collective-permute-start(f32[128,256]{1,0:T(8,128)S(1)} %get-tuple-element.48), channel_id=1, source_target_pairs={{0,7},{8,15},{16,23},{24,31},{32,39},{40,47},{48,55},{56,63},{64,7... | collective-permute-start | bytes 393224 | tf_op jit(solution)/shard_map/ppermute | solution.py:300
  10.7 1.3 collective-permute-start.5
  12.0 1.3 collective-permute-start.4
  13.3 1.3 collective-permute-start.3
  14.6 1.3 collective-permute-start.2
  15.9 0.0 collective-permute-done.6.refs_7_
  16.0 1.3 collective-permute-start.1
  17.3 0.0 collective-permute-done.5.refs_6_
  17.3 1.3 collective-permute-start
  18.6 0.0 collective-permute-done.4.refs_5_
  18.6 0.0 collective-permute-done.3.refs_4_
  18.6 2.5 %collective-permute-done.2.refs_3_ = f32[128,256]{1,0:T(8,128)S(1)} collective-permute-done((f32[128,256]{1,0:T(8,128)S(1)}, f32[128,256]{1,0:T(8,128)S(1)}, u32[]{:S(2)}, u32[]{:S(2)}) %collective-permute-start.2) | collective-permute-done | bytes 131104 | tf_op jit(solution)/shard_map/ppermute | solution.py:300
  21.1 2.8 %collective-permute-done.1.refs_2_ = f32[128,256]{1,0:T(8,128)S(1)} collective-permute-done((f32[128,256]{1,0:T(8,128)S(1)}, f32[128,256]{1,0:T(8,128)S(1)}, u32[]{:S(2)}, u32[]{:S(2)}) %collective-permute-start.1) | collective-permute-done | bytes 131104 | tf_op jit(solution)/shard_map/ppermute | solution.py:300
  23.9 0.0 collective-permute-done.refs_1_
  23.9 1.0 shard_map.41
  24.9 3.6 %all-to-all-start = ((f32[8,128,256]{2,1,0:T(8,128)}), f32[8,128,256]{2,1,0:T(8,128)S(1)}, u32[]{:S(2)}, u32[]{:S(2)}) async-start(f32[8,128,256]{2,1,0:T(8,128)} %get-tuple-element.25), calls=%async_computation | async-start | bytes 2097152 | tf_op jit(solution)/shard_map/all_to_all | solution.py:256
  28.5 0.7 collective-permute-start.7
  29.2 0.0 collective-permute-done.7.block_ref
  29.2 13.3 %all-to-all-done = f32[8,128,256]{2,1,0:T(8,128)S(1)} async-done(((f32[8,128,256]{2,1,0:T(8,128)}), f32[8,128,256]{2,1,0:T(8,128)S(1)}, u32[]{:S(2)}, u32[]{:S(2)}) %all-to-all-start) | async-done | bytes 1048608 | tf_op jit(solution)/shard_map/all_to_all | solution.py:256
  42.5 2.3 %shard_map.42 = (f32[8,320,128]{2,1,0:T(8,128)}, bf16[512,1024]{1,0:T(8,128)(2,1)S(1)}) custom-call(f32[1024,256]{1,0:T(8,128)S(1)} %bitcast.9, f32[256,128]{1,0:T(8,128)S(1)} %collective-permute-done.7.block_ref), custom_call_target="tpu_custom_call" | custom-call | flops 2000000000 | bytes 1024 | tf_op jit(solution)/shard_map/pallas_call | solution.py:306
  44.8 1.0 copy-done.6
  45.8 10.4 %all-to-all-start.1 = ((f32[8,320,128]{2,1,0:T(8,128)}), f32[8,320,128]{2,1,0:T(8,128)S(1)}, u32[]{:S(2)}, u32[]{:S(2)}) async-start(f32[8,320,128]{2,1,0:T(8,128)} %get-tuple-element.30), calls=%async_computation.1 | async-start | bytes 2621440 | tf_op jit(solution)/shard_map/all_to_all | solution.py:256
  56.3 10.4 %shard_map.43 = (f32[8,384,128]{2,1,0:T(8,128)}, f32[8,384,128]{2,1,0:T(8,128)}) custom-call(s32[1]{0:T(128)} %bitcast.core_ref, bf16[512,1024]{1,0:T(8,128)(2,1)} %copy-done.6, f32[1024,2048]{1,0:T(8,128)} %matrix_ref.1, f32[1024,2048]{1,0:T(8,128)} %matrix_ref.1, f32[1024,1024]{1,0:T(8,128)} %vectors_ref.3), custom_call_target="tpu_custom_call" | custom-call | flops 12000000000 | bytes 1024 | tf_op jit(solution)/shard_map/pallas_call | solution.py:311
  66.7 6.5 %all-to-all-done.1.panel_ref.pmine_ref = f32[8,320,128]{2,1,0:T(8,128)S(1)} async-done(((f32[8,320,128]{2,1,0:T(8,128)}), f32[8,320,128]{2,1,0:T(8,128)S(1)}, u32[]{:S(2)}, u32[]{:S(2)}) %all-to-all-start.1) | async-done | bytes 1310752 | tf_op jit(solution)/shard_map/all_to_all | solution.py:256
  73.2 2.7 %collective-permute-start.8 = (f32[8,384,128]{2,1,0:T(8,128)}, f32[8,384,128]{2,1,0:T(8,128)S(1)}, u32[]{:S(2)}, u32[]{:S(2)}) collective-permute-start(f32[8,384,128]{2,1,0:T(8,128)} %get-tuple-element.32), channel_id=1, source_target_pairs={{0,8},{8,0},{1,9},{9,1},{2,10},{10,2},{3,11},{11,3},{4,12},{12,4},... | collective-permute-start | bytes 4718600 | tf_op jit(solution)/shard_map/ppermute | solution.py:260
  76.0 0.1 collective-permute-start.9
  76.1 2.8 %collective-permute-done.9.other_ref = f32[64,128]{1,0:T(8,128)S(1)} collective-permute-done((f32[64,128]{1,0:T(8,128)S(1)}, f32[64,128]{1,0:T(8,128)S(1)}, u32[]{:S(2)}, u32[]{:S(2)}) %collective-permute-start.9) | collective-permute-done | bytes 32800 | tf_op jit(solution)/shard_map/ppermute | solution.py:260
  78.9 0.3 collective-permute-done.8.got_ref
  79.3 1.4 copy-done.1
  80.7 0.2 shard_map.44
  80.8 25.6 %all_to_all.30.in_ref = f32[8,448,128]{2,1,0:T(8,128)S(1)} all-to-all(f32[8,448,128]{2,1,0:T(8,128)S(1)} %shard_map.44), channel_id=1, replica_groups=mesh['y'=4,'zl'=2,'co'=2,'x'=4,'zh'=2] {'y','zl'}, dimensions={0} | all-to-all | bytes 3670016 | tf_op jit(solution)/shard_map/all_to_all | solution.py:256
  106.5 0.1 shard_map.45
  106.6 0.7 collective-permute-start.10
  107.3 1.2 broadcast_in_dim.21
  108.5 6.7 %all-to-all-start.3 = ((f32[8,384,128]{2,1,0:T(8,128)}), f32[8,384,128]{2,1,0:T(8,128)S(1)}, u32[]{:S(2)}, u32[]{:S(2)}) async-start(f32[8,384,128]{2,1,0:T(8,128)} %broadcast_in_dim.21), calls=%async_computation.3 | async-start | bytes 3145728 | tf_op jit(solution)/shard_map/all_to_all | solution.py:256
  115.2 7.0 %shard_map.46 = (f32[128,128]{1,0:T(8,128)S(1)}, f32[128,128]{1,0:T(8,128)S(1)}, f32[128,128]{1,0:T(8,128)S(1)}) custom-call(f32[8,64,128]{2,1,0:T(8,128)S(1)} %get-tuple-element.36.gram_ref), custom_call_target="tpu_custom_call" | custom-call | flops 8999999488 | bytes 1024 | tf_op jit(solution)/shard_map/pallas_call | solution.py:338
  122.2 0.0 collective-permute-done.10
  122.2 0.5 collective-permute-start.13
  122.7 2.2 %collective-permute-start.12 = (f32[128,256]{1,0:T(8,128)S(1)}, f32[128,256]{1,0:T(8,128)S(1)}, u32[]{:S(2)}, u32[]{:S(2)}) collective-permute-start(f32[128,256]{1,0:T(8,128)S(1)} %collective-permute-done.10), channel_id=1, source_target_pairs={{4,0},{6,2},{0,4},{2,6},{5,1},{7,3},{1,5},{3,7},{12,8},{14,10},{8,... | collective-permute-start | bytes 393224 | tf_op jit(solution)/shard_map/ppermute | solution.py:264
  124.9 1.2 collective-permute-start.11
  126.1 7.0 %shard_map.47.inverse_ref = f32[256,256]{1,0:T(8,128)S(1)} custom-call(f32[128,128]{1,0:T(8,128)S(1)} %get-tuple-element.37.ai_ref, f32[128,128]{1,0:T(8,128)S(1)} %get-tuple-element.38.t_ref, f32[128,128]{1,0:T(8,128)S(1)} %get-tuple-element.39.schur_ref), custom_call_target="tpu_custom_call" | custom-call | flops 8999999488 | bytes 1024 | tf_op jit(solution)/shard_map/pallas_call | solution.py:339
  133.1 0.0 collective-permute-done.13
  133.2 1.4 shard_map.48
  134.7 0.8 copy-done.5
  135.5 1.2 copy-done.7
  136.7 0.0 all-to-all-done.3.product_ref.mine_ref
  136.7 2.9 %collective-permute-start.15 = (f32[8,384,128]{2,1,0:T(8,128)S(1)}, f32[8,384,128]{2,1,0:T(8,128)}, u32[]{:S(2)}, u32[]{:S(2)}) collective-permute-start(f32[8,384,128]{2,1,0:T(8,128)S(1)} %all-to-all-done.3.product_ref.mine_ref), channel_id=1, source_target_pairs={{0,8},{8,0},{1,9},{9,1},{2,10},{10,2},{3,11},{11,3},{4,12},{12,4},... | collective-permute-start | bytes 4718600 | tf_op jit(solution)/shard_map/ppermute | solution.py:260
  139.6 0.1 collective-permute-start.16
  139.7 1.3 shard_map.49
  141.1 6.3 %all-to-all-start.4 = ((f32[16,16,256]{2,1,0:T(8,128)}), f32[16,16,256]{2,1,0:T(8,128)S(1)}, u32[]{:S(2)}, u32[]{:S(2)}) async-start(f32[16,16,256]{2,1,0:T(8,128)} %shard_map.49), calls=%async_computation.4 | async-start | bytes 524288 | tf_op jit(solution)/shard_map/all_to_all | solution.py:256
  147.3 0.6 pad_add_fusion.where_ref
  147.9 2.9 %collective-permute-start.14 = (f32[4,128,256]{2,1,0:T(8,128)}, f32[4,128,256]{2,1,0:T(8,128)}, u32[]{:S(2)}, u32[]{:S(2)}) collective-permute-start(f32[4,128,256]{2,1,0:T(8,128)} %copy-done.5), channel_id=1, source_target_pairs={{0,1},{1,0},{2,3},{3,2},{4,5},{5,4},{6,7},{7,6},{8,9},{9,8},{10,11... | collective-permute-start | bytes 1572872 | tf_op jit(solution)/shard_map/ppermute | solution.py:345
  150.8 5.2 %all-to-all-done.4.in_ref = f32[16,16,256]{2,1,0:T(8,128)S(1)} async-done(((f32[16,16,256]{2,1,0:T(8,128)}), f32[16,16,256]{2,1,0:T(8,128)S(1)}, u32[]{:S(2)}, u32[]{:S(2)}) %all-to-all-start.4) | async-done | bytes 262176 | tf_op jit(solution)/shard_map/all_to_all | solution.py:256
  156.0 0.7 shard_map.50
  156.7 4.5 %all-to-all-start.5 = ((f32[16,16,256]{2,1,0:T(8,128)}), f32[16,16,256]{2,1,0:T(8,128)S(1)}, u32[]{:S(2)}, u32[]{:S(2)}) async-start(f32[16,16,256]{2,1,0:T(8,128)} %shard_map.50), calls=%async_computation.5 | async-start | bytes 524288 | tf_op jit(solution)/shard_map/all_to_all | solution.py:256
  161.2 0.0 collective-permute-done.15.other_ref
  161.2 6.8 %shard_map.51 = f32[1024,1024]{1,0:T(8,128)} custom-call(s32[1]{0:T(128)} %bitcast.core_ref, bf16[1024,768]{1,0:T(8,128)(2,1)} %copy-done.7, f32[8,384,128]{2,1,0:T(8,128)} %copy-done.2, f32[8,384,128]{2,1,0:T(8,128)} %collective-permute-done.15.other_ref, f32[1024,1024]{1,0:T(8,128)} %vectors_ref.3), custom_call_target="tpu_custom_call" | custom-call | flops 6000000000 | bytes 1024 | tf_op jit(solution)/shard_map/pallas_call | solution.py:359
  168.0 1.8 all-to-all-done.5.coupling_ref
  169.8 0.0 collective-permute-done.16.pother_ref
  169.8 0.0 collective-permute-done.14.far_ref
  169.9 0.7 copy-done.9
  170.5 14.9 %shard_map.52 = f32[1024,2048]{1,0:T(8,128)} custom-call(s32[3]{0:T(128)} %pad_add_fusion.where_ref, bf16[1024,768]{1,0:T(8,128)(2,1)} %copy-done.7, f32[4,128,256]{2,1,0:T(8,128)} %copy-done.5, f32[4,128,256]{2,1,0:T(8,128)} %collective-permute-done.14.far_ref, f32[256,256]{1,0:T(8,128)} %copy-done.8, f32[16,16,256]{2,1,0:T(8,128)} %copy-done.9, ...), custom_call_target="tpu_custom_call" | custom-call | flops 12000000000 | bytes 1024 | tf_op jit(solution)/shard_map/pallas_call | solution.py:373
  (20 shorter events, 0.1 us)
Async XLA Ops:
  2.2 13.8 %collective-permute-start.6 = (f32[128,256]{1,0:T(8,128)S(1)}, f32[128,256]{1,0:T(8,128)S(1)}, u32[]{:S(2)}, u32[]{:S(2)}) collective-permute-start(f32[128,256]{1,0:T(8,128)S(1)} %get-tuple-element.48), channel_id=1, source_target_pairs={{0,7},{8,15},{16,23},{24,31},{32,39},{40,47},{48,55},{56,63},{64,7... | collective-permute-start | bytes 393224 | tf_op jit(solution)/shard_map/ppermute | solution.py:300
  10.7 6.5 %collective-permute-start.5 = (f32[128,256]{1,0:T(8,128)S(1)}, f32[128,256]{1,0:T(8,128)S(1)}, u32[]{:S(2)}, u32[]{:S(2)}) collective-permute-start(f32[128,256]{1,0:T(8,128)S(1)} %get-tuple-element.49), channel_id=1, source_target_pairs={{0,6},{8,14},{16,22},{24,30},{32,38},{40,46},{48,54},{56,62},{64,7... | collective-permute-start | bytes 393224 | tf_op jit(solution)/shard_map/ppermute | solution.py:300
  12.0 6.6 %collective-permute-start.4 = (f32[128,256]{1,0:T(8,128)S(1)}, f32[128,256]{1,0:T(8,128)S(1)}, u32[]{:S(2)}, u32[]{:S(2)}) collective-permute-start(f32[128,256]{1,0:T(8,128)S(1)} %get-tuple-element.50), channel_id=1, source_target_pairs={{0,5},{8,13},{16,21},{24,29},{32,37},{40,45},{48,53},{56,61},{64,6... | collective-permute-start | bytes 393224 | tf_op jit(solution)/shard_map/ppermute | solution.py:300
  13.3 5.3 %collective-permute-start.3 = (f32[128,256]{1,0:T(8,128)S(1)}, f32[128,256]{1,0:T(8,128)S(1)}, u32[]{:S(2)}, u32[]{:S(2)}) collective-permute-start(f32[128,256]{1,0:T(8,128)S(1)} %get-tuple-element.51), channel_id=1, source_target_pairs={{0,4},{8,12},{16,20},{24,28},{32,36},{40,44},{48,52},{56,60},{64,6... | collective-permute-start | bytes 393224 | tf_op jit(solution)/shard_map/ppermute | solution.py:300
  14.6 6.5 %collective-permute-start.2 = (f32[128,256]{1,0:T(8,128)S(1)}, f32[128,256]{1,0:T(8,128)S(1)}, u32[]{:S(2)}, u32[]{:S(2)}) collective-permute-start(f32[128,256]{1,0:T(8,128)S(1)} %get-tuple-element.52), channel_id=1, source_target_pairs={{0,3},{8,11},{16,19},{24,27},{32,35},{40,43},{48,51},{56,59},{64,6... | collective-permute-start | bytes 393224 | tf_op jit(solution)/shard_map/ppermute | solution.py:300
  16.0 7.9 %collective-permute-start.1 = (f32[128,256]{1,0:T(8,128)S(1)}, f32[128,256]{1,0:T(8,128)S(1)}, u32[]{:S(2)}, u32[]{:S(2)}) collective-permute-start(f32[128,256]{1,0:T(8,128)S(1)} %get-tuple-element.53), channel_id=1, source_target_pairs={{0,2},{8,10},{16,18},{24,26},{32,34},{40,42},{48,50},{56,58},{64,6... | collective-permute-start | bytes 393224 | tf_op jit(solution)/shard_map/ppermute | solution.py:300
  17.3 6.6 %collective-permute-start = (f32[128,256]{1,0:T(8,128)S(1)}, f32[128,256]{1,0:T(8,128)S(1)}, u32[]{:S(2)}, u32[]{:S(2)}) collective-permute-start(f32[128,256]{1,0:T(8,128)S(1)} %get-tuple-element.54), channel_id=1, source_target_pairs={{0,1},{8,9},{16,17},{24,25},{32,33},{40,41},{48,49},{56,57},{64,65... | collective-permute-start | bytes 393224 | tf_op jit(solution)/shard_map/ppermute | solution.py:300
  24.9 17.5 %all-to-all-start = ((f32[8,128,256]{2,1,0:T(8,128)}), f32[8,128,256]{2,1,0:T(8,128)S(1)}, u32[]{:S(2)}, u32[]{:S(2)}) async-start(f32[8,128,256]{2,1,0:T(8,128)} %get-tuple-element.25), calls=%async_computation | async-start | bytes 2097152 | tf_op jit(solution)/shard_map/all_to_all | solution.py:256
  28.5 0.7 collective-permute-start.7
  42.5 2.3 %copy-start.3 = (f32[8,128,256]{2,1,0:T(8,128)}, f32[8,128,256]{2,1,0:T(8,128)S(1)}, u32[]{:S(2)}) copy-start(f32[8,128,256]{2,1,0:T(8,128)S(1)} %all-to-all-done) | copy-start | bytes 3145732
  44.8 1.0 copy-start.6
  45.8 27.4 %all-to-all-start.1 = ((f32[8,320,128]{2,1,0:T(8,128)}), f32[8,320,128]{2,1,0:T(8,128)S(1)}, u32[]{:S(2)}, u32[]{:S(2)}) async-start(f32[8,320,128]{2,1,0:T(8,128)} %get-tuple-element.30), calls=%async_computation.1 | async-start | bytes 2621440 | tf_op jit(solution)/shard_map/all_to_all | solution.py:256
  73.2 66.5 %copy-start = (f32[8,320,128]{2,1,0:T(8,128)}, f32[8,320,128]{2,1,0:T(8,128)S(1)}, u32[]{:S(2)}) copy-start(f32[8,320,128]{2,1,0:T(8,128)S(1)} %all-to-all-done.1.panel_ref.pmine_ref) | copy-start | bytes 3932164
  73.2 6.0 %collective-permute-start.8 = (f32[8,384,128]{2,1,0:T(8,128)}, f32[8,384,128]{2,1,0:T(8,128)S(1)}, u32[]{:S(2)}, u32[]{:S(2)}) collective-permute-start(f32[8,384,128]{2,1,0:T(8,128)} %get-tuple-element.32), channel_id=1, source_target_pairs={{0,8},{8,0},{1,9},{9,1},{2,10},{10,2},{3,11},{11,3},{4,12},{12,4},... | collective-permute-start | bytes 4718600 | tf_op jit(solution)/shard_map/ppermute | solution.py:260
  76.0 2.9 %collective-permute-start.9 = (f32[64,128]{1,0:T(8,128)S(1)}, f32[64,128]{1,0:T(8,128)S(1)}, u32[]{:S(2)}, u32[]{:S(2)}) collective-permute-start(f32[64,128]{1,0:T(8,128)S(1)} %slice_reduce_fusion.gram_ref), channel_id=1, source_target_pairs={{0,8},{8,0},{1,9},{9,1},{2,10},{10,2},{3,11},{11,3},{4,12},{12,4},... | collective-permute-start | bytes 98312 | tf_op jit(solution)/shard_map/ppermute | solution.py:260
  79.3 1.4 copy-start.1
  106.6 15.6 %collective-permute-start.10 = (f32[128,256]{1,0:T(8,128)S(1)}, f32[128,256]{1,0:T(8,128)S(1)}, u32[]{:S(2)}, u32[]{:S(2)}) collective-permute-start(f32[128,256]{1,0:T(8,128)S(1)} %get-tuple-element.35), channel_id=1, source_target_pairs={{0,0},{16,1},{32,2},{48,3},{64,4},{80,5},{96,6},{112,7},{8,8},{24,... | collective-permute-start | bytes 393224 | tf_op jit(solution)/shard_map/ppermute | solution.py:337
  108.5 28.2 %all-to-all-start.3 = ((f32[8,384,128]{2,1,0:T(8,128)}), f32[8,384,128]{2,1,0:T(8,128)S(1)}, u32[]{:S(2)}, u32[]{:S(2)}) async-start(f32[8,384,128]{2,1,0:T(8,128)} %broadcast_in_dim.21), calls=%async_computation.3 | async-start | bytes 3145728 | tf_op jit(solution)/shard_map/all_to_all | solution.py:256
  122.2 10.9 %collective-permute-start.13 = (f32[128,256]{1,0:T(8,128)S(1)}, f32[128,256]{1,0:T(8,128)S(1)}, u32[]{:S(2)}, u32[]{:S(2)}) collective-permute-start(f32[128,256]{1,0:T(8,128)S(1)} %collective-permute-done.10), channel_id=1, source_target_pairs={{6,0},{0,2},{2,4},{4,6},{7,1},{1,3},{3,5},{5,7},{14,8},{8,10},{10,... | collective-permute-start | bytes 393224 | tf_op jit(solution)/shard_map/ppermute | solution.py:264
  122.7 10.5 %collective-permute-start.12 = (f32[128,256]{1,0:T(8,128)S(1)}, f32[128,256]{1,0:T(8,128)S(1)}, u32[]{:S(2)}, u32[]{:S(2)}) collective-permute-start(f32[128,256]{1,0:T(8,128)S(1)} %collective-permute-done.10), channel_id=1, source_target_pairs={{4,0},{6,2},{0,4},{2,6},{5,1},{7,3},{1,5},{3,7},{12,8},{14,10},{8,... | collective-permute-start | bytes 393224 | tf_op jit(solution)/shard_map/ppermute | solution.py:264
  124.9 8.3 %collective-permute-start.11 = (f32[128,256]{1,0:T(8,128)S(1)}, f32[128,256]{1,0:T(8,128)S(1)}, u32[]{:S(2)}, u32[]{:S(2)}) collective-permute-start(f32[128,256]{1,0:T(8,128)S(1)} %collective-permute-done.10), channel_id=1, source_target_pairs={{2,0},{4,2},{6,4},{0,6},{3,1},{5,3},{7,5},{1,7},{10,8},{12,10},{14... | collective-permute-start | bytes 393224 | tf_op jit(solution)/shard_map/ppermute | solution.py:264
  126.1 7.1 %copy-start.4 = (f32[8,128,256]{2,1,0:T(8,128)S(1)}, f32[8,128,256]{2,1,0:T(8,128)}, u32[]{:S(2)}) copy-start(f32[8,128,256]{2,1,0:T(8,128)} %copy-done.3) | copy-start | bytes 3145732
  133.1 1.5 copy-start.8
  134.7 0.8 copy-start.5
  135.5 1.2 copy-start.7
  136.7 4.3 %copy-start.2 = (f32[8,384,128]{2,1,0:T(8,128)}, f32[8,384,128]{2,1,0:T(8,128)S(1)}, u32[]{:S(2)}) copy-start(f32[8,384,128]{2,1,0:T(8,128)S(1)} %all-to-all-done.3.product_ref.mine_ref) | copy-start | bytes 4718596
  136.7 24.5 %collective-permute-start.15 = (f32[8,384,128]{2,1,0:T(8,128)S(1)}, f32[8,384,128]{2,1,0:T(8,128)}, u32[]{:S(2)}, u32[]{:S(2)}) collective-permute-start(f32[8,384,128]{2,1,0:T(8,128)S(1)} %all-to-all-done.3.product_ref.mine_ref), channel_id=1, source_target_pairs={{0,8},{8,0},{1,9},{9,1},{2,10},{10,2},{3,11},{11,3},{4,12},{12,4},... | collective-permute-start | bytes 4718600 | tf_op jit(solution)/shard_map/ppermute | solution.py:260
  139.6 30.2 %collective-permute-start.16 = (f32[8,320,128]{2,1,0:T(8,128)S(1)}, f32[8,320,128]{2,1,0:T(8,128)}, u32[]{:S(2)}, u32[]{:S(2)}) collective-permute-start(f32[8,320,128]{2,1,0:T(8,128)S(1)} %all-to-all-done.1.panel_ref.pmine_ref), channel_id=1, source_target_pairs={{0,8},{8,0},{1,9},{9,1},{2,10},{10,2},{3,11},{11,3},{4,12},{12,4},... | collective-permute-start | bytes 3932168 | tf_op jit(solution)/shard_map/ppermute | solution.py:260
  141.1 14.9 %all-to-all-start.4 = ((f32[16,16,256]{2,1,0:T(8,128)}), f32[16,16,256]{2,1,0:T(8,128)S(1)}, u32[]{:S(2)}, u32[]{:S(2)}) async-start(f32[16,16,256]{2,1,0:T(8,128)} %shard_map.49), calls=%async_computation.4 | async-start | bytes 524288 | tf_op jit(solution)/shard_map/all_to_all | solution.py:256
  147.9 21.9 %collective-permute-start.14 = (f32[4,128,256]{2,1,0:T(8,128)}, f32[4,128,256]{2,1,0:T(8,128)}, u32[]{:S(2)}, u32[]{:S(2)}) collective-permute-start(f32[4,128,256]{2,1,0:T(8,128)} %copy-done.5), channel_id=1, source_target_pairs={{0,1},{1,0},{2,3},{3,2},{4,5},{5,4},{6,7},{7,6},{8,9},{9,8},{10,11... | collective-permute-start | bytes 1572872 | tf_op jit(solution)/shard_map/ppermute | solution.py:345
  156.7 13.1 %all-to-all-start.5 = ((f32[16,16,256]{2,1,0:T(8,128)}), f32[16,16,256]{2,1,0:T(8,128)S(1)}, u32[]{:S(2)}, u32[]{:S(2)}) async-start(f32[16,16,256]{2,1,0:T(8,128)} %shard_map.50), calls=%async_computation.5 | async-start | bytes 524288 | tf_op jit(solution)/shard_map/all_to_all | solution.py:256
  169.8 0.7 copy-start.9

commit v6 on v5

--- a/solution.py
+++ b/solution.py
@@ -210,7 +210,8 @@
         out_ref[k] = 2.0 * dot(product_ref[k], inverse)
 
 
-def rotate_kernel(core_ref, left_ref, mine_ref, other_ref, vectors_ref, out_ref):
+def rotate_kernel(core_ref, left_ref, mine_ref, other_ref, vectors_ref, *out):
+    out_ref = out[-1]
     core = core_ref[0]
     mine, other = mine_ref[...], other_ref[...]
     both = jnp.where(core == 0, mine, other), jnp.where(core == 0, other, mine)
@@ -282,6 +283,21 @@
 
 def fixed(*shape):
     return pl.BlockSpec(shape, lambda t, w: (0,) * len(shape))
+
+
+def rotate(at, core, first, final, other, vectors, *done):
+    mixing = pl.BlockSpec((8, 32, 128), lambda t: (0, 8 + at + t, 0))
+    tile = pl.BlockSpec((1024, 256), lambda t: (0, at + t))
+    return call(
+        rotate_kernel,
+        f32(1024, 1024),
+        3,
+        60,
+        grid=(2,),
+        in_specs=[SMEM, whole(1024, 768), mixing, mixing, tile] + [pl.BlockSpec(memory_space=pl.ANY)] * len(done),
+        out_specs=tile,
+        input_output_aliases={5: 0} if done else {},
+    )(core, first, final, other, vectors, *done)
 
 
 def body(matrix, vectors):
@@ -354,17 +370,10 @@
         ],
         out_specs=whole(16, 16, 256),
     )(panel, final)
-    coupling = exchange(call(sum_kernel, f32(16, 16, 256), 1)(exchange(coupling, COUPLED)), COUPLED)
-    mixing = pl.BlockSpec((8, 32, 128), lambda t: (0, 8 + t, 0))
-    rotated = call(
-        rotate_kernel,
-        f32(1024, 1024),
-        6,
-        60,
-        grid=(4,),
-        in_specs=[SMEM, whole(1024, 768), mixing, mixing, pl.BlockSpec((1024, 256), lambda t: (0, t))],
-        out_specs=pl.BlockSpec((1024, 256), lambda t: (0, t)),
-    )(core, first, final, other, vectors)
+    rotated = rotate(0, core, first, final, other, vectors)
+    coupling, rotated = lax.optimization_barrier((exchange(coupling, COUPLED), rotated))
+    coupling = exchange(call(sum_kernel, f32(16, 16, 256), 1)(coupling), COUPLED)
+    rotated = rotate(2, core, first, final, other, vectors, rotated)
     coupling, rotated = lax.optimization_barrier((coupling, rotated))
 
     mine = pl.BlockSpec((4, 256, 128), lambda t, w: (jnp.clip(t - 2 * w[0], 0, 1), 0, 0))

time: 186 us -> 187 us (level)
    pallas_call x2 -> x3, Pallas kernels: 7.57 us -> 8.92 us  [the longest x2 8.17 us: rotate(): call(rotate_kernel, f32(1024, 1024), 3, 60, grid=(2,), in_specs=[SMEM, wh...]
where the time goes in v6:
time: 187 us; the launch traced here: 186 us
  starting transfers between devices  61.6 us (33%)
  Pallas kernels  54.7 us (29%)
  waiting for transfers between devices  34.6 us (19%)
  blocking collectives  25.6 us (14%)
  local copies, waits for them, and re-layouts  6.45 us (3%)
  other arithmetic  2.09 us (1%)
    all_to_all x5, starting transfers between devices, exchange(): return lax.all_to_all(blocks, axes, 0, 0, tiled=True)  31.4 us
    all_to_all x5, waiting for transfers between devices, exchange(): return lax.all_to_all(blocks, axes, 0, 0, tiled=True)  26.1 us
    all_to_all x1, blocking collectives, exchange(): return lax.all_to_all(blocks, axes, 0, 0, tiled=True)  25.6 us
    ppermute x7, starting transfers between devices, body(): parts.append(lax.ppermute(columns[k * 128:(k + 1) * 128], COL, [(0, k)]))  16.3 us
    pallas_call x1, Pallas kernels, body(): call(update_kernel, f32(1024, 2048), 12, 60, grid_spec=pltpu.PrefetchScal...  14.9 us
    pallas_call x1, Pallas kernels, body(): call(product_kernel, (f32(8, 384, 128), f32(8, 384, 128)), 12, 60, grid_s...  10.4 us
    pallas_call x2, Pallas kernels, rotate(): call(rotate_kernel, f32(1024, 1024), 3, 60, grid=(2,), in_specs=[SMEM, wh...  8.17 us
    pallas_call x1, Pallas kernels, body(): inverse = call(invert_second, f32(B, B), 9)(ai, t, schur)  7.03 us
  transfers between devices with their start and end apart: 22, of which 8 were waited for; matrix products, arithmetic and copies ran while one was open for 1% of the time, Pallas kernels for 19%

profile of v6, /device:TPU:1, one launch (start us, length us, event | category | flops | bytes accessed | tf_op | source)
XLA Modules:
  0.0 186.1 jit_solution(4243763482869489273)
XLA Ops:
  0.7 1.4 slice_select_fusion
  2.1 0.1 fusion
  2.2 8.5 %collective-permute-start.6 = (f32[128,256]{1,0:T(8,128)S(1)}, f32[128,256]{1,0:T(8,128)S(1)}, u32[]{:S(2)}, u32[]{:S(2)}) collective-permute-start(f32[128,256]{1,0:T(8,128)S(1)} %get-tuple-element.52), channel_id=1, source_target_pairs={{0,7},{8,15},{16,23},{24,31},{32,39},{40,47},{48,55},{56,63},{64,7... | collective-permute-start | bytes 393224 | tf_op jit(solution)/shard_map/ppermute | solution.py:316
  10.7 1.3 collective-permute-start.5
  12.0 1.3 collective-permute-start.4
  13.3 1.3 collective-permute-start.3
  14.6 1.3 collective-permute-start.2
  15.9 0.0 collective-permute-done.6.refs_7_
  16.0 1.3 collective-permute-start.1
  17.3 0.0 collective-permute-done.5.refs_6_
  17.3 1.3 collective-permute-start
  18.6 0.0 collective-permute-done.4.refs_5_
  18.6 0.0 collective-permute-done.3.refs_4_
  18.6 2.5 %collective-permute-done.2.refs_3_ = f32[128,256]{1,0:T(8,128)S(1)} collective-permute-done((f32[128,256]{1,0:T(8,128)S(1)}, f32[128,256]{1,0:T(8,128)S(1)}, u32[]{:S(2)}, u32[]{:S(2)}) %collective-permute-start.2) | collective-permute-done | bytes 131104 | tf_op jit(solution)/shard_map/ppermute | solution.py:316
  21.1 2.8 %collective-permute-done.1.refs_2_ = f32[128,256]{1,0:T(8,128)S(1)} collective-permute-done((f32[128,256]{1,0:T(8,128)S(1)}, f32[128,256]{1,0:T(8,128)S(1)}, u32[]{:S(2)}, u32[]{:S(2)}) %collective-permute-start.1) | collective-permute-done | bytes 131104 | tf_op jit(solution)/shard_map/ppermute | solution.py:316
  23.9 0.0 collective-permute-done.refs_1_
  23.9 1.0 shard_map.41
  24.9 3.6 %all-to-all-start = ((f32[8,128,256]{2,1,0:T(8,128)}), f32[8,128,256]{2,1,0:T(8,128)S(1)}, u32[]{:S(2)}, u32[]{:S(2)}) async-start(f32[8,128,256]{2,1,0:T(8,128)} %get-tuple-element.27), calls=%async_computation | async-start | bytes 2097152 | tf_op jit(solution)/shard_map/all_to_all | solution.py:257
  28.5 0.7 collective-permute-start.7
  29.2 0.0 collective-permute-done.7.block_ref
  29.2 13.3 %all-to-all-done = f32[8,128,256]{2,1,0:T(8,128)S(1)} async-done(((f32[8,128,256]{2,1,0:T(8,128)}), f32[8,128,256]{2,1,0:T(8,128)S(1)}, u32[]{:S(2)}, u32[]{:S(2)}) %all-to-all-start) | async-done | bytes 1048608 | tf_op jit(solution)/shard_map/all_to_all | solution.py:257
  42.5 2.3 %shard_map.42 = (f32[8,320,128]{2,1,0:T(8,128)}, bf16[512,1024]{1,0:T(8,128)(2,1)S(1)}) custom-call(f32[1024,256]{1,0:T(8,128)S(1)} %bitcast.9, f32[256,128]{1,0:T(8,128)S(1)} %collective-permute-done.7.block_ref), custom_call_target="tpu_custom_call" | custom-call | flops 2000000000 | bytes 1024 | tf_op jit(solution)/shard_map/pallas_call | solution.py:322
  44.8 1.0 copy-done.7
  45.8 10.4 %all-to-all-start.1 = ((f32[8,320,128]{2,1,0:T(8,128)}), f32[8,320,128]{2,1,0:T(8,128)S(1)}, u32[]{:S(2)}, u32[]{:S(2)}) async-start(f32[8,320,128]{2,1,0:T(8,128)} %get-tuple-element.32), calls=%async_computation.1 | async-start | bytes 2621440 | tf_op jit(solution)/shard_map/all_to_all | solution.py:257
  56.3 10.4 %shard_map.43 = (f32[8,384,128]{2,1,0:T(8,128)}, f32[8,384,128]{2,1,0:T(8,128)}) custom-call(s32[1]{0:T(128)} %bitcast.core_ref, bf16[512,1024]{1,0:T(8,128)(2,1)} %copy-done.7, f32[1024,2048]{1,0:T(8,128)} %matrix_ref.1, f32[1024,2048]{1,0:T(8,128)} %matrix_ref.1, f32[1024,1024]{1,0:T(8,128)} %vectors_ref.5), custom_call_target="tpu_custom_call" | custom-call | flops 12000000000 | bytes 1024 | tf_op jit(solution)/shard_map/pallas_call | solution.py:327
  66.7 6.5 %all-to-all-done.1.panel_ref.pmine_ref = f32[8,320,128]{2,1,0:T(8,128)S(1)} async-done(((f32[8,320,128]{2,1,0:T(8,128)}), f32[8,320,128]{2,1,0:T(8,128)S(1)}, u32[]{:S(2)}, u32[]{:S(2)}) %all-to-all-start.1) | async-done | bytes 1310752 | tf_op jit(solution)/shard_map/all_to_all | solution.py:257
  73.2 2.7 %collective-permute-start.8 = (f32[8,384,128]{2,1,0:T(8,128)}, f32[8,384,128]{2,1,0:T(8,128)S(1)}, u32[]{:S(2)}, u32[]{:S(2)}) collective-permute-start(f32[8,384,128]{2,1,0:T(8,128)} %get-tuple-element.34), channel_id=1, source_target_pairs={{0,8},{8,0},{1,9},{9,1},{2,10},{10,2},{3,11},{11,3},{4,12},{12,4},... | collective-permute-start | bytes 4718600 | tf_op jit(solution)/shard_map/ppermute | solution.py:261
  76.0 0.1 collective-permute-start.9
  76.1 2.8 %collective-permute-done.9.other_ref = f32[64,128]{1,0:T(8,128)S(1)} collective-permute-done((f32[64,128]{1,0:T(8,128)S(1)}, f32[64,128]{1,0:T(8,128)S(1)}, u32[]{:S(2)}, u32[]{:S(2)}) %collective-permute-start.9) | collective-permute-done | bytes 32800 | tf_op jit(solution)/shard_map/ppermute | solution.py:261
  78.9 0.3 collective-permute-done.8.got_ref
  79.3 1.4 copy-done.3
  80.7 0.2 shard_map.44
  80.8 25.6 %all_to_all.30.in_ref = f32[8,448,128]{2,1,0:T(8,128)S(1)} all-to-all(f32[8,448,128]{2,1,0:T(8,128)S(1)} %shard_map.44), channel_id=1, replica_groups=mesh['y'=4,'zl'=2,'co'=2,'x'=4,'zh'=2] {'y','zl'}, dimensions={0} | all-to-all | bytes 3670016 | tf_op jit(solution)/shard_map/all_to_all | solution.py:257
  106.5 0.1 shard_map.45
  106.6 0.7 collective-permute-start.10
  107.3 1.2 broadcast_in_dim.21
  108.5 6.7 %all-to-all-start.3 = ((f32[8,384,128]{2,1,0:T(8,128)}), f32[8,384,128]{2,1,0:T(8,128)S(1)}, u32[]{:S(2)}, u32[]{:S(2)}) async-start(f32[8,384,128]{2,1,0:T(8,128)} %broadcast_in_dim.21), calls=%async_computation.3 | async-start | bytes 3145728 | tf_op jit(solution)/shard_map/all_to_all | solution.py:257
  115.2 7.0 %shard_map.46 = (f32[128,128]{1,0:T(8,128)S(1)}, f32[128,128]{1,0:T(8,128)S(1)}, f32[128,128]{1,0:T(8,128)S(1)}) custom-call(f32[8,64,128]{2,1,0:T(8,128)S(1)} %get-tuple-element.38.gram_ref), custom_call_target="tpu_custom_call" | custom-call | flops 8999999488 | bytes 1024 | tf_op jit(solution)/shard_map/pallas_call | solution.py:354
  122.2 0.0 collective-permute-done.10
  122.2 0.5 collective-permute-start.13
  122.7 2.2 %collective-permute-start.12 = (f32[128,256]{1,0:T(8,128)S(1)}, f32[128,256]{1,0:T(8,128)S(1)}, u32[]{:S(2)}, u32[]{:S(2)}) collective-permute-start(f32[128,256]{1,0:T(8,128)S(1)} %collective-permute-done.10), channel_id=1, source_target_pairs={{4,0},{6,2},{0,4},{2,6},{5,1},{7,3},{1,5},{3,7},{12,8},{14,10},{8,... | collective-permute-start | bytes 393224 | tf_op jit(solution)/shard_map/ppermute | solution.py:265
  124.9 1.2 collective-permute-start.11
  126.1 7.0 %shard_map.47.inverse_ref = f32[256,256]{1,0:T(8,128)S(1)} custom-call(f32[128,128]{1,0:T(8,128)S(1)} %get-tuple-element.39.ai_ref, f32[128,128]{1,0:T(8,128)S(1)} %get-tuple-element.40.t_ref, f32[128,128]{1,0:T(8,128)S(1)} %get-tuple-element.41.schur_ref), custom_call_target="tpu_custom_call" | custom-call | flops 8999999488 | bytes 1024 | tf_op jit(solution)/shard_map/pallas_call | solution.py:355
  133.1 0.0 collective-permute-done.13
  133.2 0.0 collective-permute-done.11
  133.2 1.4 shard_map.48
  134.7 1.2 copy-done.1
  135.9 0.8 copy-done.6
  136.7 2.9 %collective-permute-start.15 = (f32[8,384,128]{2,1,0:T(8,128)S(1)}, f32[8,384,128]{2,1,0:T(8,128)}, u32[]{:S(2)}, u32[]{:S(2)}) collective-permute-start(f32[8,384,128]{2,1,0:T(8,128)S(1)} %all-to-all-done.3.product_ref.mine_ref), channel_id=1, source_target_pairs={{0,8},{8,0},{1,9},{9,1},{2,10},{10,2},{3,11},{11,3},{4,12},{12,4},... | collective-permute-start | bytes 4718600 | tf_op jit(solution)/shard_map/ppermute | solution.py:261
  139.6 0.1 collective-permute-start.16
  139.7 0.6 pad_add_fusion.where_ref
  140.3 1.3 shard_map.49
  141.7 6.3 %all-to-all-start.4 = ((f32[16,16,256]{2,1,0:T(8,128)}), f32[16,16,256]{2,1,0:T(8,128)S(1)}, u32[]{:S(2)}, u32[]{:S(2)}) async-start(f32[16,16,256]{2,1,0:T(8,128)} %shard_map.49), calls=%async_computation.4 | async-start | bytes 524288 | tf_op jit(solution)/shard_map/all_to_all | solution.py:257
  147.9 2.9 %collective-permute-start.14 = (f32[4,128,256]{2,1,0:T(8,128)}, f32[4,128,256]{2,1,0:T(8,128)}, u32[]{:S(2)}, u32[]{:S(2)}) collective-permute-start(f32[4,128,256]{2,1,0:T(8,128)} %copy-done.6), channel_id=1, source_target_pairs={{0,1},{1,0},{2,3},{3,2},{4,5},{5,4},{6,7},{7,6},{8,9},{9,8},{10,11... | collective-permute-start | bytes 1572872 | tf_op jit(solution)/shard_map/ppermute | solution.py:361
  150.8 4.1 %shard_map.50.out_0_ = f32[1024,1024]{1,0:T(8,128)} custom-call(s32[1]{0:T(128)} %bitcast.core_ref, bf16[1024,768]{1,0:T(8,128)(2,1)} %copy-done.1, f32[8,384,128]{2,1,0:T(8,128)} %copy-done, f32[8,384,128]{2,1,0:T(8,128)} %collective-permute-done.15.other_ref, f32[1024,1024]{1,0:T(8,128)} %vectors_ref.5), custom_call_target="tpu_custom_call" | custom-call | flops 3000000000 | bytes 1024 | tf_op jit(solution)/shard_map/pallas_call | solution.py:291
  154.9 1.7 all-to-all-done.4.in_ref
  156.6 0.7 shard_map.51
  157.3 4.5 %all-to-all-start.5 = ((f32[16,16,256]{2,1,0:T(8,128)}), f32[16,16,256]{2,1,0:T(8,128)S(1)}, u32[]{:S(2)}, u32[]{:S(2)}) async-start(f32[16,16,256]{2,1,0:T(8,128)} %shard_map.51), calls=%async_computation.5 | async-start | bytes 524288 | tf_op jit(solution)/shard_map/all_to_all | solution.py:257
  161.8 4.1 %shard_map.52 = f32[1024,1024]{1,0:T(8,128)} custom-call(s32[1]{0:T(128)} %bitcast.core_ref, bf16[1024,768]{1,0:T(8,128)(2,1)} %copy-done.1, f32[8,384,128]{2,1,0:T(8,128)} %copy-done, f32[8,384,128]{2,1,0:T(8,128)} %collective-permute-done.15.other_ref, f32[1024,1024]{1,0:T(8,128)} %vectors_ref.5, ...), custom_call_target="tpu_custom_call", output_to_operand_aliasing={{}: (5, {})} | custom-call | flops 3000000000 | bytes 1024 | tf_op jit(solution)/shard_map/pallas_call | solution.py:291
  165.9 4.5 %all-to-all-done.5.coupling_ref = f32[16,16,256]{2,1,0:T(8,128)S(1)} async-done(((f32[16,16,256]{2,1,0:T(8,128)}), f32[16,16,256]{2,1,0:T(8,128)S(1)}, u32[]{:S(2)}, u32[]{:S(2)}) %all-to-all-start.5) | async-done | bytes 262176 | tf_op jit(solution)/shard_map/all_to_all | solution.py:257
  170.4 0.0 collective-permute-done.16.pother_ref
  170.4 0.0 collective-permute-done.14.far_ref
  170.5 0.7 copy-done.9
  171.1 14.9 %shard_map.53 = f32[1024,2048]{1,0:T(8,128)} custom-call(s32[3]{0:T(128)} %pad_add_fusion.where_ref, bf16[1024,768]{1,0:T(8,128)(2,1)} %copy-done.1, f32[4,128,256]{2,1,0:T(8,128)} %copy-done.6, f32[4,128,256]{2,1,0:T(8,128)} %collective-permute-done.14.far_ref, f32[256,256]{1,0:T(8,128)} %copy-done.8, f32[16,16,256]{2,1,0:T(8,128)} %copy-done.9, ...), custom_call_target="tpu_custom_call" | custom-call | flops 12000000000 | bytes 1024 | tf_op jit(solution)/shard_map/pallas_call | solution.py:382
  (21 shorter events, 0.1 us)
Async XLA Ops:
  2.2 13.8 %collective-permute-start.6 = (f32[128,256]{1,0:T(8,128)S(1)}, f32[128,256]{1,0:T(8,128)S(1)}, u32[]{:S(2)}, u32[]{:S(2)}) collective-permute-start(f32[128,256]{1,0:T(8,128)S(1)} %get-tuple-element.52), channel_id=1, source_target_pairs={{0,7},{8,15},{16,23},{24,31},{32,39},{40,47},{48,55},{56,63},{64,7... | collective-permute-start | bytes 393224 | tf_op jit(solution)/shard_map/ppermute | solution.py:316
  10.7 6.5 %collective-permute-start.5 = (f32[128,256]{1,0:T(8,128)S(1)}, f32[128,256]{1,0:T(8,128)S(1)}, u32[]{:S(2)}, u32[]{:S(2)}) collective-permute-start(f32[128,256]{1,0:T(8,128)S(1)} %get-tuple-element.53), channel_id=1, source_target_pairs={{0,6},{8,14},{16,22},{24,30},{32,38},{40,46},{48,54},{56,62},{64,7... | collective-permute-start | bytes 393224 | tf_op jit(solution)/shard_map/ppermute | solution.py:316
  12.0 6.6 %collective-permute-start.4 = (f32[128,256]{1,0:T(8,128)S(1)}, f32[128,256]{1,0:T(8,128)S(1)}, u32[]{:S(2)}, u32[]{:S(2)}) collective-permute-start(f32[128,256]{1,0:T(8,128)S(1)} %get-tuple-element.54), channel_id=1, source_target_pairs={{0,5},{8,13},{16,21},{24,29},{32,37},{40,45},{48,53},{56,61},{64,6... | collective-permute-start | bytes 393224 | tf_op jit(solution)/shard_map/ppermute | solution.py:316
  13.3 5.3 %collective-permute-start.3 = (f32[128,256]{1,0:T(8,128)S(1)}, f32[128,256]{1,0:T(8,128)S(1)}, u32[]{:S(2)}, u32[]{:S(2)}) collective-permute-start(f32[128,256]{1,0:T(8,128)S(1)} %get-tuple-element.55), channel_id=1, source_target_pairs={{0,4},{8,12},{16,20},{24,28},{32,36},{40,44},{48,52},{56,60},{64,6... | collective-permute-start | bytes 393224 | tf_op jit(solution)/shard_map/ppermute | solution.py:316
  14.6 6.5 %collective-permute-start.2 = (f32[128,256]{1,0:T(8,128)S(1)}, f32[128,256]{1,0:T(8,128)S(1)}, u32[]{:S(2)}, u32[]{:S(2)}) collective-permute-start(f32[128,256]{1,0:T(8,128)S(1)} %get-tuple-element.56), channel_id=1, source_target_pairs={{0,3},{8,11},{16,19},{24,27},{32,35},{40,43},{48,51},{56,59},{64,6... | collective-permute-start | bytes 393224 | tf_op jit(solution)/shard_map/ppermute | solution.py:316
  16.0 7.9 %collective-permute-start.1 = (f32[128,256]{1,0:T(8,128)S(1)}, f32[128,256]{1,0:T(8,128)S(1)}, u32[]{:S(2)}, u32[]{:S(2)}) collective-permute-start(f32[128,256]{1,0:T(8,128)S(1)} %get-tuple-element.57), channel_id=1, source_target_pairs={{0,2},{8,10},{16,18},{24,26},{32,34},{40,42},{48,50},{56,58},{64,6... | collective-permute-start | bytes 393224 | tf_op jit(solution)/shard_map/ppermute | solution.py:316
  17.3 6.6 %collective-permute-start = (f32[128,256]{1,0:T(8,128)S(1)}, f32[128,256]{1,0:T(8,128)S(1)}, u32[]{:S(2)}, u32[]{:S(2)}) collective-permute-start(f32[128,256]{1,0:T(8,128)S(1)} %get-tuple-element.58), channel_id=1, source_target_pairs={{0,1},{8,9},{16,17},{24,25},{32,33},{40,41},{48,49},{56,57},{64,65... | collective-permute-start | bytes 393224 | tf_op jit(solution)/shard_map/ppermute | solution.py:316
  24.9 17.5 %all-to-all-start = ((f32[8,128,256]{2,1,0:T(8,128)}), f32[8,128,256]{2,1,0:T(8,128)S(1)}, u32[]{:S(2)}, u32[]{:S(2)}) async-start(f32[8,128,256]{2,1,0:T(8,128)} %get-tuple-element.27), calls=%async_computation | async-start | bytes 2097152 | tf_op jit(solution)/shard_map/all_to_all | solution.py:257
  28.5 0.7 collective-permute-start.7
  42.5 2.3 %copy-start.4 = (f32[8,128,256]{2,1,0:T(8,128)}, f32[8,128,256]{2,1,0:T(8,128)S(1)}, u32[]{:S(2)}) copy-start(f32[8,128,256]{2,1,0:T(8,128)S(1)} %all-to-all-done) | copy-start | bytes 3145732
  44.8 1.0 copy-start.7
  45.8 27.4 %all-to-all-start.1 = ((f32[8,320,128]{2,1,0:T(8,128)}), f32[8,320,128]{2,1,0:T(8,128)S(1)}, u32[]{:S(2)}, u32[]{:S(2)}) async-start(f32[8,320,128]{2,1,0:T(8,128)} %get-tuple-element.32), calls=%async_computation.1 | async-start | bytes 2621440 | tf_op jit(solution)/shard_map/all_to_all | solution.py:257
  73.2 67.1 %copy-start.2 = (f32[8,320,128]{2,1,0:T(8,128)}, f32[8,320,128]{2,1,0:T(8,128)S(1)}, u32[]{:S(2)}) copy-start(f32[8,320,128]{2,1,0:T(8,128)S(1)} %all-to-all-done.1.panel_ref.pmine_ref) | copy-start | bytes 3932164
  73.2 6.0 %collective-permute-start.8 = (f32[8,384,128]{2,1,0:T(8,128)}, f32[8,384,128]{2,1,0:T(8,128)S(1)}, u32[]{:S(2)}, u32[]{:S(2)}) collective-permute-start(f32[8,384,128]{2,1,0:T(8,128)} %get-tuple-element.34), channel_id=1, source_target_pairs={{0,8},{8,0},{1,9},{9,1},{2,10},{10,2},{3,11},{11,3},{4,12},{12,4},... | collective-permute-start | bytes 4718600 | tf_op jit(solution)/shard_map/ppermute | solution.py:261
  76.0 2.9 %collective-permute-start.9 = (f32[64,128]{1,0:T(8,128)S(1)}, f32[64,128]{1,0:T(8,128)S(1)}, u32[]{:S(2)}, u32[]{:S(2)}) collective-permute-start(f32[64,128]{1,0:T(8,128)S(1)} %slice_reduce_fusion.gram_ref), channel_id=1, source_target_pairs={{0,8},{8,0},{1,9},{9,1},{2,10},{10,2},{3,11},{11,3},{4,12},{12,4},... | collective-permute-start | bytes 98312 | tf_op jit(solution)/shard_map/ppermute | solution.py:261
  79.3 1.4 copy-start.3
  106.6 15.6 %collective-permute-start.10 = (f32[128,256]{1,0:T(8,128)S(1)}, f32[128,256]{1,0:T(8,128)S(1)}, u32[]{:S(2)}, u32[]{:S(2)}) collective-permute-start(f32[128,256]{1,0:T(8,128)S(1)} %get-tuple-element.37), channel_id=1, source_target_pairs={{0,0},{16,1},{32,2},{48,3},{64,4},{80,5},{96,6},{112,7},{8,8},{24,... | collective-permute-start | bytes 393224 | tf_op jit(solution)/shard_map/ppermute | solution.py:353
  108.5 28.2 %all-to-all-start.3 = ((f32[8,384,128]{2,1,0:T(8,128)}), f32[8,384,128]{2,1,0:T(8,128)S(1)}, u32[]{:S(2)}, u32[]{:S(2)}) async-start(f32[8,384,128]{2,1,0:T(8,128)} %broadcast_in_dim.21), calls=%async_computation.3 | async-start | bytes 3145728 | tf_op jit(solution)/shard_map/all_to_all | solution.py:257
  122.2 10.9 %collective-permute-start.13 = (f32[128,256]{1,0:T(8,128)S(1)}, f32[128,256]{1,0:T(8,128)S(1)}, u32[]{:S(2)}, u32[]{:S(2)}) collective-permute-start(f32[128,256]{1,0:T(8,128)S(1)} %collective-permute-done.10), channel_id=1, source_target_pairs={{6,0},{0,2},{2,4},{4,6},{7,1},{1,3},{3,5},{5,7},{14,8},{8,10},{10,... | collective-permute-start | bytes 393224 | tf_op jit(solution)/shard_map/ppermute | solution.py:265
  122.7 10.5 %collective-permute-start.12 = (f32[128,256]{1,0:T(8,128)S(1)}, f32[128,256]{1,0:T(8,128)S(1)}, u32[]{:S(2)}, u32[]{:S(2)}) collective-permute-start(f32[128,256]{1,0:T(8,128)S(1)} %collective-permute-done.10), channel_id=1, source_target_pairs={{4,0},{6,2},{0,4},{2,6},{5,1},{7,3},{1,5},{3,7},{12,8},{14,10},{8,... | collective-permute-start | bytes 393224 | tf_op jit(solution)/shard_map/ppermute | solution.py:265
  124.9 8.3 %collective-permute-start.11 = (f32[128,256]{1,0:T(8,128)S(1)}, f32[128,256]{1,0:T(8,128)S(1)}, u32[]{:S(2)}, u32[]{:S(2)}) collective-permute-start(f32[128,256]{1,0:T(8,128)S(1)} %collective-permute-done.10), channel_id=1, source_target_pairs={{2,0},{4,2},{6,4},{0,6},{3,1},{5,3},{7,5},{1,7},{10,8},{12,10},{14... | collective-permute-start | bytes 393224 | tf_op jit(solution)/shard_map/ppermute | solution.py:265
  126.1 7.1 %copy-start.5 = (f32[8,128,256]{2,1,0:T(8,128)S(1)}, f32[8,128,256]{2,1,0:T(8,128)}, u32[]{:S(2)}) copy-start(f32[8,128,256]{2,1,0:T(8,128)} %copy-done.4) | copy-start | bytes 3145732
  133.1 1.5 copy-start.8
  134.7 1.2 copy-start.1
  135.9 0.8 copy-start.6
  136.7 4.9 %copy-start = (f32[8,384,128]{2,1,0:T(8,128)}, f32[8,384,128]{2,1,0:T(8,128)S(1)}, u32[]{:S(2)}) copy-start(f32[8,384,128]{2,1,0:T(8,128)S(1)} %all-to-all-done.3.product_ref.mine_ref) | copy-start | bytes 4718596
  136.7 14.1 %collective-permute-start.15 = (f32[8,384,128]{2,1,0:T(8,128)S(1)}, f32[8,384,128]{2,1,0:T(8,128)}, u32[]{:S(2)}, u32[]{:S(2)}) collective-permute-start(f32[8,384,128]{2,1,0:T(8,128)S(1)} %all-to-all-done.3.product_ref.mine_ref), channel_id=1, source_target_pairs={{0,8},{8,0},{1,9},{9,1},{2,10},{10,2},{3,11},{11,3},{4,12},{12,4},... | collective-permute-start | bytes 4718600 | tf_op jit(solution)/shard_map/ppermute | solution.py:261
  139.6 30.8 %collective-permute-start.16 = (f32[8,320,128]{2,1,0:T(8,128)S(1)}, f32[8,320,128]{2,1,0:T(8,128)}, u32[]{:S(2)}, u32[]{:S(2)}) collective-permute-start(f32[8,320,128]{2,1,0:T(8,128)S(1)} %all-to-all-done.1.panel_ref.pmine_ref), channel_id=1, source_target_pairs={{0,8},{8,0},{1,9},{9,1},{2,10},{10,2},{3,11},{11,3},{4,12},{12,4},... | collective-permute-start | bytes 3932168 | tf_op jit(solution)/shard_map/ppermute | solution.py:261
  141.7 14.9 %all-to-all-start.4 = ((f32[16,16,256]{2,1,0:T(8,128)}), f32[16,16,256]{2,1,0:T(8,128)S(1)}, u32[]{:S(2)}, u32[]{:S(2)}) async-start(f32[16,16,256]{2,1,0:T(8,128)} %shard_map.49), calls=%async_computation.4 | async-start | bytes 524288 | tf_op jit(solution)/shard_map/all_to_all | solution.py:257
  147.9 22.5 %collective-permute-start.14 = (f32[4,128,256]{2,1,0:T(8,128)}, f32[4,128,256]{2,1,0:T(8,128)}, u32[]{:S(2)}, u32[]{:S(2)}) collective-permute-start(f32[4,128,256]{2,1,0:T(8,128)} %copy-done.6), channel_id=1, source_target_pairs={{0,1},{1,0},{2,3},{3,2},{4,5},{5,4},{6,7},{7,6},{8,9},{9,8},{10,11... | collective-permute-start | bytes 1572872 | tf_op jit(solution)/shard_map/ppermute | solution.py:361
  157.3 13.1 %all-to-all-start.5 = ((f32[16,16,256]{2,1,0:T(8,128)}), f32[16,16,256]{2,1,0:T(8,128)S(1)}, u32[]{:S(2)}, u32[]{:S(2)}) async-start(f32[16,16,256]{2,1,0:T(8,128)} %shard_map.51), calls=%async_computation.5 | async-start | bytes 524288 | tf_op jit(solution)/shard_map/all_to_all | solution.py:257
  170.4 0.7 copy-start.9

commit v7 on v6

--- a/solution.py
+++ b/solution.py
@@ -14,6 +14,7 @@
 ALL = ("y", "zl", "co", "x", "zh")
 HIGHEST = lax.Precision.HIGHEST
 F32 = jnp.float32
+ORDER = (0, 1, 6, 2, 5, 7, 3, 4)
 BF16 = jnp.bfloat16
 NN = (((1,), (0,)), ((), ()))
 NT = (((1,), (1,)), ((), ()))
@@ -133,21 +134,19 @@
 def choose_kernel(col_ref, *refs):
     parts, (out_ref, turned_ref) = refs[:8], refs[8:]
     mine = parts[0][...]
-    for k in range(1, 8):
-        mine = jnp.where(col_ref[0] == k, parts[k][...], mine)
+    for k, part in zip(ORDER[1:], parts[1:]):
+        mine = jnp.where(col_ref[0] == k, part[...], mine)
     for k in range(8):
         out_ref[k] = mine
     turned_ref[...] = mine.T
 
 
-def gram_kernel(panel_ref, block_ref, out_ref, turned_ref):
-    turned = panel_ref[...].T
-    gram = dot(turned, panel_ref[...]).reshape(8, 32, B)
+def gram_kernel(panel_ref, block_ref, out_ref):
+    gram = dot(panel_ref[...].T, panel_ref[...]).reshape(8, 32, B)
     for m in range(8):
         out_ref[m, :256, :] = block_ref[...]
     out_ref[:, 256:288, :] = gram[:, :, :128]
     out_ref[:, 288:, :] = gram[:, :, 128:]
-    turned_ref[:256], turned_ref[256:] = split(turned)
 
 
 def panel_product(turned_ref, right):
@@ -156,8 +155,13 @@
     return both[:256] + (both[256:] + lax.dot_general(turned_ref[:256], lo, NN, preferred_element_type=F32))
 
 
-def product_kernel(core_ref, turned_ref, theirs_ref, mine_ref, vectors_ref, give_ref, keep_ref):
+def product_kernel(core_ref, panel_ref, theirs_ref, mine_ref, vectors_ref, give_ref, keep_ref, turned_ref):
     step = pl.program_id(0)
+
+    @pl.when(step == 0)
+    def _():
+        turned_ref[:256], turned_ref[256:] = split(panel_ref[...].T)
+
     for matrix_ref, out_ref in ((theirs_ref, give_ref), (mine_ref, keep_ref)):
         product = panel_product(turned_ref, matrix_ref[...])
         out_ref[2 * step, :256, :] = product[:, :128]
@@ -311,17 +315,15 @@
 
     global_rows = row_index * rows_here + jnp.arange(rows_here, dtype=jnp.int32)
     columns = jnp.where(global_rows[:, None] >= B, matrix[:, :B], F32(0.0))
-    parts = [columns[:128]]
-    for k in range(1, 8):
-        parts.append(lax.ppermute(columns[k * 128 : (k + 1) * 128], COL, [(0, k)]))
+    parts = {0: columns[:128]}
+    for k in ORDER[1:]:
+        parts[k] = lax.ppermute(columns[k * 128 : (k + 1) * 128], COL, [(0, k)])
     sent, turned = call(
         choose_kernel, (f32(8, 128, 256), f32(256, 128)), 1, in_specs=[SMEM] + [VMEM] * 8
-    )(col_index.astype(jnp.int32).reshape(1), *parts)
+    )(col_index.astype(jnp.int32).reshape(1), *(parts[k] for k in ORDER))
     turned = lax.ppermute(turned, ALL, there)
     panel_rows = exchange(sent, COL).reshape(1024, B)
-    sent, stacked = call(gram_kernel, (f32(8, 320, 128), jax.ShapeDtypeStruct((512, 1024), BF16)), 2, 12)(
-        panel_rows, turned
-    )
+    sent = call(gram_kernel, f32(8, 320, 128), 2, 12)(panel_rows, turned)
     panel = exchange(sent, CHIPS)
     half = pl.BlockSpec((8, 384, 128), lambda t, core: (0, 0, 0))
     give, keep = call(
@@ -333,15 +335,16 @@
             num_scalar_prefetch=1,
             grid=(4,),
             in_specs=[
-                pl.BlockSpec((512, 1024), lambda t, core: (0, 0)),
+                pl.BlockSpec((1024, 256), lambda t, core: (0, 0)),
                 pl.BlockSpec((1024, 256), lambda t, core: (0, (1 - core[0]) * 4 + t)),
                 pl.BlockSpec((1024, 256), lambda t, core: (0, core[0] * 4 + t)),
                 pl.BlockSpec((1024, 256), lambda t, core: (0, t)),
             ],
             out_specs=(half, half),
+            scratch_shapes=[pltpu.VMEM((512, 1024), BF16)],
         ),
-    )(core, stacked, matrix, matrix, vectors)
-    give, keep, panel = lax.optimization_barrier((give, keep, panel))
+    )(core, panel_rows, matrix, matrix, vectors)
+    give, keep, panel, where = lax.optimization_barrier((give, keep, panel, where))
     got = swap_cores(give)
     gram = jnp.sum(panel[:, 256:], axis=0)
     other_gram = swap_cores(gram)

time: 187 us -> 184 us (0.984)
  starting transfers between devices: 61.6 us -> 59.6 us
    ppermute x7, waiting for transfers between devices: 5.31 us -> 2.12 us  [body(): parts[k] = lax.ppermute(columns[k * 128:(k + 1) * 128], COL, [(0, k)])]
    all_to_all x5, waiting for transfers between devices: 26.1 us -> 28.7 us  [exchange(): return lax.all_to_all(blocks, axes, 0, 0, tiled=True)]
    unnamed x20 -> x18, local copies, waits for them, and re-layouts: 5.12 us -> 4.16 us
  transfers between devices with their start and end apart: 22 -> 22, of which waited for: 8 -> 9; matrix products, arithmetic and copies ran while one was open for 1% -> 1% of each run, Pallas kernels for 19% -> 20%
where the time goes in v7:
time: 184 us; the launch traced here: 183 us
  starting transfers between devices  59.6 us (32%)
  Pallas kernels  55 us (30%)
  waiting for transfers between devices  34 us (18%)
  blocking collectives  25.8 us (14%)
  local copies, waits for them, and re-layouts  5.49 us (3%)
  other arithmetic  2.15 us (1%)
    all_to_all x5, starting transfers between devices, exchange(): return lax.all_to_all(blocks, axes, 0, 0, tiled=True)  33.2 us
    all_to_all x5, waiting for transfers between devices, exchange(): return lax.all_to_all(blocks, axes, 0, 0, tiled=True)  28.7 us
    all_to_all x1, blocking collectives, exchange(): return lax.all_to_all(blocks, axes, 0, 0, tiled=True)  25.8 us
    ppermute x7, starting transfers between devices, body(): parts[k] = lax.ppermute(columns[k * 128:(k + 1) * 128], COL, [(0, k)])  15.1 us
    pallas_call x1, Pallas kernels, body(): call(update_kernel, f32(1024, 2048), 12, 60, grid_spec=pltpu.PrefetchScal...  14.9 us
    pallas_call x1, Pallas kernels, body(): call(product_kernel, (f32(8, 384, 128), f32(8, 384, 128)), 12, 60, grid_s...  10.8 us
    pallas_call x2, Pallas kernels, rotate(): call(rotate_kernel, f32(1024, 1024), 3, 60, grid=(2,), in_specs=[SMEM, wh...  8.17 us
    pallas_call x1, Pallas kernels, body(): inverse = call(invert_second, f32(B, B), 9)(ai, t, schur)  7.03 us
  transfers between devices with their start and end apart: 22, of which 9 were waited for; matrix products, arithmetic and copies ran while one was open for 1% of the time, Pallas kernels for 20%

profile of v7, /device:TPU:1, one launch (start us, length us, event | category | flops | bytes accessed | tf_op | source)
XLA Modules:
  0.0 183.0 jit_solution(16282353808188494136)
XLA Ops:
  0.7 1.4 slice_select_fusion
  2.1 0.1 fusion
  2.2 5.5 %collective-permute-start.6 = (f32[128,256]{1,0:T(8,128)S(1)}, f32[128,256]{1,0:T(8,128)S(1)}, u32[]{:S(2)}, u32[]{:S(2)}) collective-permute-start(f32[128,256]{1,0:T(8,128)S(1)} %get-tuple-element.50), channel_id=1, source_target_pairs={{0,4},{8,12},{16,20},{24,28},{32,36},{40,44},{48,52},{56,60},{64,6... | collective-permute-start | bytes 393224 | tf_op jit(solution)/shard_map/ppermute | solution.py:320
  7.7 2.4 %collective-permute-start.5 = (f32[128,256]{1,0:T(8,128)S(1)}, f32[128,256]{1,0:T(8,128)S(1)}, u32[]{:S(2)}, u32[]{:S(2)}) collective-permute-start(f32[128,256]{1,0:T(8,128)S(1)} %get-tuple-element.51), channel_id=1, source_target_pairs={{0,3},{8,11},{16,19},{24,27},{32,35},{40,43},{48,51},{56,59},{64,6... | collective-permute-start | bytes 393224 | tf_op jit(solution)/shard_map/ppermute | solution.py:320
  10.1 1.9 %collective-permute-start.4 = (f32[128,256]{1,0:T(8,128)S(1)}, f32[128,256]{1,0:T(8,128)S(1)}, u32[]{:S(2)}, u32[]{:S(2)}) collective-permute-start(f32[128,256]{1,0:T(8,128)S(1)} %get-tuple-element.52), channel_id=1, source_target_pairs={{0,7},{8,15},{16,23},{24,31},{32,39},{40,47},{48,55},{56,63},{64,7... | collective-permute-start | bytes 393224 | tf_op jit(solution)/shard_map/ppermute | solution.py:320
  12.1 1.3 collective-permute-start.3
  13.4 1.3 collective-permute-start.2
  14.7 0.0 collective-permute-done.6.refs_7_
  14.7 1.3 collective-permute-start.1
  16.0 0.0 collective-permute-done.5.refs_6_
  16.0 1.3 collective-permute-start
  17.3 0.0 collective-permute-done.4.refs_5_
  17.3 0.0 collective-permute-done.3.refs_4_
  17.3 1.0 collective-permute-done.2.refs_3_
  18.3 0.0 collective-permute-done.1.refs_2_
  18.3 1.1 collective-permute-done.refs_1_
  19.5 1.0 shard_map.41
  20.5 5.0 %all-to-all-start = ((f32[8,128,256]{2,1,0:T(8,128)}), f32[8,128,256]{2,1,0:T(8,128)S(1)}, u32[]{:S(2)}, u32[]{:S(2)}) async-start(f32[8,128,256]{2,1,0:T(8,128)} %get-tuple-element.26), calls=%async_computation | async-start | bytes 2097152 | tf_op jit(solution)/shard_map/all_to_all | solution.py:261
  25.5 0.7 collective-permute-start.7
  26.1 0.0 collective-permute-done.7.block_ref
  26.2 14.3 %all-to-all-done = f32[8,128,256]{2,1,0:T(8,128)S(1)} async-done(((f32[8,128,256]{2,1,0:T(8,128)}), f32[8,128,256]{2,1,0:T(8,128)S(1)}, u32[]{:S(2)}, u32[]{:S(2)}) %all-to-all-start) | async-done | bytes 1048608 | tf_op jit(solution)/shard_map/all_to_all | solution.py:261
  40.5 2.3 %shard_map.43 = f32[8,320,128]{2,1,0:T(8,128)} custom-call(f32[1024,256]{1,0:T(8,128)S(1)} %bitcast.9, f32[256,128]{1,0:T(8,128)S(1)} %collective-permute-done.7.block_ref), custom_call_target="tpu_custom_call" | custom-call | flops 2000000000 | bytes 1024 | tf_op jit(solution)/shard_map/pallas_call | solution.py:326
  42.8 10.5 %all-to-all-start.1 = ((f32[8,320,128]{2,1,0:T(8,128)}), f32[8,320,128]{2,1,0:T(8,128)S(1)}, u32[]{:S(2)}, u32[]{:S(2)}) async-start(f32[8,320,128]{2,1,0:T(8,128)} %shard_map.43), calls=%async_computation.1 | async-start | bytes 2621440 | tf_op jit(solution)/shard_map/all_to_all | solution.py:261
  53.3 0.7 pad_add_fusion.where_ref
  53.9 10.8 %shard_map.42 = (f32[8,384,128]{2,1,0:T(8,128)}, f32[8,384,128]{2,1,0:T(8,128)}) custom-call(s32[1]{0:T(128)} %bitcast.core_ref, f32[1024,256]{1,0:T(8,128)} %bitcast.10, f32[1024,2048]{1,0:T(8,128)} %matrix_ref.1, f32[1024,2048]{1,0:T(8,128)} %matrix_ref.1, f32[1024,1024]{1,0:T(8,128)} %vectors_ref.5), custom_call_target="tpu_custom_call" | custom-call | flops 12000000000 | bytes 1024 | tf_op jit(solution)/shard_map/pallas_call | solution.py:329
  64.7 6.6 %all-to-all-done.1.panel_ref.pmine_ref = f32[8,320,128]{2,1,0:T(8,128)S(1)} async-done(((f32[8,320,128]{2,1,0:T(8,128)}), f32[8,320,128]{2,1,0:T(8,128)S(1)}, u32[]{:S(2)}, u32[]{:S(2)}) %all-to-all-start.1) | async-done | bytes 1310752 | tf_op jit(solution)/shard_map/all_to_all | solution.py:261
  71.3 2.0 %collective-permute-start.8 = (f32[8,384,128]{2,1,0:T(8,128)}, f32[8,384,128]{2,1,0:T(8,128)S(1)}, u32[]{:S(2)}, u32[]{:S(2)}) collective-permute-start(f32[8,384,128]{2,1,0:T(8,128)} %get-tuple-element.32), channel_id=1, source_target_pairs={{0,8},{8,0},{1,9},{9,1},{2,10},{10,2},{3,11},{11,3},{4,12},{12,4},... | collective-permute-start | bytes 4718600 | tf_op jit(solution)/shard_map/ppermute | solution.py:265
  73.3 0.1 collective-permute-start.9
  73.4 2.8 %collective-permute-done.9.other_ref = f32[64,128]{1,0:T(8,128)S(1)} collective-permute-done((f32[64,128]{1,0:T(8,128)S(1)}, f32[64,128]{1,0:T(8,128)S(1)}, u32[]{:S(2)}, u32[]{:S(2)}) %collective-permute-start.9) | collective-permute-done | bytes 32800 | tf_op jit(solution)/shard_map/ppermute | solution.py:265
  76.2 0.3 collective-permute-done.8.got_ref
  76.6 1.4 copy-done.3
  78.0 0.2 shard_map.44
  78.2 25.8 %all_to_all.30.in_ref = f32[8,448,128]{2,1,0:T(8,128)S(1)} all-to-all(f32[8,448,128]{2,1,0:T(8,128)S(1)} %shard_map.44), channel_id=1, replica_groups=mesh['y'=4,'zl'=2,'co'=2,'x'=4,'zh'=2] {'y','zl'}, dimensions={0} | all-to-all | bytes 3670016 | tf_op jit(solution)/shard_map/all_to_all | solution.py:261
  104.0 0.1 shard_map.45
  104.1 0.7 collective-permute-start.10
  104.8 1.2 broadcast_in_dim.21
  106.0 7.7 %all-to-all-start.3 = ((f32[8,384,128]{2,1,0:T(8,128)}), f32[8,384,128]{2,1,0:T(8,128)S(1)}, u32[]{:S(2)}, u32[]{:S(2)}) async-start(f32[8,384,128]{2,1,0:T(8,128)} %broadcast_in_dim.21), calls=%async_computation.3 | async-start | bytes 3145728 | tf_op jit(solution)/shard_map/all_to_all | solution.py:261
  113.7 7.0 %shard_map.46 = (f32[128,128]{1,0:T(8,128)S(1)}, f32[128,128]{1,0:T(8,128)S(1)}, f32[128,128]{1,0:T(8,128)S(1)}) custom-call(f32[8,64,128]{2,1,0:T(8,128)S(1)} %get-tuple-element.36.gram_ref), custom_call_target="tpu_custom_call" | custom-call | flops 8999999488 | bytes 1024 | tf_op jit(solution)/shard_map/pallas_call | solution.py:357
  120.7 0.0 collective-permute-done.10
  120.8 0.5 collective-permute-start.13
  121.3 1.0 collective-permute-start.12
  122.3 1.5 collective-permute-start.11
  123.8 7.0 %shard_map.47.inverse_ref = f32[256,256]{1,0:T(8,128)S(1)} custom-call(f32[128,128]{1,0:T(8,128)S(1)} %get-tuple-element.37.ai_ref, f32[128,128]{1,0:T(8,128)S(1)} %get-tuple-element.38.t_ref, f32[128,128]{1,0:T(8,128)S(1)} %get-tuple-element.39.schur_ref), custom_call_target="tpu_custom_call" | custom-call | flops 8999999488 | bytes 1024 | tf_op jit(solution)/shard_map/pallas_call | solution.py:358
  130.8 0.0 collective-permute-done.13
  130.9 1.4 shard_map.48
  132.4 1.2 copy-done.1
  133.6 0.8 copy-done.6
  134.4 1.5 all-to-all-done.3.product_ref.mine_ref
  135.8 2.1 %collective-permute-start.15 = (f32[8,384,128]{2,1,0:T(8,128)S(1)}, f32[8,384,128]{2,1,0:T(8,128)}, u32[]{:S(2)}, u32[]{:S(2)}) collective-permute-start(f32[8,384,128]{2,1,0:T(8,128)S(1)} %all-to-all-done.3.product_ref.mine_ref), channel_id=1, source_target_pairs={{0,8},{8,0},{1,9},{9,1},{2,10},{10,2},{3,11},{11,3},{4,12},{12,4},... | collective-permute-start | bytes 4718600 | tf_op jit(solution)/shard_map/ppermute | solution.py:265
  138.0 0.0 collective-permute-start.16
  138.0 1.3 shard_map.49
  139.3 5.3 %all-to-all-start.4 = ((f32[16,16,256]{2,1,0:T(8,128)}), f32[16,16,256]{2,1,0:T(8,128)S(1)}, u32[]{:S(2)}, u32[]{:S(2)}) async-start(f32[16,16,256]{2,1,0:T(8,128)} %shard_map.49), calls=%async_computation.4 | async-start | bytes 524288 | tf_op jit(solution)/shard_map/all_to_all | solution.py:261
  144.7 2.9 %collective-permute-start.14 = (f32[4,128,256]{2,1,0:T(8,128)}, f32[4,128,256]{2,1,0:T(8,128)}, u32[]{:S(2)}, u32[]{:S(2)}) collective-permute-start(f32[4,128,256]{2,1,0:T(8,128)} %copy-done.6), channel_id=1, source_target_pairs={{0,1},{1,0},{2,3},{3,2},{4,5},{5,4},{6,7},{7,6},{8,9},{9,8},{10,11... | collective-permute-start | bytes 1572872 | tf_op jit(solution)/shard_map/ppermute | solution.py:364
  147.5 0.0 collective-permute-done.15.other_ref
  147.5 4.1 %shard_map.50.out_0_ = f32[1024,1024]{1,0:T(8,128)} custom-call(s32[1]{0:T(128)} %bitcast.core_ref, bf16[1024,768]{1,0:T(8,128)(2,1)} %copy-done.1, f32[8,384,128]{2,1,0:T(8,128)} %copy-done, f32[8,384,128]{2,1,0:T(8,128)} %collective-permute-done.15.other_ref, f32[1024,1024]{1,0:T(8,128)} %vectors_ref.5), custom_call_target="tpu_custom_call" | custom-call | flops 3000000000 | bytes 1024 | tf_op jit(solution)/shard_map/pallas_call | solution.py:295
  151.6 1.7 all-to-all-done.4.in_ref
  153.3 0.7 shard_map.51
  154.1 4.6 %all-to-all-start.5 = ((f32[16,16,256]{2,1,0:T(8,128)}), f32[16,16,256]{2,1,0:T(8,128)S(1)}, u32[]{:S(2)}, u32[]{:S(2)}) async-start(f32[16,16,256]{2,1,0:T(8,128)} %shard_map.51), calls=%async_computation.5 | async-start | bytes 524288 | tf_op jit(solution)/shard_map/all_to_all | solution.py:261
  158.7 4.1 %shard_map.52 = f32[1024,1024]{1,0:T(8,128)} custom-call(s32[1]{0:T(128)} %bitcast.core_ref, bf16[1024,768]{1,0:T(8,128)(2,1)} %copy-done.1, f32[8,384,128]{2,1,0:T(8,128)} %copy-done, f32[8,384,128]{2,1,0:T(8,128)} %collective-permute-done.15.other_ref, f32[1024,1024]{1,0:T(8,128)} %vectors_ref.5, ...), custom_call_target="tpu_custom_call", output_to_operand_aliasing={{}: (5, {})} | custom-call | flops 3000000000 | bytes 1024 | tf_op jit(solution)/shard_map/pallas_call | solution.py:295
  162.8 4.5 %all-to-all-done.5.coupling_ref = f32[16,16,256]{2,1,0:T(8,128)S(1)} async-done(((f32[16,16,256]{2,1,0:T(8,128)}), f32[16,16,256]{2,1,0:T(8,128)S(1)}, u32[]{:S(2)}, u32[]{:S(2)}) %all-to-all-start.5) | async-done | bytes 262176 | tf_op jit(solution)/shard_map/all_to_all | solution.py:261
  167.4 0.0 collective-permute-done.16.pother_ref
  167.4 0.0 collective-permute-done.14.far_ref
  167.4 0.7 copy-done.8
  168.1 14.9 %shard_map.53 = f32[1024,2048]{1,0:T(8,128)} custom-call(s32[3]{0:T(128)} %pad_add_fusion.where_ref, bf16[1024,768]{1,0:T(8,128)(2,1)} %copy-done.1, f32[4,128,256]{2,1,0:T(8,128)} %copy-done.6, f32[4,128,256]{2,1,0:T(8,128)} %collective-permute-done.14.far_ref, f32[256,256]{1,0:T(8,128)} %copy-done.7, f32[16,16,256]{2,1,0:T(8,128)} %copy-done.8, ...), custom_call_target="tpu_custom_call" | custom-call | flops 12000000000 | bytes 1024 | tf_op jit(solution)/shard_map/pallas_call | solution.py:385
  (19 shorter events, 0.1 us)
Async XLA Ops:
  2.2 12.5 %collective-permute-start.6 = (f32[128,256]{1,0:T(8,128)S(1)}, f32[128,256]{1,0:T(8,128)S(1)}, u32[]{:S(2)}, u32[]{:S(2)}) collective-permute-start(f32[128,256]{1,0:T(8,128)S(1)} %get-tuple-element.50), channel_id=1, source_target_pairs={{0,4},{8,12},{16,20},{24,28},{32,36},{40,44},{48,52},{56,60},{64,6... | collective-permute-start | bytes 393224 | tf_op jit(solution)/shard_map/ppermute | solution.py:320
  7.7 8.3 %collective-permute-start.5 = (f32[128,256]{1,0:T(8,128)S(1)}, f32[128,256]{1,0:T(8,128)S(1)}, u32[]{:S(2)}, u32[]{:S(2)}) collective-permute-start(f32[128,256]{1,0:T(8,128)S(1)} %get-tuple-element.51), channel_id=1, source_target_pairs={{0,3},{8,11},{16,19},{24,27},{32,35},{40,43},{48,51},{56,59},{64,6... | collective-permute-start | bytes 393224 | tf_op jit(solution)/shard_map/ppermute | solution.py:320
  10.1 7.2 %collective-permute-start.4 = (f32[128,256]{1,0:T(8,128)S(1)}, f32[128,256]{1,0:T(8,128)S(1)}, u32[]{:S(2)}, u32[]{:S(2)}) collective-permute-start(f32[128,256]{1,0:T(8,128)S(1)} %get-tuple-element.52), channel_id=1, source_target_pairs={{0,7},{8,15},{16,23},{24,31},{32,39},{40,47},{48,55},{56,63},{64,7... | collective-permute-start | bytes 393224 | tf_op jit(solution)/shard_map/ppermute | solution.py:320
  12.1 5.3 %collective-permute-start.3 = (f32[128,256]{1,0:T(8,128)S(1)}, f32[128,256]{1,0:T(8,128)S(1)}, u32[]{:S(2)}, u32[]{:S(2)}) collective-permute-start(f32[128,256]{1,0:T(8,128)S(1)} %get-tuple-element.53), channel_id=1, source_target_pairs={{0,5},{8,13},{16,21},{24,29},{32,37},{40,45},{48,53},{56,61},{64,6... | collective-permute-start | bytes 393224 | tf_op jit(solution)/shard_map/ppermute | solution.py:320
  13.4 4.9 %collective-permute-start.2 = (f32[128,256]{1,0:T(8,128)S(1)}, f32[128,256]{1,0:T(8,128)S(1)}, u32[]{:S(2)}, u32[]{:S(2)}) collective-permute-start(f32[128,256]{1,0:T(8,128)S(1)} %get-tuple-element.54), channel_id=1, source_target_pairs={{0,2},{8,10},{16,18},{24,26},{32,34},{40,42},{48,50},{56,58},{64,6... | collective-permute-start | bytes 393224 | tf_op jit(solution)/shard_map/ppermute | solution.py:320
  14.7 3.6 %collective-permute-start.1 = (f32[128,256]{1,0:T(8,128)S(1)}, f32[128,256]{1,0:T(8,128)S(1)}, u32[]{:S(2)}, u32[]{:S(2)}) collective-permute-start(f32[128,256]{1,0:T(8,128)S(1)} %get-tuple-element.55), channel_id=1, source_target_pairs={{0,6},{8,14},{16,22},{24,30},{32,38},{40,46},{48,54},{56,62},{64,7... | collective-permute-start | bytes 393224 | tf_op jit(solution)/shard_map/ppermute | solution.py:320
  16.0 3.4 %collective-permute-start = (f32[128,256]{1,0:T(8,128)S(1)}, f32[128,256]{1,0:T(8,128)S(1)}, u32[]{:S(2)}, u32[]{:S(2)}) collective-permute-start(f32[128,256]{1,0:T(8,128)S(1)} %get-tuple-element.56), channel_id=1, source_target_pairs={{0,1},{8,9},{16,17},{24,25},{32,33},{40,41},{48,49},{56,57},{64,65... | collective-permute-start | bytes 393224 | tf_op jit(solution)/shard_map/ppermute | solution.py:320
  20.5 20.0 %all-to-all-start = ((f32[8,128,256]{2,1,0:T(8,128)}), f32[8,128,256]{2,1,0:T(8,128)S(1)}, u32[]{:S(2)}, u32[]{:S(2)}) async-start(f32[8,128,256]{2,1,0:T(8,128)} %get-tuple-element.26), calls=%async_computation | async-start | bytes 2097152 | tf_op jit(solution)/shard_map/all_to_all | solution.py:261
  25.5 0.7 collective-permute-start.7
  40.5 2.3 %copy-start.4 = (f32[8,128,256]{2,1,0:T(8,128)}, f32[8,128,256]{2,1,0:T(8,128)S(1)}, u32[]{:S(2)}) copy-start(f32[8,128,256]{2,1,0:T(8,128)S(1)} %all-to-all-done) | copy-start | bytes 3145732
  42.8 28.6 %all-to-all-start.1 = ((f32[8,320,128]{2,1,0:T(8,128)}), f32[8,320,128]{2,1,0:T(8,128)S(1)}, u32[]{:S(2)}, u32[]{:S(2)}) async-start(f32[8,320,128]{2,1,0:T(8,128)} %shard_map.43), calls=%async_computation.1 | async-start | bytes 2621440 | tf_op jit(solution)/shard_map/all_to_all | solution.py:261
  71.3 66.6 %copy-start.2 = (f32[8,320,128]{2,1,0:T(8,128)}, f32[8,320,128]{2,1,0:T(8,128)S(1)}, u32[]{:S(2)}) copy-start(f32[8,320,128]{2,1,0:T(8,128)S(1)} %all-to-all-done.1.panel_ref.pmine_ref) | copy-start | bytes 3932164
  71.3 5.3 %collective-permute-start.8 = (f32[8,384,128]{2,1,0:T(8,128)}, f32[8,384,128]{2,1,0:T(8,128)S(1)}, u32[]{:S(2)}, u32[]{:S(2)}) collective-permute-start(f32[8,384,128]{2,1,0:T(8,128)} %get-tuple-element.32), channel_id=1, source_target_pairs={{0,8},{8,0},{1,9},{9,1},{2,10},{10,2},{3,11},{11,3},{4,12},{12,4},... | collective-permute-start | bytes 4718600 | tf_op jit(solution)/shard_map/ppermute | solution.py:265
  73.3 2.9 %collective-permute-start.9 = (f32[64,128]{1,0:T(8,128)S(1)}, f32[64,128]{1,0:T(8,128)S(1)}, u32[]{:S(2)}, u32[]{:S(2)}) collective-permute-start(f32[64,128]{1,0:T(8,128)S(1)} %slice_reduce_fusion.gram_ref), channel_id=1, source_target_pairs={{0,8},{8,0},{1,9},{9,1},{2,10},{10,2},{3,11},{11,3},{4,12},{12,4},... | collective-permute-start | bytes 98312 | tf_op jit(solution)/shard_map/ppermute | solution.py:265
  76.6 1.4 copy-start.3
  104.1 16.6 %collective-permute-start.10 = (f32[128,256]{1,0:T(8,128)S(1)}, f32[128,256]{1,0:T(8,128)S(1)}, u32[]{:S(2)}, u32[]{:S(2)}) collective-permute-start(f32[128,256]{1,0:T(8,128)S(1)} %get-tuple-element.35), channel_id=1, source_target_pairs={{0,0},{16,1},{32,2},{48,3},{64,4},{80,5},{96,6},{112,7},{8,8},{24,... | collective-permute-start | bytes 393224 | tf_op jit(solution)/shard_map/ppermute | solution.py:356
  106.0 29.8 %all-to-all-start.3 = ((f32[8,384,128]{2,1,0:T(8,128)}), f32[8,384,128]{2,1,0:T(8,128)S(1)}, u32[]{:S(2)}, u32[]{:S(2)}) async-start(f32[8,384,128]{2,1,0:T(8,128)} %broadcast_in_dim.21), calls=%async_computation.3 | async-start | bytes 3145728 | tf_op jit(solution)/shard_map/all_to_all | solution.py:261
  120.8 10.1 %collective-permute-start.13 = (f32[128,256]{1,0:T(8,128)S(1)}, f32[128,256]{1,0:T(8,128)S(1)}, u32[]{:S(2)}, u32[]{:S(2)}) collective-permute-start(f32[128,256]{1,0:T(8,128)S(1)} %collective-permute-done.10), channel_id=1, source_target_pairs={{6,0},{0,2},{2,4},{4,6},{7,1},{1,3},{3,5},{5,7},{14,8},{8,10},{10,... | collective-permute-start | bytes 393224 | tf_op jit(solution)/shard_map/ppermute | solution.py:269
  121.3 9.5 %collective-permute-start.12 = (f32[128,256]{1,0:T(8,128)S(1)}, f32[128,256]{1,0:T(8,128)S(1)}, u32[]{:S(2)}, u32[]{:S(2)}) collective-permute-start(f32[128,256]{1,0:T(8,128)S(1)} %collective-permute-done.10), channel_id=1, source_target_pairs={{4,0},{6,2},{0,4},{2,6},{5,1},{7,3},{1,5},{3,7},{12,8},{14,10},{8,... | collective-permute-start | bytes 393224 | tf_op jit(solution)/shard_map/ppermute | solution.py:269
  122.3 8.6 %collective-permute-start.11 = (f32[128,256]{1,0:T(8,128)S(1)}, f32[128,256]{1,0:T(8,128)S(1)}, u32[]{:S(2)}, u32[]{:S(2)}) collective-permute-start(f32[128,256]{1,0:T(8,128)S(1)} %collective-permute-done.10), channel_id=1, source_target_pairs={{2,0},{4,2},{6,4},{0,6},{3,1},{5,3},{7,5},{1,7},{10,8},{12,10},{14... | collective-permute-start | bytes 393224 | tf_op jit(solution)/shard_map/ppermute | solution.py:269
  123.8 7.1 %copy-start.5 = (f32[8,128,256]{2,1,0:T(8,128)S(1)}, f32[8,128,256]{2,1,0:T(8,128)}, u32[]{:S(2)}) copy-start(f32[8,128,256]{2,1,0:T(8,128)} %copy-done.4) | copy-start | bytes 3145732
  130.8 1.5 copy-start.7
  132.4 1.2 copy-start.1
  133.6 0.8 copy-start.6
  135.8 3.5 %copy-start = (f32[8,384,128]{2,1,0:T(8,128)}, f32[8,384,128]{2,1,0:T(8,128)S(1)}, u32[]{:S(2)}) copy-start(f32[8,384,128]{2,1,0:T(8,128)S(1)} %all-to-all-done.3.product_ref.mine_ref) | copy-start | bytes 4718596
  135.8 11.7 %collective-permute-start.15 = (f32[8,384,128]{2,1,0:T(8,128)S(1)}, f32[8,384,128]{2,1,0:T(8,128)}, u32[]{:S(2)}, u32[]{:S(2)}) collective-permute-start(f32[8,384,128]{2,1,0:T(8,128)S(1)} %all-to-all-done.3.product_ref.mine_ref), channel_id=1, source_target_pairs={{0,8},{8,0},{1,9},{9,1},{2,10},{10,2},{3,11},{11,3},{4,12},{12,4},... | collective-permute-start | bytes 4718600 | tf_op jit(solution)/shard_map/ppermute | solution.py:265
  138.0 29.4 %collective-permute-start.16 = (f32[8,320,128]{2,1,0:T(8,128)S(1)}, f32[8,320,128]{2,1,0:T(8,128)}, u32[]{:S(2)}, u32[]{:S(2)}) collective-permute-start(f32[8,320,128]{2,1,0:T(8,128)S(1)} %all-to-all-done.1.panel_ref.pmine_ref), channel_id=1, source_target_pairs={{0,8},{8,0},{1,9},{9,1},{2,10},{10,2},{3,11},{11,3},{4,12},{12,4},... | collective-permute-start | bytes 3932168 | tf_op jit(solution)/shard_map/ppermute | solution.py:265
  139.3 14.0 %all-to-all-start.4 = ((f32[16,16,256]{2,1,0:T(8,128)}), f32[16,16,256]{2,1,0:T(8,128)S(1)}, u32[]{:S(2)}, u32[]{:S(2)}) async-start(f32[16,16,256]{2,1,0:T(8,128)} %shard_map.49), calls=%async_computation.4 | async-start | bytes 524288 | tf_op jit(solution)/shard_map/all_to_all | solution.py:261
  144.7 22.7 %collective-permute-start.14 = (f32[4,128,256]{2,1,0:T(8,128)}, f32[4,128,256]{2,1,0:T(8,128)}, u32[]{:S(2)}, u32[]{:S(2)}) collective-permute-start(f32[4,128,256]{2,1,0:T(8,128)} %copy-done.6), channel_id=1, source_target_pairs={{0,1},{1,0},{2,3},{3,2},{4,5},{5,4},{6,7},{7,6},{8,9},{9,8},{10,11... | collective-permute-start | bytes 1572872 | tf_op jit(solution)/shard_map/ppermute | solution.py:364
  154.1 13.3 %all-to-all-start.5 = ((f32[16,16,256]{2,1,0:T(8,128)}), f32[16,16,256]{2,1,0:T(8,128)S(1)}, u32[]{:S(2)}, u32[]{:S(2)}) async-start(f32[16,16,256]{2,1,0:T(8,128)} %shard_map.51), calls=%async_computation.5 | async-start | bytes 524288 | tf_op jit(solution)/shard_map/all_to_all | solution.py:261
  167.4 0.7 copy-start.8

commit v8 on v7

--- a/solution.py
+++ b/solution.py
@@ -182,12 +182,13 @@
         out_ref[m, 384:, :] = gram
 
 
-def reduce_kernel(in_ref, product_ref, own_ref, gram_ref):
+def reduce_kernel(in_ref, product_ref, out_ref, gram_ref):
     own = in_ref[0, :384, :]
     for m in range(1, 8):
         own = own + in_ref[m, :384, :]
     product_ref[...] = own[:256].T
-    own_ref[...] = own
+    for m in range(8):
+        out_ref[m] = own
     gram_ref[...] = in_ref[:, 384:, :]
 
 
@@ -351,8 +352,8 @@
     other_panel = swap_cores(panel)
     came = exchange(call(join_kernel, f32(8, 448, 128), 1, 12)(keep, got, gram, other_gram), CHIPS)
 
-    product, own, gram = call(reduce_kernel, (f32(128, 256), f32(384, 128), f32(8, 64, 128)), 2, 12)(came)
-    final = exchange(repeat(own), CHIPS)
+    product, sent, gram = call(reduce_kernel, (f32(128, 256), f32(8, 384, 128), f32(8, 64, 128)), 2, 12)(came)
+    final = exchange(sent, CHIPS)
     near = gather_x(lax.ppermute(product, ALL, back))
     ai, t, schur = call(invert_first, (f32(128, 128),) * 3, 9)(gram)
     inverse = call(invert_second, f32(B, B), 9)(ai, t, schur)

time: 184 us -> 184 us (level)
    ppermute x3, starting transfers between devices: 3.02 us -> 8.94 us  [gather_x(): lax.ppermute(block, 'x', [((x + k) % 4, x) for x in range(4)])]
    all_to_all x5, starting transfers between devices: 33.2 us -> 28.2 us  [exchange(): return lax.all_to_all(blocks, axes, 0, 0, tiled=True)]
    unnamed x18 -> x20, local copies, waits for them, and re-layouts: 4.16 us -> 5.29 us
  transfers between devices with their start and end apart: 22 -> 22, of which waited for: 9 -> 8; matrix products, arithmetic and copies ran while one was open for 1% -> 0% of each run, Pallas kernels for 20% -> 20%
where the time goes in v8:
time: 184 us; the launch traced here: 183 us
  starting transfers between devices  61.3 us (33%)
  Pallas kernels  55.1 us (30%)
  waiting for transfers between devices  32.6 us (18%)
  blocking collectives  25.8 us (14%)
  local copies, waits for them, and re-layouts  5.38 us (3%)
  other arithmetic  2.12 us (1%)
    all_to_all x5, starting transfers between devices, exchange(): return lax.all_to_all(blocks, axes, 0, 0, tiled=True)  28.2 us
    all_to_all x5, waiting for transfers between devices, exchange(): return lax.all_to_all(blocks, axes, 0, 0, tiled=True)  27.3 us
    all_to_all x1, blocking collectives, exchange(): return lax.all_to_all(blocks, axes, 0, 0, tiled=True)  25.8 us
    ppermute x7, starting transfers between devices, body(): parts[k] = lax.ppermute(columns[k * 128:(k + 1) * 128], COL, [(0, k)])  15.1 us
    pallas_call x1, Pallas kernels, body(): call(update_kernel, f32(1024, 2048), 12, 60, grid_spec=pltpu.PrefetchScal...  14.9 us
    pallas_call x1, Pallas kernels, body(): call(product_kernel, (f32(8, 384, 128), f32(8, 384, 128)), 12, 60, grid_s...  10.8 us
    ppermute x3, starting transfers between devices, gather_x(): lax.ppermute(block, 'x', [((x + k) % 4, x) for x in range(4)])  8.94 us
    pallas_call x2, Pallas kernels, rotate(): call(rotate_kernel, f32(1024, 1024), 3, 60, grid=(2,), in_specs=[SMEM, wh...  8.17 us
  transfers between devices with their start and end apart: 22, of which 8 were waited for; matrix products, arithmetic and copies ran while one was open for 0% of the time, Pallas kernels for 20%

profile of v8, /device:TPU:1, one launch (start us, length us, event | category | flops | bytes accessed | tf_op | source)
XLA Modules:
  0.0 183.2 jit_solution(14773432008696732382)
XLA Ops:
  0.7 1.4 slice_select_fusion
  2.1 0.1 fusion
  2.2 5.5 %collective-permute-start.6 = (f32[128,256]{1,0:T(8,128)S(1)}, f32[128,256]{1,0:T(8,128)S(1)}, u32[]{:S(2)}, u32[]{:S(2)}) collective-permute-start(f32[128,256]{1,0:T(8,128)S(1)} %get-tuple-element.50), channel_id=1, source_target_pairs={{0,4},{8,12},{16,20},{24,28},{32,36},{40,44},{48,52},{56,60},{64,6... | collective-permute-start | bytes 393224 | tf_op jit(solution)/shard_map/ppermute | solution.py:321
  7.7 2.4 %collective-permute-start.5 = (f32[128,256]{1,0:T(8,128)S(1)}, f32[128,256]{1,0:T(8,128)S(1)}, u32[]{:S(2)}, u32[]{:S(2)}) collective-permute-start(f32[128,256]{1,0:T(8,128)S(1)} %get-tuple-element.51), channel_id=1, source_target_pairs={{0,3},{8,11},{16,19},{24,27},{32,35},{40,43},{48,51},{56,59},{64,6... | collective-permute-start | bytes 393224 | tf_op jit(solution)/shard_map/ppermute | solution.py:321
  10.1 1.9 %collective-permute-start.4 = (f32[128,256]{1,0:T(8,128)S(1)}, f32[128,256]{1,0:T(8,128)S(1)}, u32[]{:S(2)}, u32[]{:S(2)}) collective-permute-start(f32[128,256]{1,0:T(8,128)S(1)} %get-tuple-element.52), channel_id=1, source_target_pairs={{0,7},{8,15},{16,23},{24,31},{32,39},{40,47},{48,55},{56,63},{64,7... | collective-permute-start | bytes 393224 | tf_op jit(solution)/shard_map/ppermute | solution.py:321
  12.1 1.3 collective-permute-start.3
  13.4 1.3 collective-permute-start.2
  14.7 0.0 collective-permute-done.6.refs_7_
  14.7 1.3 collective-permute-start.1
  16.0 0.0 collective-permute-done.5.refs_6_
  16.0 1.3 collective-permute-start
  17.3 0.0 collective-permute-done.4.refs_5_
  17.3 0.0 collective-permute-done.3.refs_4_
  17.3 1.0 collective-permute-done.2.refs_3_
  18.3 0.0 collective-permute-done.1.refs_2_
  18.3 1.1 collective-permute-done.refs_1_
  19.5 1.0 shard_map.41
  20.5 5.0 %all-to-all-start = ((f32[8,128,256]{2,1,0:T(8,128)}), f32[8,128,256]{2,1,0:T(8,128)S(1)}, u32[]{:S(2)}, u32[]{:S(2)}) async-start(f32[8,128,256]{2,1,0:T(8,128)} %get-tuple-element.26), calls=%async_computation | async-start | bytes 2097152 | tf_op jit(solution)/shard_map/all_to_all | solution.py:262
  25.5 0.7 collective-permute-start.7
  26.1 0.0 collective-permute-done.7.block_ref
  26.2 14.3 %all-to-all-done = f32[8,128,256]{2,1,0:T(8,128)S(1)} async-done(((f32[8,128,256]{2,1,0:T(8,128)}), f32[8,128,256]{2,1,0:T(8,128)S(1)}, u32[]{:S(2)}, u32[]{:S(2)}) %all-to-all-start) | async-done | bytes 1048608 | tf_op jit(solution)/shard_map/all_to_all | solution.py:262
  40.5 2.3 %shard_map.43 = f32[8,320,128]{2,1,0:T(8,128)} custom-call(f32[1024,256]{1,0:T(8,128)S(1)} %bitcast.9, f32[256,128]{1,0:T(8,128)S(1)} %collective-permute-done.7.block_ref), custom_call_target="tpu_custom_call" | custom-call | flops 2000000000 | bytes 1024 | tf_op jit(solution)/shard_map/pallas_call | solution.py:327
  42.8 10.5 %all-to-all-start.1 = ((f32[8,320,128]{2,1,0:T(8,128)}), f32[8,320,128]{2,1,0:T(8,128)S(1)}, u32[]{:S(2)}, u32[]{:S(2)}) async-start(f32[8,320,128]{2,1,0:T(8,128)} %shard_map.43), calls=%async_computation.1 | async-start | bytes 2621440 | tf_op jit(solution)/shard_map/all_to_all | solution.py:262
  53.3 0.6 pad_add_fusion.where_ref
  53.9 10.8 %shard_map.42 = (f32[8,384,128]{2,1,0:T(8,128)}, f32[8,384,128]{2,1,0:T(8,128)}) custom-call(s32[1]{0:T(128)} %bitcast.core_ref, f32[1024,256]{1,0:T(8,128)} %bitcast.10, f32[1024,2048]{1,0:T(8,128)} %matrix_ref.1, f32[1024,2048]{1,0:T(8,128)} %matrix_ref.1, f32[1024,1024]{1,0:T(8,128)} %vectors_ref.5), custom_call_target="tpu_custom_call" | custom-call | flops 12000000000 | bytes 1024 | tf_op jit(solution)/shard_map/pallas_call | solution.py:330
  64.7 6.7 %all-to-all-done.1.panel_ref.pmine_ref = f32[8,320,128]{2,1,0:T(8,128)S(1)} async-done(((f32[8,320,128]{2,1,0:T(8,128)}), f32[8,320,128]{2,1,0:T(8,128)S(1)}, u32[]{:S(2)}, u32[]{:S(2)}) %all-to-all-start.1) | async-done | bytes 1310752 | tf_op jit(solution)/shard_map/all_to_all | solution.py:262
  71.3 2.0 %collective-permute-start.8 = (f32[8,384,128]{2,1,0:T(8,128)}, f32[8,384,128]{2,1,0:T(8,128)S(1)}, u32[]{:S(2)}, u32[]{:S(2)}) collective-permute-start(f32[8,384,128]{2,1,0:T(8,128)} %get-tuple-element.32), channel_id=1, source_target_pairs={{0,8},{8,0},{1,9},{9,1},{2,10},{10,2},{3,11},{11,3},{4,12},{12,4},... | collective-permute-start | bytes 4718600 | tf_op jit(solution)/shard_map/ppermute | solution.py:266
  73.3 0.1 collective-permute-start.9
  73.4 2.8 %collective-permute-done.9.other_ref = f32[64,128]{1,0:T(8,128)S(1)} collective-permute-done((f32[64,128]{1,0:T(8,128)S(1)}, f32[64,128]{1,0:T(8,128)S(1)}, u32[]{:S(2)}, u32[]{:S(2)}) %collective-permute-start.9) | collective-permute-done | bytes 32800 | tf_op jit(solution)/shard_map/ppermute | solution.py:266
  76.2 0.3 collective-permute-done.8.got_ref
  76.6 1.4 copy-done.3
  78.0 0.2 shard_map.44
  78.2 25.8 %all_to_all.30.in_ref = f32[8,448,128]{2,1,0:T(8,128)S(1)} all-to-all(f32[8,448,128]{2,1,0:T(8,128)S(1)} %shard_map.44), channel_id=1, replica_groups=mesh['y'=4,'zl'=2,'co'=2,'x'=4,'zh'=2] {'y','zl'}, dimensions={0} | all-to-all | bytes 3670016 | tf_op jit(solution)/shard_map/all_to_all | solution.py:262
  104.0 0.2 shard_map.45
  104.2 0.0 copy-start.4
  104.2 1.1 copy-done.4
  105.4 3.6 %all-to-all-start.3 = ((f32[8,384,128]{2,1,0:T(8,128)}), f32[8,384,128]{2,1,0:T(8,128)S(1)}, u32[]{:S(2)}, u32[]{:S(2)}) async-start(f32[8,384,128]{2,1,0:T(8,128)} %copy-done.4), calls=%async_computation.3 | async-start | bytes 3145728 | tf_op jit(solution)/shard_map/all_to_all | solution.py:262
  109.0 0.7 collective-permute-start.10
  109.6 7.0 %shard_map.46 = (f32[128,128]{1,0:T(8,128)S(1)}, f32[128,128]{1,0:T(8,128)S(1)}, f32[128,128]{1,0:T(8,128)S(1)}) custom-call(f32[8,64,128]{2,1,0:T(8,128)S(1)} %get-tuple-element.36.gram_ref), custom_call_target="tpu_custom_call" | custom-call | flops 8999999488 | bytes 1024 | tf_op jit(solution)/shard_map/pallas_call | solution.py:358
  116.6 0.0 collective-permute-done.10
  116.6 3.8 %collective-permute-start.13 = (f32[128,256]{1,0:T(8,128)S(1)}, f32[128,256]{1,0:T(8,128)S(1)}, u32[]{:S(2)}, u32[]{:S(2)}) collective-permute-start(f32[128,256]{1,0:T(8,128)S(1)} %collective-permute-done.10), channel_id=1, source_target_pairs={{6,0},{0,2},{2,4},{4,6},{7,1},{1,3},{3,5},{5,7},{14,8},{8,10},{10,... | collective-permute-start | bytes 393224 | tf_op jit(solution)/shard_map/ppermute | solution.py:270
  120.5 3.6 %collective-permute-start.12 = (f32[128,256]{1,0:T(8,128)S(1)}, f32[128,256]{1,0:T(8,128)S(1)}, u32[]{:S(2)}, u32[]{:S(2)}) collective-permute-start(f32[128,256]{1,0:T(8,128)S(1)} %collective-permute-done.10), channel_id=1, source_target_pairs={{4,0},{6,2},{0,4},{2,6},{5,1},{7,3},{1,5},{3,7},{12,8},{14,10},{8,... | collective-permute-start | bytes 393224 | tf_op jit(solution)/shard_map/ppermute | solution.py:270
  124.1 1.5 collective-permute-start.11
  125.6 7.0 %shard_map.47.inverse_ref = f32[256,256]{1,0:T(8,128)S(1)} custom-call(f32[128,128]{1,0:T(8,128)S(1)} %get-tuple-element.37.ai_ref, f32[128,128]{1,0:T(8,128)S(1)} %get-tuple-element.38.t_ref, f32[128,128]{1,0:T(8,128)S(1)} %get-tuple-element.39.schur_ref), custom_call_target="tpu_custom_call" | custom-call | flops 8999999488 | bytes 1024 | tf_op jit(solution)/shard_map/pallas_call | solution.py:359
  132.6 0.0 collective-permute-done.13
  132.6 0.0 collective-permute-done.11
  132.7 1.4 shard_map.48
  134.2 1.2 copy-done.1
  135.4 0.8 copy-done.7
  136.2 0.0 all-to-all-done.3.product_ref.mine_ref
  136.2 2.8 %collective-permute-start.15 = (f32[8,384,128]{2,1,0:T(8,128)S(1)}, f32[8,384,128]{2,1,0:T(8,128)}, u32[]{:S(2)}, u32[]{:S(2)}) collective-permute-start(f32[8,384,128]{2,1,0:T(8,128)S(1)} %all-to-all-done.3.product_ref.mine_ref), channel_id=1, source_target_pairs={{0,8},{8,0},{1,9},{9,1},{2,10},{10,2},{3,11},{11,3},{4,12},{12,4},... | collective-permute-start | bytes 4718600 | tf_op jit(solution)/shard_map/ppermute | solution.py:266
  139.0 0.1 collective-permute-start.16
  139.1 1.3 shard_map.49
  140.4 4.7 %all-to-all-start.4 = ((f32[16,16,256]{2,1,0:T(8,128)}), f32[16,16,256]{2,1,0:T(8,128)S(1)}, u32[]{:S(2)}, u32[]{:S(2)}) async-start(f32[16,16,256]{2,1,0:T(8,128)} %shard_map.49), calls=%async_computation.4 | async-start | bytes 524288 | tf_op jit(solution)/shard_map/all_to_all | solution.py:262
  145.1 2.9 %collective-permute-start.14 = (f32[4,128,256]{2,1,0:T(8,128)}, f32[4,128,256]{2,1,0:T(8,128)}, u32[]{:S(2)}, u32[]{:S(2)}) collective-permute-start(f32[4,128,256]{2,1,0:T(8,128)} %copy-done.7), channel_id=1, source_target_pairs={{0,1},{1,0},{2,3},{3,2},{4,5},{5,4},{6,7},{7,6},{8,9},{9,8},{10,11... | collective-permute-start | bytes 1572872 | tf_op jit(solution)/shard_map/ppermute | solution.py:365
  148.0 0.0 collective-permute-done.15.other_ref
  148.0 4.1 %shard_map.50.out_0_ = f32[1024,1024]{1,0:T(8,128)} custom-call(s32[1]{0:T(128)} %bitcast.core_ref, bf16[1024,768]{1,0:T(8,128)(2,1)} %copy-done.1, f32[8,384,128]{2,1,0:T(8,128)} %copy-done, f32[8,384,128]{2,1,0:T(8,128)} %collective-permute-done.15.other_ref, f32[1024,1024]{1,0:T(8,128)} %vectors_ref.5), custom_call_target="tpu_custom_call" | custom-call | flops 3000000000 | bytes 1024 | tf_op jit(solution)/shard_map/pallas_call | solution.py:296
  152.0 1.7 all-to-all-done.4.in_ref
  153.7 0.7 shard_map.51
  154.5 4.5 %all-to-all-start.5 = ((f32[16,16,256]{2,1,0:T(8,128)}), f32[16,16,256]{2,1,0:T(8,128)S(1)}, u32[]{:S(2)}, u32[]{:S(2)}) async-start(f32[16,16,256]{2,1,0:T(8,128)} %shard_map.51), calls=%async_computation.5 | async-start | bytes 524288 | tf_op jit(solution)/shard_map/all_to_all | solution.py:262
  159.0 4.1 %shard_map.52 = f32[1024,1024]{1,0:T(8,128)} custom-call(s32[1]{0:T(128)} %bitcast.core_ref, bf16[1024,768]{1,0:T(8,128)(2,1)} %copy-done.1, f32[8,384,128]{2,1,0:T(8,128)} %copy-done, f32[8,384,128]{2,1,0:T(8,128)} %collective-permute-done.15.other_ref, f32[1024,1024]{1,0:T(8,128)} %vectors_ref.5, ...), custom_call_target="tpu_custom_call", output_to_operand_aliasing={{}: (5, {})} | custom-call | flops 3000000000 | bytes 1024 | tf_op jit(solution)/shard_map/pallas_call | solution.py:296
  163.1 4.5 %all-to-all-done.5.coupling_ref = f32[16,16,256]{2,1,0:T(8,128)S(1)} async-done(((f32[16,16,256]{2,1,0:T(8,128)}), f32[16,16,256]{2,1,0:T(8,128)S(1)}, u32[]{:S(2)}, u32[]{:S(2)}) %all-to-all-start.5) | async-done | bytes 262176 | tf_op jit(solution)/shard_map/all_to_all | solution.py:262
  167.6 0.7 copy-done.9
  168.3 14.9 %shard_map.53 = f32[1024,2048]{1,0:T(8,128)} custom-call(s32[3]{0:T(128)} %pad_add_fusion.where_ref, bf16[1024,768]{1,0:T(8,128)(2,1)} %copy-done.1, f32[4,128,256]{2,1,0:T(8,128)} %copy-done.7, f32[4,128,256]{2,1,0:T(8,128)} %collective-permute-done.14.far_ref, f32[256,256]{1,0:T(8,128)} %copy-done.8, f32[16,16,256]{2,1,0:T(8,128)} %copy-done.9, ...), custom_call_target="tpu_custom_call" | custom-call | flops 12000000000 | bytes 1024 | tf_op jit(solution)/shard_map/pallas_call | solution.py:386
  (20 shorter events, 0.1 us)
Async XLA Ops:
  2.2 12.5 %collective-permute-start.6 = (f32[128,256]{1,0:T(8,128)S(1)}, f32[128,256]{1,0:T(8,128)S(1)}, u32[]{:S(2)}, u32[]{:S(2)}) collective-permute-start(f32[128,256]{1,0:T(8,128)S(1)} %get-tuple-element.50), channel_id=1, source_target_pairs={{0,4},{8,12},{16,20},{24,28},{32,36},{40,44},{48,52},{56,60},{64,6... | collective-permute-start | bytes 393224 | tf_op jit(solution)/shard_map/ppermute | solution.py:321
  7.7 8.3 %collective-permute-start.5 = (f32[128,256]{1,0:T(8,128)S(1)}, f32[128,256]{1,0:T(8,128)S(1)}, u32[]{:S(2)}, u32[]{:S(2)}) collective-permute-start(f32[128,256]{1,0:T(8,128)S(1)} %get-tuple-element.51), channel_id=1, source_target_pairs={{0,3},{8,11},{16,19},{24,27},{32,35},{40,43},{48,51},{56,59},{64,6... | collective-permute-start | bytes 393224 | tf_op jit(solution)/shard_map/ppermute | solution.py:321
  10.1 7.2 %collective-permute-start.4 = (f32[128,256]{1,0:T(8,128)S(1)}, f32[128,256]{1,0:T(8,128)S(1)}, u32[]{:S(2)}, u32[]{:S(2)}) collective-permute-start(f32[128,256]{1,0:T(8,128)S(1)} %get-tuple-element.52), channel_id=1, source_target_pairs={{0,7},{8,15},{16,23},{24,31},{32,39},{40,47},{48,55},{56,63},{64,7... | collective-permute-start | bytes 393224 | tf_op jit(solution)/shard_map/ppermute | solution.py:321
  12.1 5.3 %collective-permute-start.3 = (f32[128,256]{1,0:T(8,128)S(1)}, f32[128,256]{1,0:T(8,128)S(1)}, u32[]{:S(2)}, u32[]{:S(2)}) collective-permute-start(f32[128,256]{1,0:T(8,128)S(1)} %get-tuple-element.53), channel_id=1, source_target_pairs={{0,5},{8,13},{16,21},{24,29},{32,37},{40,45},{48,53},{56,61},{64,6... | collective-permute-start | bytes 393224 | tf_op jit(solution)/shard_map/ppermute | solution.py:321
  13.4 4.9 %collective-permute-start.2 = (f32[128,256]{1,0:T(8,128)S(1)}, f32[128,256]{1,0:T(8,128)S(1)}, u32[]{:S(2)}, u32[]{:S(2)}) collective-permute-start(f32[128,256]{1,0:T(8,128)S(1)} %get-tuple-element.54), channel_id=1, source_target_pairs={{0,2},{8,10},{16,18},{24,26},{32,34},{40,42},{48,50},{56,58},{64,6... | collective-permute-start | bytes 393224 | tf_op jit(solution)/shard_map/ppermute | solution.py:321
  14.7 3.6 %collective-permute-start.1 = (f32[128,256]{1,0:T(8,128)S(1)}, f32[128,256]{1,0:T(8,128)S(1)}, u32[]{:S(2)}, u32[]{:S(2)}) collective-permute-start(f32[128,256]{1,0:T(8,128)S(1)} %get-tuple-element.55), channel_id=1, source_target_pairs={{0,6},{8,14},{16,22},{24,30},{32,38},{40,46},{48,54},{56,62},{64,7... | collective-permute-start | bytes 393224 | tf_op jit(solution)/shard_map/ppermute | solution.py:321
  16.0 3.4 %collective-permute-start = (f32[128,256]{1,0:T(8,128)S(1)}, f32[128,256]{1,0:T(8,128)S(1)}, u32[]{:S(2)}, u32[]{:S(2)}) collective-permute-start(f32[128,256]{1,0:T(8,128)S(1)} %get-tuple-element.56), channel_id=1, source_target_pairs={{0,1},{8,9},{16,17},{24,25},{32,33},{40,41},{48,49},{56,57},{64,65... | collective-permute-start | bytes 393224 | tf_op jit(solution)/shard_map/ppermute | solution.py:321
  20.5 20.0 %all-to-all-start = ((f32[8,128,256]{2,1,0:T(8,128)}), f32[8,128,256]{2,1,0:T(8,128)S(1)}, u32[]{:S(2)}, u32[]{:S(2)}) async-start(f32[8,128,256]{2,1,0:T(8,128)} %get-tuple-element.26), calls=%async_computation | async-start | bytes 2097152 | tf_op jit(solution)/shard_map/all_to_all | solution.py:262
  25.5 0.7 collective-permute-start.7
  40.5 2.3 %copy-start.5 = (f32[8,128,256]{2,1,0:T(8,128)}, f32[8,128,256]{2,1,0:T(8,128)S(1)}, u32[]{:S(2)}) copy-start(f32[8,128,256]{2,1,0:T(8,128)S(1)} %all-to-all-done) | copy-start | bytes 3145732
  42.8 28.6 %all-to-all-start.1 = ((f32[8,320,128]{2,1,0:T(8,128)}), f32[8,320,128]{2,1,0:T(8,128)S(1)}, u32[]{:S(2)}, u32[]{:S(2)}) async-start(f32[8,320,128]{2,1,0:T(8,128)} %shard_map.43), calls=%async_computation.1 | async-start | bytes 2621440 | tf_op jit(solution)/shard_map/all_to_all | solution.py:262
  71.3 67.7 %copy-start.2 = (f32[8,320,128]{2,1,0:T(8,128)}, f32[8,320,128]{2,1,0:T(8,128)S(1)}, u32[]{:S(2)}) copy-start(f32[8,320,128]{2,1,0:T(8,128)S(1)} %all-to-all-done.1.panel_ref.pmine_ref) | copy-start | bytes 3932164
  71.3 5.3 %collective-permute-start.8 = (f32[8,384,128]{2,1,0:T(8,128)}, f32[8,384,128]{2,1,0:T(8,128)S(1)}, u32[]{:S(2)}, u32[]{:S(2)}) collective-permute-start(f32[8,384,128]{2,1,0:T(8,128)} %get-tuple-element.32), channel_id=1, source_target_pairs={{0,8},{8,0},{1,9},{9,1},{2,10},{10,2},{3,11},{11,3},{4,12},{12,4},... | collective-permute-start | bytes 4718600 | tf_op jit(solution)/shard_map/ppermute | solution.py:266
  73.3 2.9 %collective-permute-start.9 = (f32[64,128]{1,0:T(8,128)S(1)}, f32[64,128]{1,0:T(8,128)S(1)}, u32[]{:S(2)}, u32[]{:S(2)}) collective-permute-start(f32[64,128]{1,0:T(8,128)S(1)} %slice_reduce_fusion.gram_ref), channel_id=1, source_target_pairs={{0,8},{8,0},{1,9},{9,1},{2,10},{10,2},{3,11},{11,3},{4,12},{12,4},... | collective-permute-start | bytes 98312 | tf_op jit(solution)/shard_map/ppermute | solution.py:266
  76.6 1.4 copy-start.3
  104.2 1.1 copy-start.4
  105.4 30.8 %all-to-all-start.3 = ((f32[8,384,128]{2,1,0:T(8,128)}), f32[8,384,128]{2,1,0:T(8,128)S(1)}, u32[]{:S(2)}, u32[]{:S(2)}) async-start(f32[8,384,128]{2,1,0:T(8,128)} %copy-done.4), calls=%async_computation.3 | async-start | bytes 3145728 | tf_op jit(solution)/shard_map/all_to_all | solution.py:262
  109.0 7.7 %collective-permute-start.10 = (f32[128,256]{1,0:T(8,128)S(1)}, f32[128,256]{1,0:T(8,128)S(1)}, u32[]{:S(2)}, u32[]{:S(2)}) collective-permute-start(f32[128,256]{1,0:T(8,128)S(1)} %get-tuple-element.35), channel_id=1, source_target_pairs={{0,0},{16,1},{32,2},{48,3},{64,4},{80,5},{96,6},{112,7},{8,8},{24,... | collective-permute-start | bytes 393224 | tf_op jit(solution)/shard_map/ppermute | solution.py:357
  116.6 16.0 %collective-permute-start.13 = (f32[128,256]{1,0:T(8,128)S(1)}, f32[128,256]{1,0:T(8,128)S(1)}, u32[]{:S(2)}, u32[]{:S(2)}) collective-permute-start(f32[128,256]{1,0:T(8,128)S(1)} %collective-permute-done.10), channel_id=1, source_target_pairs={{6,0},{0,2},{2,4},{4,6},{7,1},{1,3},{3,5},{5,7},{14,8},{8,10},{10,... | collective-permute-start | bytes 393224 | tf_op jit(solution)/shard_map/ppermute | solution.py:270
  120.5 12.2 %collective-permute-start.12 = (f32[128,256]{1,0:T(8,128)S(1)}, f32[128,256]{1,0:T(8,128)S(1)}, u32[]{:S(2)}, u32[]{:S(2)}) collective-permute-start(f32[128,256]{1,0:T(8,128)S(1)} %collective-permute-done.10), channel_id=1, source_target_pairs={{4,0},{6,2},{0,4},{2,6},{5,1},{7,3},{1,5},{3,7},{12,8},{14,10},{8,... | collective-permute-start | bytes 393224 | tf_op jit(solution)/shard_map/ppermute | solution.py:270
  124.1 8.5 %collective-permute-start.11 = (f32[128,256]{1,0:T(8,128)S(1)}, f32[128,256]{1,0:T(8,128)S(1)}, u32[]{:S(2)}, u32[]{:S(2)}) collective-permute-start(f32[128,256]{1,0:T(8,128)S(1)} %collective-permute-done.10), channel_id=1, source_target_pairs={{2,0},{4,2},{6,4},{0,6},{3,1},{5,3},{7,5},{1,7},{10,8},{12,10},{14... | collective-permute-start | bytes 393224 | tf_op jit(solution)/shard_map/ppermute | solution.py:270
  125.6 7.1 %copy-start.6 = (f32[8,128,256]{2,1,0:T(8,128)S(1)}, f32[8,128,256]{2,1,0:T(8,128)}, u32[]{:S(2)}) copy-start(f32[8,128,256]{2,1,0:T(8,128)} %copy-done.5) | copy-start | bytes 3145732
  132.6 1.5 copy-start.8
  134.2 1.2 copy-start.1
  135.4 0.9 copy-start.7
  136.2 4.2 %copy-start = (f32[8,384,128]{2,1,0:T(8,128)}, f32[8,384,128]{2,1,0:T(8,128)S(1)}, u32[]{:S(2)}) copy-start(f32[8,384,128]{2,1,0:T(8,128)S(1)} %all-to-all-done.3.product_ref.mine_ref) | copy-start | bytes 4718596
  136.2 11.7 %collective-permute-start.15 = (f32[8,384,128]{2,1,0:T(8,128)S(1)}, f32[8,384,128]{2,1,0:T(8,128)}, u32[]{:S(2)}, u32[]{:S(2)}) collective-permute-start(f32[8,384,128]{2,1,0:T(8,128)S(1)} %all-to-all-done.3.product_ref.mine_ref), channel_id=1, source_target_pairs={{0,8},{8,0},{1,9},{9,1},{2,10},{10,2},{3,11},{11,3},{4,12},{12,4},... | collective-permute-start | bytes 4718600 | tf_op jit(solution)/shard_map/ppermute | solution.py:266
  139.0 28.6 %collective-permute-start.16 = (f32[8,320,128]{2,1,0:T(8,128)S(1)}, f32[8,320,128]{2,1,0:T(8,128)}, u32[]{:S(2)}, u32[]{:S(2)}) collective-permute-start(f32[8,320,128]{2,1,0:T(8,128)S(1)} %all-to-all-done.1.panel_ref.pmine_ref), channel_id=1, source_target_pairs={{0,8},{8,0},{1,9},{9,1},{2,10},{10,2},{3,11},{11,3},{4,12},{12,4},... | collective-permute-start | bytes 3932168 | tf_op jit(solution)/shard_map/ppermute | solution.py:266
  140.4 13.4 %all-to-all-start.4 = ((f32[16,16,256]{2,1,0:T(8,128)}), f32[16,16,256]{2,1,0:T(8,128)S(1)}, u32[]{:S(2)}, u32[]{:S(2)}) async-start(f32[16,16,256]{2,1,0:T(8,128)} %shard_map.49), calls=%async_computation.4 | async-start | bytes 524288 | tf_op jit(solution)/shard_map/all_to_all | solution.py:262
  145.1 22.5 %collective-permute-start.14 = (f32[4,128,256]{2,1,0:T(8,128)}, f32[4,128,256]{2,1,0:T(8,128)}, u32[]{:S(2)}, u32[]{:S(2)}) collective-permute-start(f32[4,128,256]{2,1,0:T(8,128)} %copy-done.7), channel_id=1, source_target_pairs={{0,1},{1,0},{2,3},{3,2},{4,5},{5,4},{6,7},{7,6},{8,9},{9,8},{10,11... | collective-permute-start | bytes 1572872 | tf_op jit(solution)/shard_map/ppermute | solution.py:365
  154.5 13.1 %all-to-all-start.5 = ((f32[16,16,256]{2,1,0:T(8,128)}), f32[16,16,256]{2,1,0:T(8,128)S(1)}, u32[]{:S(2)}, u32[]{:S(2)}) async-start(f32[16,16,256]{2,1,0:T(8,128)} %shard_map.51), calls=%async_computation.5 | async-start | bytes 524288 | tf_op jit(solution)/shard_map/all_to_all | solution.py:262
  167.6 0.7 copy-start.9
